TPU v7x, 32 devices: a whole 2x2x4 slice. The times are simulated.
32 devices in a mesh: groups: 1, gx: 32 (over z, y, x, core).
Axes of the slice: x: 2, y: 2, z: 4, core: 2. Of those that a mesh axis runs over, the one named last changes fastest.
Arguments:
- features: bfloat16 [32, 32, 32768], P(None, ('groups', 'gx')), may hold values from -6 to 6
- block_scale: float32 [32, 32], P(None, ('groups', 'gx')), may hold values from 0.25 to 4
- spec_weight: bfloat16 [2, 32, 32, 8192], P(None, None, None, 'gx'), may hold values from -12 to 12
- bypass_weight: bfloat16 [32, 32], replicated, may hold values from -1 to 1
- mlp_in: bfloat16 [128, 32], replicated, may hold values from -1 to 1
- mlp_out: bfloat16 [32, 128], replicated, may hold values from -0.5 to 0.5
- decode_weight: bfloat16 [2, 32], replicated, may hold values from -1 to 1
- zone_ids: int32 [32, 32768], P(('groups', 'gx')), may hold values from 0 to 7
- face_open: int32 [3, 32, 32768], P(None, ('groups', 'gx')), may hold values 0 or 1
- perm_table: float32 [8], replicated, may hold values from 0.05 to 20
Outputs:
- fields: float32 [2, 32, 32768], P(None, ('groups', 'gx'))
- residual: float32 [32, 32768], P(('groups', 'gx'))
All inputs are finite; a program needn't handle non-finite values. No bound on the sum of `face_open` on one device may be relied on, other than what follows from the above.
Results may differ from a plain program's by a relative error of at most 0.011.
Values sent between devices are 32-bit elements; how exact they have to be, the bound alone decides.
No kernel may reach another device: no remote copies, remote signals or barrier semaphores. Data moves between devices by JAX's collectives and lax.ppermute only.
A program may use at most 64 MiB of HBM per device.

v0:
```python
import functools
import math

import jax
import jax.numpy as jnp
import ml_dtypes
import numpy as np
from jax import lax
from jax.experimental import pallas as pl
from jax.experimental.pallas import tpu as pltpu
from jax.sharding import PartitionSpec as P

NY = 512
NZ = 64
KX = 32
KY = 32
KZ = 8
ZONES = 8
LANES = 128
SUB = 8
PAIRS = LANES // NZ
ROWS = NY // PAIRS
TILES = 4
HALF = KZ * 2 * TILES
GELU_A = math.sqrt(2.0 / math.pi)
GELU_B = GELU_A * 0.044715
F32 = jnp.float32
BF16 = jnp.bfloat16


def signed(count):
    steps = np.arange(count)
    return np.where(steps < count // 2, steps, steps - count)


def angles(freqs, positions, length):
    return 2.0 * np.pi * ((freqs[:, None] * positions[None, :]) % length) / length


def halves(table, axis):
    high = np.asarray(table, np.float64).astype(ml_dtypes.bfloat16)
    low = (table - high.astype(np.float64)).astype(ml_dtypes.bfloat16)
    return np.concatenate([high, low], axis=axis)


def spread(small):
    return np.kron(small, np.eye(SUB))


def z_forward_table():
    angle = angles(np.arange(KZ), np.arange(NZ), NZ)
    table = np.zeros((TILES, PAIRS, NZ, 2, PAIRS, KZ, 2, TILES))
    for t in range(TILES):
        for p in range(PAIRS):
            table[t, p, :, 0, p, :, 0, t] = np.cos(angle).T
            table[t, p, :, 0, p, :, 1, t] = -np.sin(angle).T
            table[t, p, :, 1, p, :, 0, t] = -np.sin(angle).T
            table[t, p, :, 1, p, :, 1, t] = -np.cos(angle).T
    return halves(table.reshape(TILES * LANES, 2 * PAIRS * HALF), 0)


def y_forward_table(rows):
    angle = angles(signed(KY), np.arange(rows) * PAIRS, NY)
    return halves(np.concatenate([spread(np.cos(angle)), spread(np.sin(angle))], axis=0), 1)


def turn_tables(rows):
    parity = np.repeat(angles(signed(KY), np.arange(PAIRS), NY), HALF, axis=1)
    step = np.repeat(angles(signed(KY), np.array([rows * PAIRS]), NY), LANES, axis=1)
    tables = [np.cos(parity), np.sin(parity), np.cos(step), np.sin(step)]
    return np.repeat(np.stack(tables), SUB, axis=1).astype(np.float32)


def x_forward_table(planes):
    angle = angles(signed(KX), np.arange(planes), planes)

    def one(small):
        wide = np.zeros((planes, SUB, SUB, KX))
        for s in range(SUB):
            wide[:, s, s, :] = small.T
        return wide.reshape(planes * SUB, SUB * KX)

    return np.concatenate([one(np.cos(angle)), one(np.sin(angle))], axis=0).astype(np.float32)


def x_back_table(planes):
    return np.ascontiguousarray(x_forward_table(planes).T.reshape(SUB, KX, 2, planes, SUB)
                                .transpose(3, 4, 2, 0, 1).reshape(planes * SUB, 2 * SUB * KX))


def y_back_table(rows):
    angle = angles(signed(KY), np.arange(rows) * PAIRS, NY)
    return halves(np.concatenate([spread(np.cos(angle).T), spread(np.sin(angle).T)], axis=1), 1)


def z_back_table(total):
    angle = angles(np.arange(KZ), np.arange(NZ), NZ)
    weight = np.where(np.arange(KZ) == 0, 1.0, 2.0)[:, None] / total
    table = np.zeros((PAIRS, KZ, 2, TILES, TILES, PAIRS, NZ))
    for t in range(TILES):
        for p in range(PAIRS):
            table[p, :, 0, t, t, p, :] = weight * np.cos(angle)
            table[p, :, 1, t, t, p, :] = -weight * np.sin(angle)
    return halves(table.reshape(PAIRS * HALF, TILES * LANES), 0)


def dot(a, b, dims=((1,), (0,)), precision=None):
    return lax.dot_general(a, b, (dims, ((), ())), precision=precision, preferred_element_type=F32)


def split(x):
    high = x.astype(BF16)
    return high, (x - high.astype(F32)).astype(BF16)


def column(row):
    n = row.shape[1]
    square = lax.broadcasted_iota(jnp.int32, (n, n), 0) == lax.broadcasted_iota(jnp.int32, (n, n), 1)
    return jnp.sum(jnp.where(square, row, 0.0), axis=1, keepdims=True)


def forward_kernel(
    features, scale, zone, opened, perm_table, table_z, table_y, turns, lines, rock, total
):
    step = pl.program_id(0)
    rows = features.shape[1] // LANES

    @pl.when(step == 0)
    def _():
        total[...] = jnp.zeros_like(total)
        zones = zone[...]
        perm = jnp.zeros(zones.shape, F32)
        for k in range(ZONES):
            perm = jnp.where(zones == k, perm_table[k], perm)
        rock[0] = perm
        rock[1] = perm * opened[0].astype(F32)

    values = features[...].astype(F32) * column(scale[...])
    pieces = [
        jnp.concatenate(
            [values[SUB * t : SUB * (t + 1), LANES * j : LANES * (j + 1)] for t in range(TILES)],
            axis=1,
        )
        for j in range(rows)
    ]
    cells = jnp.concatenate(pieces, axis=0).astype(BF16)
    high, low = split(dot(jnp.concatenate([cells, cells], axis=1), table_z[...]))
    table = table_y[...]
    inner = table.shape[1] // 2
    sums = dot(
        jnp.concatenate([table[:, :inner], table], axis=1),
        jnp.concatenate([low, high, high], axis=0),
    )
    n = KY * SUB
    first = sums[:n, :LANES] + sums[n:, LANES:]
    second = sums[:n, LANES:] - sums[n:, :LANES]
    total[0], total[1] = (
        first + turns[2] * total[0] + turns[3] * total[1],
        second + turns[2] * total[1] - turns[3] * total[0],
    )

    @pl.when(step == pl.num_programs(0) - 1)
    def _():
        first, second = total[0], total[1]
        straight = turns[0] * first + turns[1] * second
        turned = turns[0] * second - turns[1] * first
        straight = straight + pltpu.roll(straight, HALF, 1)
        turned = turned + pltpu.roll(turned, HALF, 1)
        lane = lax.broadcasted_iota(jnp.int32, straight.shape, 1)
        lines[...] = jnp.where(lane < HALF, straight, turned)


def swap_blocks(pieces):
    lane = lax.broadcasted_iota(jnp.int32, pieces[0].shape, 1) // KX
    out = []
    for e in range(4):
        got = None
        for b in range(4):
            moved = pieces[b] if b == e else pltpu.roll(pieces[b], (KX * (b - e)) % LANES, 1)
            got = moved if got is None else jnp.where(lane == b, moved, got)
        out.append(got)
    return out


def mix_kernel(
    lines, weight, table_x, table_back, rock, upper, lower, back, links, modes, mixed
):
    links[0] = joined(rock[1], upper[...])
    links[1] = joined(lower[...], rock[0])
    highest = lax.Precision.HIGHEST
    half = lines.shape[1] // 2
    count = half // (2 * TILES)
    groups = count // 4
    flipped = lines[...].T
    pair = jnp.concatenate([flipped[:half], flipped[half:]], axis=1)
    spectrum = dot(pair, table_x[...], precision=highest)
    for c in range(SUB // 4):
        for a in range(groups):
            got = swap_blocks(
                [
                    spectrum[SUB * (4 * a + b) : SUB * (4 * a + b + 1), LANES * c : LANES * (c + 1)]
                    for b in range(4)
                ]
            )
            for e in range(4):
                modes[4 * c + e, :, LANES * a : LANES * (a + 1)] = got[e]
    width = weight.shape[1]
    real = jnp.zeros((width, count * KX), F32)
    imag = jnp.zeros((width, count * KX), F32)
    for i in range(width):
        t, v = i // SUB, i % SUB
        in_real = modes[v, t : t + 1, :]
        in_imag = modes[v, TILES + t : TILES + t + 1, :]
        w_real = weight[0, i].astype(F32)
        w_imag = weight[1, i].astype(F32)
        real += in_real * w_real - in_imag * w_imag
        imag += in_real * w_imag + in_imag * w_real
    for a in range(groups):
        at = slice(LANES * a, LANES * (a + 1))
        mixed[0, a, :width] = real[:, at]
        mixed[0, a, width:] = imag[:, at]
        mixed[1, a, :width] = -imag[:, at]
        mixed[1, a, width:] = real[:, at]
    rows = []
    for k in range(2):
        seen = [
            [mixed[k, a, pl.ds(v, 2 * TILES, stride=SUB), :] for v in range(SUB)]
            for a in range(groups)
        ]
        parts = [[None] * (SUB // 4) for _ in range(count)]
        for c in range(SUB // 4):
            for a in range(groups):
                got = swap_blocks(seen[a][4 * c : 4 * c + 4])
                for b in range(4):
                    parts[4 * a + b][c] = got[b]
        rows.append(jnp.concatenate([jnp.concatenate(p, axis=1) for p in parts], axis=0))
    straight, turned = rows
    sides = jnp.concatenate(
        [
            jnp.concatenate([straight, turned], axis=1),
            jnp.concatenate([turned, -straight], axis=1),
        ],
        axis=0,
    )
    back[...] = dot(table_back[...], sides, ((1,), (1,)), precision=highest)


def gelu_twice(x):
    return x + x * jnp.tanh(x * (GELU_A + GELU_B * (x * x)))


def point_kernel(
    lines,
    features,
    scale,
    bypass,
    mlp_in_t,
    mlp_out,
    decode,
    table_y,
    table_z,
    turns,
    fields,
    state,
    sides,
    smooth,
    latent,
    chunk,
):
    @pl.when(pl.program_id(0) == 0)
    def _():
        held = lines[...]
        other = pltpu.roll(held, HALF, 1)
        lane = lax.broadcasted_iota(jnp.int32, held.shape, 1)
        low = lane < HALF
        n = held.shape[0]
        sides[:n] = jnp.where(low, held, turns[0] * other + turns[1] * held)
        sides[n:] = jnp.where(low, other, turns[0] * held - turns[1] * other)

    rows = features.shape[1] // LANES
    width = features.shape[0]
    high, low = split(sides[...])
    both = dot(
        table_y[...],
        jnp.concatenate(
            [
                jnp.concatenate([high, low], axis=1),
                jnp.concatenate([high, jnp.zeros_like(low)], axis=1),
            ],
            axis=0,
        ),
    )
    high, low = split(both[:, :LANES] + both[:, LANES:])
    table = table_z[...]
    smooth[...] = dot(
        jnp.concatenate([low, high, high], axis=1),
        jnp.concatenate([table[:LANES], table], axis=0),
    )
    n = lines.shape[0]
    straight, turned = sides[:n], sides[n:]
    sides[:n] = turns[2] * straight + turns[3] * turned
    sides[n:] = turns[2] * turned - turns[3] * straight
    factor = column(scale[...])
    for u in range(rows // chunk):
        span = slice(u * chunk * LANES, (u + 1) * chunk * LANES)
        values = (features[:, span].astype(F32) * factor).astype(BF16)
        spectral = jnp.concatenate(
            [
                jnp.concatenate(
                    [
                        smooth[SUB * j : SUB * (j + 1), LANES * t : LANES * (t + 1)]
                        for t in range(TILES)
                    ],
                    axis=0,
                )
                for j in range(u * chunk, (u + 1) * chunk)
            ],
            axis=1,
        )
        pre = spectral + dot(bypass[...], values)
        lifted = (0.5 * gelu_twice(pre)).astype(BF16)
        hidden = (0.5 * gelu_twice(dot(mlp_in_t[...], lifted, ((0,), (0,))))).astype(BF16)
        latent[:, span] = dot(mlp_out[...], hidden).astype(BF16)
    wide = jnp.concatenate([decode[...].astype(F32)] * SUB, axis=1)
    block = lax.broadcasted_iota(jnp.int32, (SUB, SUB * width), 1) // width
    own = block == lax.broadcasted_iota(jnp.int32, (SUB, SUB * width), 0)
    heads = jnp.concatenate(
        [jnp.where(own, wide[0:1], 0.0), jnp.where(own, wide[1:2], 0.0)], axis=0
    ).astype(BF16)
    stacked = jnp.concatenate(
        [
            jnp.concatenate(
                [
                    latent[:, (SUB * a + g) * LANES : (SUB * a + g + 1) * LANES]
                    for a in range(rows // SUB)
                ],
                axis=1,
            )
            for g in range(SUB)
        ],
        axis=0,
    )
    decoded = dot(heads, stacked)
    for a in range(rows // SUB):
        pressure = decoded[:SUB, LANES * a : LANES * (a + 1)]
        saturation = jax.nn.sigmoid(decoded[SUB:, LANES * a : LANES * (a + 1)])
        square = saturation * saturation
        rest = 1.0 - saturation
        at = slice(SUB * a, SUB * (a + 1))
        fields[0, at] = pressure
        fields[1, at] = saturation
        state[0, at] = pressure
        state[1, at] = square / (square + 0.5 * rest * rest)


def joined(first, second):
    both = first + second
    return jnp.where(both > 0.0, first * second / jnp.where(both > 0.0, both, 1.0), 0.0)


def ahead_y(field):
    rolled = pltpu.roll(field, NZ, 1)
    lane = lax.broadcasted_iota(jnp.int32, field.shape, 1)
    row = lax.broadcasted_iota(jnp.int32, field.shape, 0)
    below = pltpu.roll(rolled, field.shape[0] - 1, 0)
    below = jnp.where(row == field.shape[0] - 1, 0.0, below)
    return jnp.where(lane < LANES - NZ, rolled, below)


def behind_y(field):
    rolled = pltpu.roll(field, NZ, 1)
    lane = lax.broadcasted_iota(jnp.int32, field.shape, 1)
    row = lax.broadcasted_iota(jnp.int32, field.shape, 0)
    above = pltpu.roll(rolled, 1, 0)
    above = jnp.where(row == 0, 0.0, above)
    return jnp.where(lane >= NZ, rolled, above)


def ahead_z(field):
    lane = lax.broadcasted_iota(jnp.int32, field.shape, 1)
    return jnp.where(lane % NZ == NZ - 1, 0.0, pltpu.roll(field, LANES - 1, 1))


def behind_z(field):
    lane = lax.broadcasted_iota(jnp.int32, field.shape, 1)
    return jnp.where(lane % NZ == 0, 0.0, pltpu.roll(field, 1, 1))


def inner_kernel(state, rock, opened, partial):
    pressure, mobility, perm = state[0], state[1], rock[0]
    residual = jnp.zeros(pressure.shape, F32)
    for axis, ahead, behind in ((1, ahead_y, behind_y), (2, ahead_z, behind_z)):
        link = opened[axis].astype(F32) * joined(perm, ahead(perm))
        flux = link * (mobility + ahead(mobility)) * (pressure - ahead(pressure))
        residual = residual + (flux - behind(flux))
    partial[...] = residual


def outer_kernel(partial, links, state, after, before, residual):
    pressure, mobility = state[0], state[1]
    upper = links[0] * (mobility + after[1]) * (pressure - after[0])
    lower = links[1] * (before[1] + mobility) * (before[0] - pressure)
    residual[...] = partial[...] + upper - lower


def near(x):
    return pltpu.with_memory_space_constraint(x, pltpu.HBM)


def whole():
    return pl.BlockSpec(memory_space=pltpu.VMEM)


def params():
    return pltpu.CompilerParams(vmem_limit_bytes=40 * 1024 * 1024)


def body(
    features,
    block_scale,
    spec_weight,
    bypass_weight,
    mlp_in,
    mlp_out,
    decode_weight,
    zone_ids,
    face_open,
    perm_table,
):
    width, rows, cells = features.shape
    devices = lax.axis_size("gx")
    planes = rows * devices
    assert rows == 1 and cells == ROWS * LANES and width == TILES * SUB
    plane = features.reshape(width, cells)
    scale = block_scale.reshape(1, width)
    zone = zone_ids.reshape(ROWS, LANES)
    opened = face_open.reshape(3, ROWS, LANES)
    shares = devices // KY
    held = KZ // shares

    steps = 4
    span = cells // steps
    part = span // LANES
    turns = jnp.asarray(turn_tables(part))
    lines, rock = pl.pallas_call(
        forward_kernel,
        grid=(steps,),
        in_specs=[
            pl.BlockSpec((width, span), lambda i: (0, steps - 1 - i)),
            pl.BlockSpec((1, width), lambda i: (0, 0)),
            pl.BlockSpec((ROWS, LANES), lambda i: (0, 0)),
            pl.BlockSpec((1, ROWS, LANES), lambda i: (0, 0, 0)),
            pl.BlockSpec(memory_space=pltpu.SMEM),
            pl.BlockSpec((2 * TILES * LANES, 2 * LANES), lambda i: (0, 0)),
            pl.BlockSpec((2 * KY * SUB, 2 * part * SUB), lambda i: (0, 0)),
            pl.BlockSpec((4, KY * SUB, LANES), lambda i: (0, 0, 0)),
        ],
        out_specs=[
            pl.BlockSpec((KY * SUB, LANES), lambda i: (0, 0)),
            pl.BlockSpec((2, ROWS, LANES), lambda i: (0, 0, 0)),
        ],
        out_shape=[
            jax.ShapeDtypeStruct((KY * SUB, LANES), F32),
            jax.ShapeDtypeStruct((2, ROWS, LANES), F32),
        ],
        scratch_shapes=[pltpu.VMEM((2, KY * SUB, LANES), F32)],
        compiler_params=params(),
        name="forward_yz",
    )(
        near(plane),
        near(scale),
        near(zone),
        near(opened),
        perm_table,
        near(jnp.asarray(z_forward_table())),
        near(jnp.asarray(y_forward_table(part))),
        near(turns),
    )
    up = [(i, i + 1) for i in range(devices - 1)]
    down = [(i + 1, i) for i in range(devices - 1)]
    upper = lax.ppermute(rock[0], "gx", down)
    lower = lax.ppermute(rock[1], "gx", up)

    blocks = lines.reshape(KY, SUB, 2, shares, held * 2 * TILES)
    blocks = blocks.transpose(0, 3, 1, 2, 4).reshape(devices, SUB, 2 * held * 2 * TILES)
    blocks = lax.all_to_all(blocks, "gx", 0, 0, tiled=True)
    lines = blocks.reshape(planes * SUB, 2 * held * 2 * TILES)

    modes = spec_weight.shape[3]
    back, links = pl.pallas_call(
        mix_kernel,
        in_specs=[whole()] * 7,
        out_specs=[whole()] * 2,
        out_shape=[
            jax.ShapeDtypeStruct((planes * SUB, 2 * held * 2 * TILES), F32),
            jax.ShapeDtypeStruct((2, ROWS, LANES), F32),
        ],
        scratch_shapes=[
            pltpu.VMEM((SUB, 2 * TILES, modes), F32),
            pltpu.VMEM((2, modes // LANES, 2 * width, LANES), F32),
        ],
        compiler_params=params(),
        name="mix_modes",
    )(
        lines,
        spec_weight,
        jnp.asarray(x_forward_table(planes)),
        jnp.asarray(x_back_table(planes)),
        rock,
        upper,
        lower,
    )

    blocks = back.reshape(devices, SUB, 2 * held * 2 * TILES)
    blocks = lax.all_to_all(blocks, "gx", 0, 0, tiled=True)
    blocks = blocks.reshape(KY, shares, SUB, 2, held * 2 * TILES).transpose(0, 2, 3, 1, 4)
    lines = blocks.reshape(KY * SUB, 2 * HALF)

    fixed = lambda i: (0, 0)
    fields, state = pl.pallas_call(
        functools.partial(point_kernel, chunk=64),
        grid=(steps,),
        in_specs=[
            pl.BlockSpec((KY * SUB, LANES), fixed),
            pl.BlockSpec((width, span), lambda i: (0, i)),
            pl.BlockSpec((1, width), fixed),
            pl.BlockSpec(bypass_weight.shape, fixed),
            pl.BlockSpec(mlp_in.shape[::-1], fixed),
            pl.BlockSpec(mlp_out.shape, fixed),
            pl.BlockSpec(decode_weight.shape, fixed),
            pl.BlockSpec((part * SUB, 4 * KY * SUB), fixed),
            pl.BlockSpec((2 * LANES, TILES * LANES), fixed),
            pl.BlockSpec((4, KY * SUB, LANES), lambda i: (0, 0, 0)),
        ],
        out_specs=[
            pl.BlockSpec((2, part, LANES), lambda i: (0, i, 0)),
            pl.BlockSpec((2, part, LANES), lambda i: (0, i, 0)),
        ],
        out_shape=[jax.ShapeDtypeStruct((2, ROWS, LANES), F32)] * 2,
        scratch_shapes=[
            pltpu.VMEM((2 * KY * SUB, LANES), F32),
            pltpu.VMEM((part * SUB, TILES * LANES), F32),
            pltpu.VMEM((width, span), BF16),
        ],
        compiler_params=params(),
        name="point_network",
    )(
        lines,
        plane,
        scale,
        bypass_weight,
        mlp_in.T,
        mlp_out,
        decode_weight,
        jnp.asarray(y_back_table(part)),
        jnp.asarray(z_back_table(planes * NY * NZ)),
        turns,
    )
    after = lax.ppermute(state, "gx", down)
    before = lax.ppermute(state, "gx", up)
    partial = pl.pallas_call(
        inner_kernel,
        in_specs=[whole()] * 3,
        out_specs=whole(),
        out_shape=jax.ShapeDtypeStruct((ROWS, LANES), F32),
        compiler_params=params(),
        name="faces_in_plane",
    )(state, rock, opened)
    residual = pl.pallas_call(
        outer_kernel,
        in_specs=[whole()] * 5,
        out_specs=whole(),
        out_shape=jax.ShapeDtypeStruct((ROWS, LANES), F32),
        compiler_params=params(),
        name="faces_between_planes",
    )(partial, links, state, after, before)
    return (fields.reshape(2, 1, cells), residual.reshape(1, cells))


def solution(mesh):
    in_specs = (
        P(None, ("groups", "gx"), None),
        P(None, ("groups", "gx")),
        P(None, None, None, "gx"),
        P(),
        P(),
        P(),
        P(),
        P(("groups", "gx"), None),
        P(None, ("groups", "gx"), None),
        P(),
    )
    out_specs = (P(None, ("groups", "gx"), None), P(("groups", "gx"), None))
    return jax.shard_map(body, mesh=mesh, in_specs=in_specs, out_specs=out_specs, check_vma=False)
```

profile of v0, /device:TPU:1, one launch (start us, length us, event | category | flops | bytes accessed | tf_op | source)
XLA Modules:
  0.0 73.8 jit_solution(10013313722328414823)
XLA Ops:
  0.6 0.0 copy-start.17
  0.6 0.6 copy-done.17
  1.3 0.0 copy-start.5
  1.3 0.0 copy-start.14
  1.3 8.4 %forward_yz.1 = (f32[256,128]{1,0:T(8,128)S(1)}, f32[2,256,128]{2,1,0:T(8,128)S(1)}) custom-call(bf16[32,32768]{1,0:T(8,128)(2,1)} %bitcast.15, f32[1,32]{1,0:T(1,128)} %bitcast.24, s32[256,128]{1,0:T(8,128)} %bitcast.26, s32[3,256,128]{2,1,0:T(8,128)} %bitcast.17, f32[8]{0:T(128)S(1)} %copy-done.17, bf16[1024,256]{1,0:T(8,128)(2,1)} %constant.15.clone.table_z, ...), custom_call_target="tpu_custom_call" | custom-call | tf_op jit(solution)/shard_map/forward_yz/pallas_call | solution.py:445
  9.7 0.0 copy-start.8
  9.7 0.6 copy-done.8
  10.3 0.0 copy-start
  10.3 0.0 copy-start.1
  10.3 7.1 %all-to-all-start = ((f32[32,8,128]{2,1,0:T(8,128)}), f32[32,8,128]{2,1,0:T(8,128)S(1)}, u32[]{:S(2)}, u32[]{:S(2)}) async-start(f32[32,8,128]{2,1,0:T(8,128)} %bitcast.21), calls=%async_computation | async-start | bytes 262144 | tf_op jit(solution)/shard_map/all_to_all | solution.py:486
  17.5 3.5 %collective-permute-start.1 = (f32[256,128]{1,0:T(8,128)S(1)}, f32[256,128]{1,0:T(8,128)S(1)}, u32[]{:S(2)}, u32[]{:S(2)}) collective-permute-start(f32[256,128]{1,0:T(8,128)S(1)} %get-tuple-element.16), channel_id=1, source_target_pairs={{0,1},{1,2},{2,3},{3,4},{4,5},{5,6},{6,7},{7,8},{8,9},{9,10},{10,1... | collective-permute-start | bytes 393224 | tf_op jit(solution)/shard_map/ppermute | solution.py:482
  21.0 1.9 %collective-permute-start = (f32[256,128]{1,0:T(8,128)S(1)}, f32[256,128]{1,0:T(8,128)S(1)}, u32[]{:S(2)}, u32[]{:S(2)}) collective-permute-start(f32[256,128]{1,0:T(8,128)S(1)} %get-tuple-element.17), channel_id=1, source_target_pairs={{1,0},{2,1},{3,2},{4,3},{5,4},{6,5},{7,6},{8,7},{9,8},{10,9},{11,1... | collective-permute-start | bytes 393224 | tf_op jit(solution)/shard_map/ppermute | solution.py:481
  22.9 0.3 collective-permute-done.1.lower
  23.3 0.0 copy-start.9
  23.3 0.7 copy-done.9
  23.9 3.4 %collective-permute-done.upper = f32[256,128]{1,0:T(8,128)S(1)} collective-permute-done((f32[256,128]{1,0:T(8,128)S(1)}, f32[256,128]{1,0:T(8,128)S(1)}, u32[]{:S(2)}, u32[]{:S(2)}) %collective-permute-start) | collective-permute-done | bytes 131104 | tf_op jit(solution)/shard_map/ppermute | solution.py:481
  27.3 0.0 copy-start.11
  27.3 0.7 copy-done.11
  28.0 0.0 all-to-all-done
  28.0 0.0 copy-start.3
  28.0 0.0 copy-done.5
  28.0 0.0 copy-start.4
  28.0 1.3 %copy-done.4 = bf16[2,32,32,256]{3,2,1,0:T(8,128)(2,1)S(1)} copy-done((bf16[2,32,32,256]{3,2,1,0:T(8,128)(2,1)S(1)}, bf16[2,32,32,256]{3,2,1,0:T(8,128)(2,1)}, u32[]{:S(2)}) %copy-start.4) | copy-done | bytes 1048600
  29.3 0.0 copy-start.6
  29.3 1.0 %copy-done.6 = f32[512,256]{1,0:T(8,128)S(1)} copy-done((f32[512,256]{1,0:T(8,128)S(1)}, f32[512,256]{1,0:T(8,128)}, u32[]{:S(2)}) %copy-start.6) | copy-done | bytes 524312
  30.3 0.0 copy-start.10
  30.3 0.9 %copy-done.10 = f32[256,128]{1,0:T(8,128)S(1)} copy-done((f32[256,128]{1,0:T(8,128)S(1)}, f32[256,128]{1,0:T(8,128)}, u32[]{:S(2)}) %copy-start.10) | copy-done | bytes 131096
  31.2 0.9 %copy-done.12 = f32[256,128]{1,0:T(8,128)S(1)} copy-done((f32[256,128]{1,0:T(8,128)S(1)}, f32[256,128]{1,0:T(8,128)}, u32[]{:S(2)}) %copy-start.12) | copy-done | bytes 131096
  32.1 2.0 %mix_modes.1 = (f32[256,128]{1,0:T(8,128)S(1)}, f32[2,256,128]{2,1,0:T(8,128)S(1)}) custom-call(f32[256,128]{1,0:T(8,128)S(1)} %bitcast.20, bf16[2,32,32,256]{3,2,1,0:T(8,128)(2,1)S(1)} %copy-done.4, f32[512,256]{1,0:T(8,128)S(1)} %copy-done.6, f32[256,512]{1,0:T(8,128)S(1)} %copy-done.5, f32[2,256,128]{2,1,0:T(8,128)S(1)} %get-tuple-element.9.rock, ...), custom_call_target="tpu_custom_call" | custom-call | tf_op jit(solution)/shard_map/mix_modes/pallas_call | solution.py:490
  34.2 14.2 %all_to_all.10 = f32[32,8,128]{2,1,0:T(8,128)S(1)} all-to-all(f32[32,8,128]{2,1,0:T(8,128)S(1)} %bitcast.22), channel_id=1, replica_groups=mesh['groups'=1,'gx'=32] {'gx'}, dimensions={0} | all-to-all | bytes 262144 | tf_op jit(solution)/shard_map/all_to_all | solution.py:515
  48.4 0.0 copy-done.13
  48.4 0.0 copy-done.14
  48.4 0.0 copy-done
  48.4 0.0 copy-done.1
  48.4 0.0 copy-done.3
  48.5 0.0 copy-done.15
  48.5 0.0 copy-done.16
  48.5 0.0 copy-done.18
  48.5 0.0 copy-start.7
  48.5 1.0 %copy-done.7 = bf16[256,512]{1,0:T(8,128)(2,1)S(1)} copy-done((bf16[256,512]{1,0:T(8,128)(2,1)S(1)}, bf16[256,512]{1,0:T(8,128)(2,1)}, u32[]{:S(2)}) %copy-start.7) | copy-done | bytes 262168
  49.5 13.4 %point_network.1 = (f32[2,256,128]{2,1,0:T(8,128)}, f32[2,256,128]{2,1,0:T(8,128)S(1)}) custom-call(f32[256,128]{1,0:T(8,128)S(1)} %bitcast.19, bf16[32,32768]{1,0:T(8,128)(2,1)S(1)} %bitcast.16, f32[1,32]{1,0:T(1,128)S(1)} %bitcast.25, bf16[32,32]{1,0:T(8,128)(2,1)S(1)} %copy-done.13, bf16[32,128]{1,0:T(8,128)(2,1)S(1)} %bitcast.23, ...), custom_call_target="tpu_custom_call" | custom-call | tf_op jit(solution)/shard_map/point_network/pallas_call | solution.py:520
  62.9 2.2 %collective-permute-start.3 = (f32[2,256,128]{2,1,0:T(8,128)S(1)}, f32[2,256,128]{2,1,0:T(8,128)S(1)}, u32[]{:S(2)}, u32[]{:S(2)}) collective-permute-start(f32[2,256,128]{2,1,0:T(8,128)S(1)} %get-tuple-element.12.state), channel_id=1, source_target_pairs={{0,1},{1,2},{2,3},{3,4},{4,5},{5,6},{6,7},{7,8},{8,9},{9,10},{10,1... | collective-permute-start | bytes 786440 | tf_op jit(solution)/shard_map/ppermute | solution.py:560
  65.2 2.1 %collective-permute-start.2 = (f32[2,256,128]{2,1,0:T(8,128)S(1)}, f32[2,256,128]{2,1,0:T(8,128)S(1)}, u32[]{:S(2)}, u32[]{:S(2)}) collective-permute-start(f32[2,256,128]{2,1,0:T(8,128)S(1)} %get-tuple-element.12.state), channel_id=1, source_target_pairs={{1,0},{2,1},{3,2},{4,3},{5,4},{6,5},{7,6},{8,7},{9,8},{10,9},{11,1... | collective-permute-start | bytes 786440 | tf_op jit(solution)/shard_map/ppermute | solution.py:559
  67.3 0.0 copy-done.2
  67.3 0.4 faces_in_plane.1.partial
  67.7 0.8 %collective-permute-done.3.before = f32[2,256,128]{2,1,0:T(8,128)S(1)} collective-permute-done((f32[2,256,128]{2,1,0:T(8,128)S(1)}, f32[2,256,128]{2,1,0:T(8,128)S(1)}, u32[]{:S(2)}, u32[]{:S(2)}) %collective-permute-start.3) | collective-permute-done | bytes 262176 | tf_op jit(solution)/shard_map/ppermute | solution.py:560
  68.5 4.7 %collective-permute-done.2.after = f32[2,256,128]{2,1,0:T(8,128)S(1)} collective-permute-done((f32[2,256,128]{2,1,0:T(8,128)S(1)}, f32[2,256,128]{2,1,0:T(8,128)S(1)}, u32[]{:S(2)}, u32[]{:S(2)}) %collective-permute-start.2) | collective-permute-done | bytes 262176 | tf_op jit(solution)/shard_map/ppermute | solution.py:559
  73.1 0.7 faces_between_planes.1
  (7 shorter events, 0.0 us)
Async XLA Ops:
  0.6 0.7 copy-start.17
  1.3 26.7 %copy-start.5 = (f32[256,512]{1,0:T(8,128)S(1)}, f32[256,512]{1,0:T(8,128)}, u32[]{:S(2)}) copy-start(f32[256,512]{1,0:T(8,128)} %constant.18.clone.table_back) | copy-start | bytes 1572868
  1.3 47.1 %copy-start.13 = (bf16[32,32]{1,0:T(8,128)(2,1)S(1)}, bf16[32,32]{1,0:T(8,128)(2,1)}, u32[]{:S(2)}) copy-start(bf16[32,32]{1,0:T(8,128)(2,1)} %bypass.1) | copy-start | bytes 6148
  1.3 47.1 %copy-start.14 = (bf16[128,32]{0,1:T(8,128)(2,1)S(1)}, bf16[128,32]{0,1:T(8,128)(2,1)}, u32[]{:S(2)}) copy-start(bf16[128,32]{0,1:T(8,128)(2,1)} %param.21) | copy-start | bytes 24580
  9.7 0.7 copy-start.8
  10.3 38.1 %copy-start = (bf16[32,1,32768]{2,0,1:T(8,128)(2,1)S(1)}, bf16[32,1,32768]{2,0,1:T(8,128)(2,1)}, u32[]{:S(2)}) copy-start(bf16[32,1,32768]{2,0,1:T(8,128)(2,1)} %param.17) | copy-start | bytes 6291460
  10.3 38.1 %copy-start.1 = (f32[4,256,128]{2,1,0:T(8,128)S(1)}, f32[4,256,128]{2,1,0:T(8,128)}, u32[]{:S(2)}) copy-start(f32[4,256,128]{2,1,0:T(8,128)} %constant.14.clone.turns) | copy-start | bytes 1572868
  10.3 17.6 %all-to-all-start = ((f32[32,8,128]{2,1,0:T(8,128)}), f32[32,8,128]{2,1,0:T(8,128)S(1)}, u32[]{:S(2)}, u32[]{:S(2)}) async-start(f32[32,8,128]{2,1,0:T(8,128)} %bitcast.21), calls=%async_computation | async-start | bytes 262144 | tf_op jit(solution)/shard_map/all_to_all | solution.py:486
  17.5 5.8 %collective-permute-start.1 = (f32[256,128]{1,0:T(8,128)S(1)}, f32[256,128]{1,0:T(8,128)S(1)}, u32[]{:S(2)}, u32[]{:S(2)}) collective-permute-start(f32[256,128]{1,0:T(8,128)S(1)} %get-tuple-element.16), channel_id=1, source_target_pairs={{0,1},{1,2},{2,3},{3,4},{4,5},{5,6},{6,7},{7,8},{8,9},{9,10},{10,1... | collective-permute-start | bytes 393224 | tf_op jit(solution)/shard_map/ppermute | solution.py:482
  21.0 6.3 %collective-permute-start = (f32[256,128]{1,0:T(8,128)S(1)}, f32[256,128]{1,0:T(8,128)S(1)}, u32[]{:S(2)}, u32[]{:S(2)}) collective-permute-start(f32[256,128]{1,0:T(8,128)S(1)} %get-tuple-element.17), channel_id=1, source_target_pairs={{1,0},{2,1},{3,2},{4,3},{5,4},{6,5},{7,6},{8,7},{9,8},{10,9},{11,1... | collective-permute-start | bytes 393224 | tf_op jit(solution)/shard_map/ppermute | solution.py:481
  23.3 0.7 copy-start.9
  27.3 0.7 copy-start.11
  28.0 20.5 %copy-start.3 = (bf16[512,1024]{1,0:T(8,128)(2,1)S(1)}, bf16[512,1024]{1,0:T(8,128)(2,1)}, u32[]{:S(2)}) copy-start(bf16[512,1024]{1,0:T(8,128)(2,1)} %constant.19.clone.table_y) | copy-start | bytes 3145732
  28.0 1.3 %copy-start.4 = (bf16[2,32,32,256]{3,2,1,0:T(8,128)(2,1)S(1)}, bf16[2,32,32,256]{3,2,1,0:T(8,128)(2,1)}, u32[]{:S(2)}) copy-start(bf16[2,32,32,256]{3,2,1,0:T(8,128)(2,1)} %weight.1) | copy-start | bytes 3145732
  29.3 1.0 %copy-start.6 = (f32[512,256]{1,0:T(8,128)S(1)}, f32[512,256]{1,0:T(8,128)}, u32[]{:S(2)}) copy-start(f32[512,256]{1,0:T(8,128)} %constant.17.clone.table_x) | copy-start | bytes 1572868
  30.3 0.9 %copy-start.10 = (f32[256,128]{1,0:T(8,128)S(1)}, f32[256,128]{1,0:T(8,128)}, u32[]{:S(2)}) copy-start(f32[256,128]{1,0:T(8,128)} %copy-done.9) | copy-start | bytes 393220
  31.2 0.9 %copy-start.12 = (f32[256,128]{1,0:T(8,128)S(1)}, f32[256,128]{1,0:T(8,128)}, u32[]{:S(2)}) copy-start(f32[256,128]{1,0:T(8,128)} %copy-done.11) | copy-start | bytes 393220
  32.1 16.3 %copy-start.15 = (bf16[32,128]{1,0:T(8,128)(2,1)S(1)}, bf16[32,128]{1,0:T(8,128)(2,1)}, u32[]{:S(2)}) copy-start(bf16[32,128]{1,0:T(8,128)(2,1)} %mlp_out.1) | copy-start | bytes 24580
  32.1 16.3 %copy-start.16 = (f32[32,1]{0,1:T(1,128)S(1)}, f32[32,1]{0,1:T(1,128)}, u32[]{:S(2)}) copy-start(f32[32,1]{0,1:T(1,128)} %param.18) | copy-start | bytes 388
  32.1 16.3 %copy-start.18 = (bf16[2,32]{1,0:T(2,128)(2,1)S(1)}, bf16[2,32]{1,0:T(2,128)(2,1)}, u32[]{:S(2)}) copy-start(bf16[2,32]{1,0:T(2,128)(2,1)} %decode.1) | copy-start | bytes 388
  48.4 18.8 %copy-start.2 = (s32[3,1,32768]{2,1,0:T(1,128)S(1)}, s32[3,1,32768]{2,1,0:T(1,128)}, u32[]{:S(2)}) copy-start(s32[3,1,32768]{2,1,0:T(1,128)} %param.25) | copy-start | bytes 1179652
  48.5 1.0 %copy-start.7 = (bf16[256,512]{1,0:T(8,128)(2,1)S(1)}, bf16[256,512]{1,0:T(8,128)(2,1)}, u32[]{:S(2)}) copy-start(bf16[256,512]{1,0:T(8,128)(2,1)} %constant.20.clone.table_z) | copy-start | bytes 786436
  62.9 5.5 %collective-permute-start.3 = (f32[2,256,128]{2,1,0:T(8,128)S(1)}, f32[2,256,128]{2,1,0:T(8,128)S(1)}, u32[]{:S(2)}, u32[]{:S(2)}) collective-permute-start(f32[2,256,128]{2,1,0:T(8,128)S(1)} %get-tuple-element.12.state), channel_id=1, source_target_pairs={{0,1},{1,2},{2,3},{3,4},{4,5},{5,6},{6,7},{7,8},{8,9},{9,10},{10,1... | collective-permute-start | bytes 786440 | tf_op jit(solution)/shard_map/ppermute | solution.py:560
  65.2 7.9 %collective-permute-start.2 = (f32[2,256,128]{2,1,0:T(8,128)S(1)}, f32[2,256,128]{2,1,0:T(8,128)S(1)}, u32[]{:S(2)}, u32[]{:S(2)}) collective-permute-start(f32[2,256,128]{2,1,0:T(8,128)S(1)} %get-tuple-element.12.state), channel_id=1, source_target_pairs={{1,0},{2,1},{3,2},{4,3},{5,4},{6,5},{7,6},{8,7},{9,8},{10,9},{11,1... | collective-permute-start | bytes 786440 | tf_op jit(solution)/shard_map/ppermute | solution.py:559
where the time goes:
time: 75 us; the launch traced here: 73.8 us
  Pallas kernels  25 us (33%)
  starting transfers between devices  16.9 us (23%)
  blocking collectives  14.2 us (19%)
  waiting for transfers between devices  9.1 us (12%)
  local copies, waits for them, and re-layouts  7.82 us (10%)
  between operations  0.8 us (1%)
    all_to_all x1, blocking collectives, body(): blocks = lax.all_to_all(blocks, 'gx', 0, 0, tiled=True)  14.2 us
    pallas_call x1, Pallas kernels, body(): pl.pallas_call(functools.partial(point_kernel, chunk=64), grid=(steps,),...  13.4 us
    pallas_call x1, Pallas kernels, body(): pl.pallas_call(forward_kernel, grid=(steps,), in_specs=[pl.BlockSpec((wid...  8.36 us
    unnamed x38, local copies, waits for them, and re-layouts  7.8 us
    all_to_all x1, starting transfers between devices, body(): blocks = lax.all_to_all(blocks, 'gx', 0, 0, tiled=True)  7.1 us
    ppermute x1, waiting for transfers between devices, body(): after = lax.ppermute(state, 'gx', down)  4.65 us
    ppermute x1, starting transfers between devices, body(): lower = lax.ppermute(rock[1], 'gx', up)  3.54 us
    ppermute x1, waiting for transfers between devices, body(): upper = lax.ppermute(rock[0], 'gx', down)  3.38 us
  transfers between devices with their start and end apart: 5, of which 4 were waited for; matrix products, arithmetic and copies ran while one was open for 0% of the time, Pallas kernels for 1%

commit v1 on v0

v1 whole, which is shorter than its diff:
```python
import math

import jax
import jax.numpy as jnp
import ml_dtypes
import numpy as np
from jax import lax
from jax.experimental import pallas as pl
from jax.experimental.pallas import tpu as pltpu
from jax.sharding import PartitionSpec as P

NY = 512
NZ = 64
KX = 32
KY = 32
KZ = 8
ZONES = 8
LANES = 128
SUB = 8
PAIRS = LANES // NZ
ROWS = NY // PAIRS
TILES = 4
TWO = 2
HALF = KZ * 2 * TILES
FOLD = KY // 2
GELU_A = math.sqrt(2.0 / math.pi)
GELU_B = GELU_A * 0.044715
F32 = jnp.float32
BF16 = jnp.bfloat16


def signed(count):
    steps = np.arange(count)
    return np.where(steps < count // 2, steps, steps - count)


def angles(freqs, positions, length):
    return 2.0 * np.pi * ((freqs[:, None] * positions[None, :]) % length) / length


def halves(table, axis):
    high = np.asarray(table, np.float64).astype(ml_dtypes.bfloat16)
    low = (table - high.astype(np.float64)).astype(ml_dtypes.bfloat16)
    return np.concatenate([high, low], axis=axis)


def spread(small):
    return np.kron(small, np.eye(SUB))


def z_forward_table():
    angle = angles(np.arange(KZ), np.arange(NZ), NZ)
    table = np.zeros((TWO, PAIRS, NZ, 2, KZ, PAIRS, 2, TWO))
    for t in range(TWO):
        for p in range(PAIRS):
            table[t, p, :, 0, :, p, 0, t] = np.cos(angle).T
            table[t, p, :, 0, :, p, 1, t] = -np.sin(angle).T
            table[t, p, :, 1, :, p, 0, t] = -np.sin(angle).T
            table[t, p, :, 1, :, p, 1, t] = -np.cos(angle).T
    return halves(table.reshape(TWO * LANES, LANES), 1)


def y_forward_table(rows):
    angle = angles(np.arange(FOLD + 1), np.arange(rows) * PAIRS, NY)
    return halves(np.concatenate([spread(np.cos(angle)), spread(np.sin(angle[1:]))], axis=0), 1)


def turn_forward_table(rows):
    freqs = np.arange(FOLD + 1)
    parity = angles(freqs, np.arange(PAIRS), NY)
    parity = np.tile(np.repeat(parity, 2 * TWO, axis=1), (1, 2 * KZ))
    step = np.repeat(angles(freqs, np.array([rows * PAIRS]), NY), LANES, axis=1)
    return np.stack([np.cos(parity), np.sin(parity), np.cos(step), np.sin(step)]).astype(np.float32)


def turn_back_table(rows):
    parity = np.repeat(angles(signed(KY), np.array([1]), NY), LANES, axis=1)
    step = np.repeat(angles(np.arange(1, FOLD + 1), np.array([rows * PAIRS]), NY), LANES, axis=1)
    both = np.concatenate([parity, step], axis=0)
    return np.stack([np.cos(both), np.sin(both)]).astype(np.float32)


def x_forward_table(planes):
    angle = angles(signed(KX), np.arange(planes), planes)

    def one(small):
        wide = np.zeros((planes, SUB, SUB, KX))
        for s in range(SUB):
            wide[:, s, s, :] = small.T
        return wide.reshape(planes * SUB, SUB * KX)

    return np.concatenate([one(np.cos(angle)), one(np.sin(angle))], axis=0).astype(np.float32)


def x_back_table(planes):
    table = x_forward_table(planes).reshape(2, planes * SUB, SUB * KX)
    return np.concatenate([table[0], table[1]], axis=1)


def y_back_table(rows):
    angle = angles(np.arange(1, FOLD + 1), np.arange(rows) * PAIRS, NY)
    return halves(np.concatenate([spread(np.cos(angle).T), spread(np.sin(angle).T)], axis=1), 1)


def z_back_table(total):
    angle = angles(np.arange(KZ), np.arange(NZ), NZ)
    weight = np.where(np.arange(KZ) == 0, 1.0, 2.0)[:, None] / total
    table = np.zeros((PAIRS, KZ, TILES // TWO, 2, TWO, TILES, PAIRS, NZ))
    for t in range(TILES):
        for p in range(PAIRS):
            table[p, :, t // TWO, 0, t % TWO, t, p, :] = weight * np.cos(angle)
            table[p, :, t // TWO, 1, t % TWO, t, p, :] = -weight * np.sin(angle)
    return halves(table.reshape(PAIRS * HALF, TILES * LANES), 0)


def dot(a, b, dims=((1,), (0,)), precision=None):
    return lax.dot_general(a, b, (dims, ((), ())), precision=precision, preferred_element_type=F32)


def split(x):
    high = x.astype(BF16)
    return high, (x - high.astype(F32)).astype(BF16)


def column(row):
    n = row.shape[1]
    square = lax.broadcasted_iota(jnp.int32, (n, n), 0) == lax.broadcasted_iota(jnp.int32, (n, n), 1)
    return jnp.sum(jnp.where(square, row, 0.0), axis=1, keepdims=True)


def tall(table, first, count):
    return jnp.concatenate(
        [jnp.broadcast_to(table[k : k + 1], (SUB, LANES)) for k in range(first, first + count)],
        axis=0,
    )


def twice(x):
    return jnp.concatenate([x, x], axis=1)


def forward_kernel(features, scale, table_z, table_y, turns, lines, total):
    step = pl.program_id(0)
    rows = features.shape[1] // LANES

    @pl.when(step == 0)
    def _():
        total[...] = jnp.zeros_like(total)

    values = features[...].astype(F32) * column(scale[...])

    def tile(t, j):
        return values[SUB * t : SUB * (t + 1), LANES * j : LANES * (j + 1)]

    cells = jnp.concatenate(
        [
            jnp.concatenate([tile(t, j), tile(t + 1, j)], axis=1)
            for t in range(0, TILES, TWO)
            for j in range(rows)
        ],
        axis=0,
    ).astype(BF16)
    part = dot(cells, table_z[...])
    part = part[:, :LANES] + part[:, LANES:]
    high, low = split(jnp.concatenate([part[: SUB * rows], part[SUB * rows :]], axis=1))
    table = table_y[...]
    inner = table.shape[1] // 2
    sums = dot(
        jnp.concatenate([table[:, :inner], table], axis=1),
        jnp.concatenate([low, high, high], axis=0),
    )
    n = (FOLD + 1) * SUB
    cosine = twice(tall(turns[2], 0, FOLD + 1))
    sine = twice(tall(turns[3], 0, FOLD + 1))
    first, second = total[0], total[1]
    total[0] = sums[:n] + cosine * first - sine * second
    total[1] = sine * first + cosine * second
    total[1, SUB:] += sums[n:]

    @pl.when(step == pl.num_programs(0) - 1)
    def _():
        cosine = twice(tall(turns[0], 0, FOLD + 1))
        sine = twice(tall(turns[1], 0, FOLD + 1))
        even = cosine * total[0] - sine * total[1]
        odd = sine * total[0] + cosine * total[1]
        lane = lax.broadcasted_iota(jnp.int32, (n, LANES), 1)
        own = lane // (2 * TWO) % 2 == 0

        def packed(sign):
            sides = []
            for k in range(2):
                at = slice(LANES * k, LANES * (k + 1))
                turned = pltpu.roll(odd[:, at], HALF, 1)
                whole_line = even[:, at] + jnp.where(lane < HALF, sign, -sign) * turned
                shift = LANES - 2 * TWO if k == 0 else 2 * TWO
                sides.append(whole_line + pltpu.roll(whole_line, shift, 1))
            return jnp.where(own, sides[0], sides[1])

        up, down = packed(1.0), packed(-1.0)
        lines[: FOLD * SUB] = up[: FOLD * SUB]
        for k in range(FOLD, 0, -1):
            at = (KY - k) * SUB
            lines[at : at + SUB] = down[SUB * k : SUB * (k + 1)]


def swap_blocks(pieces):
    lane = lax.broadcasted_iota(jnp.int32, pieces[0].shape, 1) // KX
    out = []
    for e in range(4):
        got = None
        for b in range(4):
            moved = pieces[b] if b == e else pltpu.roll(pieces[b], (KX * (b - e)) % LANES, 1)
            got = moved if got is None else jnp.where(lane == b, moved, got)
        out.append(got)
    return out


def mix_kernel(lines, weight, table_x, table_back, back, modes, mixed):
    highest = lax.Precision.HIGHEST
    half = lines.shape[1] // 2
    count = half // (2 * TILES)
    groups = count // 4
    flipped = lines[...].T
    pair = jnp.concatenate([flipped[:half], flipped[half:]], axis=1)
    spectrum = dot(pair, table_x[...], precision=highest)
    for c in range(SUB // 4):
        for a in range(groups):
            got = swap_blocks(
                [
                    spectrum[SUB * (4 * a + b) : SUB * (4 * a + b + 1), LANES * c : LANES * (c + 1)]
                    for b in range(4)
                ]
            )
            for e in range(4):
                modes[4 * c + e, :, LANES * a : LANES * (a + 1)] = got[e]
    width = weight.shape[1]
    real = jnp.zeros((width, count * KX), F32)
    imag = jnp.zeros((width, count * KX), F32)
    for i in range(width):
        t, v = i // SUB, i % SUB
        at = t // TWO * 2 * TWO + t % TWO
        in_real = modes[v, at : at + 1, :]
        in_imag = modes[v, at + TWO : at + TWO + 1, :]
        w_real = weight[0, i].astype(F32)
        w_imag = weight[1, i].astype(F32)
        real += in_real * w_real - in_imag * w_imag
        imag += in_real * w_imag + in_imag * w_real
    for a in range(groups):
        for t in range(TILES):
            here = slice(SUB * t, SUB * (t + 1)), slice(LANES * a, LANES * (a + 1))
            at = (t // TWO * 2 * TWO + t % TWO) * SUB
            mixed[0, a, at : at + SUB] = real[here]
            mixed[1, a, at : at + SUB] = -imag[here]
            at += TWO * SUB
            mixed[0, a, at : at + SUB] = imag[here]
            mixed[1, a, at : at + SUB] = real[here]
    rows = []
    for k in range(2):
        seen = [
            [mixed[k, a, pl.ds(v, 2 * TILES, stride=SUB), :] for v in range(SUB)]
            for a in range(groups)
        ]
        parts = [[None] * (SUB // 4) for _ in range(count)]
        for c in range(SUB // 4):
            for a in range(groups):
                got = swap_blocks(seen[a][4 * c : 4 * c + 4])
                for b in range(4):
                    parts[4 * a + b][c] = got[b]
        rows.append(jnp.concatenate([jnp.concatenate(p, axis=1) for p in parts], axis=0))
    straight, turned = rows
    sides = jnp.concatenate(
        [
            jnp.concatenate([straight, turned], axis=1),
            jnp.concatenate([turned, -straight], axis=1),
        ],
        axis=0,
    )
    back[...] = dot(table_back[...], sides, ((1,), (1,)), precision=highest)


def gelu_twice(x):
    return x + x * jnp.tanh(x * (GELU_A + GELU_B * (x * x)))


def point_kernel(
    lines,
    features,
    scale,
    bypass,
    mlp_in_t,
    mlp_out,
    decode,
    zone,
    opened,
    perm_table,
    table_y,
    table_z,
    turns,
    fields,
    near_side,
    far_side,
    sides,
    smooth,
):
    n = FOLD * SUB

    @pl.when(pl.program_id(0) == 0)
    def _():
        held = lines[...]
        other = pltpu.roll(held, HALF, 1)
        low = lax.broadcasted_iota(jnp.int32, held.shape, 1) < HALF
        cosine, sine = tall(turns[0], 0, KY), tall(turns[1], 0, KY)
        straight = jnp.where(low, held, cosine * other + sine * held)
        turned = jnp.where(low, other, cosine * held - sine * other)

        def at(x, k):
            return x[SUB * k : SUB * (k + 1)]

        for k in range(1, FOLD):
            here = slice(SUB * (k - 1), SUB * k)
            sides[0, here] = at(straight, k) + at(straight, KY - k)
            sides[1, here] = at(turned, k) - at(turned, KY - k)
        sides[0, n - SUB : n] = at(straight, FOLD)
        sides[1, n - SUB : n] = -at(turned, FOLD)
        sides[0, n:] = at(straight, 0)

    rows = features.shape[1] // LANES
    width = features.shape[0]
    even, odd = sides[0, :n], sides[1, :n]
    high, low = split(jnp.concatenate([even, odd], axis=0))
    both = jnp.concatenate([high, low], axis=1)
    both = dot(table_y[...], jnp.concatenate([both, both], axis=0))
    level = jnp.concatenate([sides[0, n:]] * rows, axis=0)
    high, low = split(both[:, :LANES] + both[:, LANES:] + level)
    table = table_z[...]
    smooth[...] = dot(
        jnp.concatenate([low, high, high], axis=1),
        jnp.concatenate([table[:LANES], table], axis=0),
    )
    cosine, sine = tall(turns[0], KY, FOLD), tall(turns[1], KY, FOLD)
    sides[0, :n] = cosine * even + sine * odd
    sides[1, :n] = cosine * odd - sine * even

    values = (features[...].astype(F32) * column(scale[...])).astype(BF16)
    spectral = jnp.concatenate(
        [
            jnp.concatenate(
                [
                    smooth[SUB * j : SUB * (j + 1), LANES * t : LANES * (t + 1)]
                    for t in range(TILES)
                ],
                axis=0,
            )
            for j in range(rows)
        ],
        axis=1,
    )
    lifted = gelu_twice(spectral + dot(bypass[...], values)).astype(BF16)
    inner = (0.5 * mlp_in_t[...].astype(F32)).astype(BF16)
    hidden = gelu_twice(dot(inner, lifted, ((0,), (0,)))).astype(BF16)

    heads = dot(decode[...], mlp_out[...])
    count = heads.shape[1]
    group = lax.broadcasted_iota(jnp.int32, (SUB, SUB * count), 1) // count
    own = group == lax.broadcasted_iota(jnp.int32, (SUB, SUB * count), 0)
    wide = jnp.concatenate([heads] * SUB, axis=1)
    wide = jnp.concatenate([jnp.where(own, wide[k : k + 1], 0.0) for k in range(2)], axis=0)
    stacked = jnp.concatenate(
        [
            jnp.concatenate(
                [
                    hidden[:, (SUB * a + g) * LANES : (SUB * a + g + 1) * LANES]
                    for a in range(rows // SUB)
                ],
                axis=1,
            )
            for g in range(SUB)
        ],
        axis=0,
    )
    decoded = dot(jnp.concatenate(split(0.5 * wide), axis=0), stacked)
    decoded = decoded[: 2 * SUB] + decoded[2 * SUB :]
    even_plane = lax.axis_index("gx") % 2 == 0
    for a in range(rows // SUB):
        pressure = decoded[:SUB, LANES * a : LANES * (a + 1)]
        saturation = jax.nn.sigmoid(decoded[SUB:, LANES * a : LANES * (a + 1)])
        square = saturation * saturation
        rest = 1.0 - saturation
        at = slice(SUB * a, SUB * (a + 1))
        fields[0, at] = pressure
        fields[1, at] = saturation
        mobility = square / (square + 0.5 * rest * rest)
        perm = lookup(zone[at], perm_table)
        gated = perm * opened[0, at].astype(F32)
        near_side[0, at] = pressure
        near_side[1, at] = mobility
        near_side[2, at] = jnp.where(even_plane, gated, perm)
        far_side[0, at] = pressure
        far_side[1, at] = mobility
        far_side[2, at] = jnp.where(even_plane, perm, gated)


def lookup(zones, perm_table):
    perm = jnp.zeros(zones.shape, F32)
    for k in range(ZONES):
        perm = jnp.where(zones == k, perm_table[k], perm)
    return perm


def joined(first, second):
    both = first + second
    return jnp.where(both > 0.0, first * second / jnp.where(both > 0.0, both, 1.0), 0.0)


def ahead_y(field):
    rolled = pltpu.roll(field, NZ, 1)
    lane = lax.broadcasted_iota(jnp.int32, field.shape, 1)
    row = lax.broadcasted_iota(jnp.int32, field.shape, 0)
    below = pltpu.roll(rolled, field.shape[0] - 1, 0)
    below = jnp.where(row == field.shape[0] - 1, 0.0, below)
    return jnp.where(lane < LANES - NZ, rolled, below)


def behind_y(field):
    rolled = pltpu.roll(field, NZ, 1)
    lane = lax.broadcasted_iota(jnp.int32, field.shape, 1)
    row = lax.broadcasted_iota(jnp.int32, field.shape, 0)
    above = pltpu.roll(rolled, 1, 0)
    above = jnp.where(row == 0, 0.0, above)
    return jnp.where(lane >= NZ, rolled, above)


def ahead_z(field):
    lane = lax.broadcasted_iota(jnp.int32, field.shape, 1)
    return jnp.where(lane % NZ == NZ - 1, 0.0, pltpu.roll(field, LANES - 1, 1))


def behind_z(field):
    lane = lax.broadcasted_iota(jnp.int32, field.shape, 1)
    return jnp.where(lane % NZ == 0, 0.0, pltpu.roll(field, 1, 1))


def inner_kernel(side, zone, opened, perm_table, partial):
    pressure, mobility = side[0], side[1]
    perm = lookup(zone[...], perm_table)
    residual = jnp.zeros(pressure.shape, F32)
    for axis, ahead, behind in ((1, ahead_y, behind_y), (2, ahead_z, behind_z)):
        link = opened[axis].astype(F32) * joined(perm, ahead(perm))
        flux = link * (mobility + ahead(mobility)) * (pressure - ahead(pressure))
        residual = residual + (flux - behind(flux))
    partial[...] = residual


def outer_kernel(partial, near_side, near_other, far_side, far_other, residual):
    total = partial[...]
    for mine, other in ((near_side, near_other), (far_side, far_other)):
        link = joined(mine[2], other[2])
        total = total + link * (mine[1] + other[1]) * (mine[0] - other[0])
    residual[...] = total


def near(x):
    return pltpu.with_memory_space_constraint(x, pltpu.HBM)


def whole():
    return pl.BlockSpec(memory_space=pltpu.VMEM)


def params():
    return pltpu.CompilerParams(vmem_limit_bytes=40 * 1024 * 1024)


def body(
    features,
    block_scale,
    spec_weight,
    bypass_weight,
    mlp_in,
    mlp_out,
    decode_weight,
    zone_ids,
    face_open,
    perm_table,
):
    width, rows, cells = features.shape
    devices = lax.axis_size("gx")
    planes = rows * devices
    assert rows == 1 and cells == ROWS * LANES and width == TILES * SUB and devices % 2 == 0
    plane = features.reshape(width, cells)
    scale = block_scale.reshape(1, width)
    zone = zone_ids.reshape(ROWS, LANES)
    opened = face_open.reshape(3, ROWS, LANES)
    shares = devices // KY
    held = KZ // shares

    fixed = lambda i: (0, 0)
    cubes = lambda i: (0, 0, 0)
    steps = 4
    span = cells // steps
    part = span // LANES
    count = 2 * FOLD + 1
    lines = pl.pallas_call(
        forward_kernel,
        grid=(steps,),
        in_specs=[
            pl.BlockSpec((width, span), lambda i: (0, steps - 1 - i)),
            pl.BlockSpec((1, width), fixed),
            pl.BlockSpec((TWO * LANES, 2 * LANES), fixed),
            pl.BlockSpec((count * SUB, 2 * part * SUB), fixed),
            pl.BlockSpec((4, FOLD + 1, LANES), cubes),
        ],
        out_specs=pl.BlockSpec((KY * SUB, LANES), fixed),
        out_shape=jax.ShapeDtypeStruct((KY * SUB, LANES), F32),
        scratch_shapes=[pltpu.VMEM((2, (FOLD + 1) * SUB, 2 * LANES), F32)],
        compiler_params=params(),
        name="forward_yz",
    )(
        near(plane),
        near(scale),
        near(jnp.asarray(z_forward_table())),
        near(jnp.asarray(y_forward_table(part))),
        near(jnp.asarray(turn_forward_table(part))),
    )

    blocks = lines.reshape(KY, SUB, 2, shares, held * 2 * TILES)
    blocks = blocks.transpose(0, 3, 1, 2, 4).reshape(devices, SUB, 2 * held * 2 * TILES)
    blocks = lax.all_to_all(blocks, "gx", 0, 0, tiled=True)
    lines = blocks.reshape(planes * SUB, 2 * held * 2 * TILES)

    modes = spec_weight.shape[3]
    back = pl.pallas_call(
        mix_kernel,
        in_specs=[whole()] * 4,
        out_specs=whole(),
        out_shape=jax.ShapeDtypeStruct((planes * SUB, 2 * held * 2 * TILES), F32),
        scratch_shapes=[
            pltpu.VMEM((SUB, 2 * TILES, modes), F32),
            pltpu.VMEM((2, modes // LANES, 2 * width, LANES), F32),
        ],
        compiler_params=params(),
        name="mix_modes",
    )(
        lines,
        spec_weight,
        jnp.asarray(x_forward_table(planes)),
        jnp.asarray(x_back_table(planes)),
    )

    blocks = back.reshape(devices, SUB, 2 * held * 2 * TILES)
    blocks = lax.all_to_all(blocks, "gx", 0, 0, tiled=True)
    blocks = blocks.reshape(KY, shares, SUB, 2, held * 2 * TILES).transpose(0, 2, 3, 1, 4)
    lines = blocks.reshape(KY * SUB, 2 * HALF)

    side = jax.ShapeDtypeStruct((3, ROWS, LANES), F32)
    fields, near_side, far_side = pl.pallas_call(
        point_kernel,
        grid=(steps,),
        in_specs=[
            pl.BlockSpec((KY * SUB, LANES), fixed),
            pl.BlockSpec((width, span), lambda i: (0, i)),
            pl.BlockSpec((1, width), fixed),
            pl.BlockSpec(bypass_weight.shape, fixed),
            pl.BlockSpec(mlp_in.shape[::-1], fixed),
            pl.BlockSpec(mlp_out.shape, fixed),
            pl.BlockSpec(decode_weight.shape, fixed),
            pl.BlockSpec((part, LANES), lambda i: (i, 0)),
            pl.BlockSpec((1, part, LANES), lambda i: (0, i, 0)),
            pl.BlockSpec(memory_space=pltpu.SMEM),
            pl.BlockSpec((part * SUB, 4 * FOLD * SUB), fixed),
            pl.BlockSpec((2 * LANES, TILES * LANES), fixed),
            pl.BlockSpec((2, KY + FOLD, LANES), cubes),
        ],
        out_specs=[
            pl.BlockSpec((2, part, LANES), lambda i: (0, i, 0)),
            pl.BlockSpec((3, part, LANES), lambda i: (0, i, 0)),
            pl.BlockSpec((3, part, LANES), lambda i: (0, i, 0)),
        ],
        out_shape=[jax.ShapeDtypeStruct((2, ROWS, LANES), F32), side, side],
        scratch_shapes=[
            pltpu.VMEM((2, (FOLD + 1) * SUB, LANES), F32),
            pltpu.VMEM((part * SUB, TILES * LANES), F32),
        ],
        compiler_params=params(),
        name="point_network",
    )(
        lines,
        plane,
        scale,
        bypass_weight,
        mlp_in.T,
        mlp_out,
        decode_weight,
        zone,
        opened,
        perm_table,
        jnp.asarray(y_back_table(part)),
        jnp.asarray(z_back_table(planes * NY * NZ)),
        jnp.asarray(turn_back_table(part)),
    )
    pairs = [(i, i + 1) for i in range(1, devices - 1, 2)]
    far_other = lax.ppermute(far_side, "gx", pairs + [(b, a) for a, b in pairs])
    pairs = [(i, i + 1) for i in range(0, devices, 2)]
    near_other = lax.ppermute(near_side, "gx", pairs + [(b, a) for a, b in pairs])
    partial = pl.pallas_call(
        inner_kernel,
        in_specs=[whole()] * 3 + [pl.BlockSpec(memory_space=pltpu.SMEM)],
        out_specs=whole(),
        out_shape=jax.ShapeDtypeStruct((ROWS, LANES), F32),
        compiler_params=params(),
        name="faces_in_plane",
    )(near_side, zone, opened, perm_table)
    residual = pl.pallas_call(
        outer_kernel,
        in_specs=[whole()] * 5,
        out_specs=whole(),
        out_shape=jax.ShapeDtypeStruct((ROWS, LANES), F32),
        compiler_params=params(),
        name="faces_between_planes",
    )(partial, near_side, near_other, far_side, far_other)
    return (fields.reshape(2, 1, cells), residual.reshape(1, cells))


def solution(mesh):
    in_specs = (
        P(None, ("groups", "gx"), None),
        P(None, ("groups", "gx")),
        P(None, None, None, "gx"),
        P(),
        P(),
        P(),
        P(),
        P(("groups", "gx"), None),
        P(None, ("groups", "gx"), None),
        P(),
    )
    out_specs = (P(None, ("groups", "gx"), None), P(("groups", "gx"), None))
    return jax.shard_map(body, mesh=mesh, in_specs=in_specs, out_specs=out_specs, check_vma=False)
```

time: 75 us -> 59 us (0.79); the launches traced: 73.8 us -> 58.8 us
  starting transfers between devices: 16.9 us -> 2.3 us
  blocking collectives: 14.2 us -> 25.1 us
  local copies, waits for them, and re-layouts: 7.82 us -> 0.09 us
  Pallas kernels: 25 us -> 20.7 us
    all_to_all x1 -> x2, blocking collectives: 14.2 us -> 25.1 us  [body(): blocks = lax.all_to_all(blocks, 'gx', 0, 0, tiled=True)]
    unnamed x38 -> x30, local copies, waits for them, and re-layouts: 7.8 us -> 0.09 us
    ppermute x4 -> x2, starting transfers between devices: 9.79 us -> 2.3 us  [the longest x1 2.23 us: body(): far_other = lax.ppermute(far_side, 'gx', pairs + [(b, a) for a, b in pairs])]
    all_to_all x1 -> x0, starting transfers between devices: 7.1 us -> none  [body(): blocks = lax.all_to_all(blocks, 'gx', 0, 0, tiled=True)]
    pallas_call x1, Pallas kernels: 8.36 us -> 5.6 us  [body(): pl.pallas_call(forward_kernel, grid=(steps,), in_specs=[pl.BlockSpec((wid...]
    pallas_call x3, Pallas kernels: 15.9 us -> 14.4 us  [the longest x1 11.4 us: body(): pl.pallas_call(point_kernel, grid=(steps,), in_specs=[pl.BlockSpec((KY *...]
    ppermute x4 -> x2, waiting for transfers between devices: 9.1 us -> 9.68 us  [the longest x1 9.68 us: body(): far_other = lax.ppermute(far_side, 'gx', pairs + [(b, a) for a, b in pairs])]
  transfers between devices with their start and end apart: 5 -> 2, of which waited for: 4 -> 1; matrix products, arithmetic and copies ran while one was open for 0% -> 0% of each run, Pallas kernels for 1% -> 2%
where the time goes in v1:
time: 59 us; the launch traced here: 58.8 us
  blocking collectives  25.1 us (43%)
  Pallas kernels  20.7 us (35%)
  waiting for transfers between devices  9.68 us (16%)
  starting transfers between devices  2.3 us (4%)
  between operations  0.87 us (1%)
    all_to_all x2, blocking collectives, body(): blocks = lax.all_to_all(blocks, 'gx', 0, 0, tiled=True)  25.1 us
    pallas_call x1, Pallas kernels, body(): pl.pallas_call(point_kernel, grid=(steps,), in_specs=[pl.BlockSpec((KY *...  11.4 us
    ppermute x1, waiting for transfers between devices, body(): far_other = lax.ppermute(far_side, 'gx', pairs + [(b, a) for a, b in pairs])  9.68 us
    pallas_call x1, Pallas kernels, body(): pl.pallas_call(forward_kernel, grid=(steps,), in_specs=[pl.BlockSpec((wid...  5.6 us
    ppermute x1, starting transfers between devices, body(): far_other = lax.ppermute(far_side, 'gx', pairs + [(b, a) for a, b in pairs])  2.23 us
    pallas_call x1, Pallas kernels, body(): pl.pallas_call(mix_kernel, in_specs=[whole()] * 4, out_specs=whole(), out...  1.99 us
  transfers between devices with their start and end apart: 2, of which 1 were waited for; matrix products, arithmetic and copies ran while one was open for 0% of the time, Pallas kernels for 2%

profile of v1, /device:TPU:1, one launch (start us, length us, event | category | flops | bytes accessed | tf_op | source)
XLA Modules:
  0.0 58.8 jit_solution(8381547893551416491)
XLA Ops:
  0.6 0.0 copy-start.4
  0.6 0.0 copy-start.5
  0.7 0.0 copy-start.2
  0.7 0.0 copy-start.3
  0.7 0.0 copy-start.8
  0.7 0.0 copy-start.10
  0.7 0.0 copy-start.11
  0.7 5.6 %forward_yz.1 = f32[256,128]{1,0:T(8,128)S(1)} custom-call(bf16[32,32768]{1,0:T(8,128)(2,1)} %bitcast.11, f32[1,32]{1,0:T(1,128)} %bitcast.22, bf16[256,256]{1,0:T(8,128)(2,1)} %constant.16.clone.table_z, bf16[264,1024]{1,0:T(8,128)(2,1)} %constant.17.clone.table_y, f32[4,17,128]{2,1,0:T(8,128)} %constant.18.clone.turns), custom_call_target="tpu_custom_call" | custom-call | tf_op jit(solution)/shard_map/forward_yz/pallas_call | solution.py:503
  6.3 0.0 copy-start
  6.3 0.0 copy-start.1
  6.3 0.0 copy-start.6
  6.4 0.0 copy-start.7
  6.4 0.0 copy-start.9
  6.4 0.0 copy-start.12
  6.4 0.0 copy-start.13
  6.4 0.0 copy-start.14
  6.4 15.1 %all_to_all.10 = f32[32,8,128]{2,1,0:T(8,128)S(1)} all-to-all(f32[32,8,128]{2,1,0:T(8,128)S(1)} %bitcast.16), channel_id=1, replica_groups=mesh['groups'=1,'gx'=32] {'gx'}, dimensions={0} | all-to-all | bytes 262144 | tf_op jit(solution)/shard_map/all_to_all | solution.py:528
  21.5 0.0 copy-done.4
  21.5 0.0 copy-done.5
  21.5 0.0 copy-done.2
  21.5 2.0 %mix_modes.1 = f32[256,128]{1,0:T(8,128)S(1)} custom-call(f32[256,128]{1,0:T(8,128)S(1)} %bitcast.17, bf16[2,32,32,256]{3,2,1,0:T(8,128)(2,1)S(1)} %copy-done.2, f32[512,256]{1,0:T(8,128)S(1)} %copy-done.5, f32[256,512]{1,0:T(8,128)S(1)} %copy-done.4), custom_call_target="tpu_custom_call" | custom-call | tf_op jit(solution)/shard_map/mix_modes/pallas_call | solution.py:532
  23.5 10.0 %all_to_all.11 = f32[32,8,128]{2,1,0:T(8,128)S(1)} all-to-all(f32[32,8,128]{2,1,0:T(8,128)S(1)} %bitcast.18), channel_id=1, replica_groups=mesh['groups'=1,'gx'=32] {'gx'}, dimensions={0} | all-to-all | bytes 262144 | tf_op jit(solution)/shard_map/all_to_all | solution.py:551
  33.5 0.0 copy-done.3
  33.5 0.0 copy-done.8
  33.5 0.0 copy-done.10
  33.5 0.0 copy-done.11
  33.6 0.0 copy-done
  33.6 0.0 copy-done.1
  33.6 0.0 copy-done.6
  33.6 0.0 copy-done.7
  33.6 0.0 copy-done.9
  33.6 0.0 copy-done.12
  33.6 0.0 copy-done.13
  33.6 0.0 copy-done.14
  33.6 11.4 %point_network.1 = (f32[2,256,128]{2,1,0:T(8,128)}, f32[3,256,128]{2,1,0:T(8,128)S(1)}, f32[3,256,128]{2,1,0:T(8,128)S(1)}) custom-call(f32[256,128]{1,0:T(8,128)S(1)} %bitcast.15, bf16[32,32768]{1,0:T(8,128)(2,1)S(1)} %bitcast.12, f32[1,32]{1,0:T(1,128)S(1)} %bitcast.23, bf16[32,32]{1,0:T(8,128)(2,1)S(1)} %copy-done.9, bf16[32,128]{1,0:T(8,128)(2,1)S(1)} %bitcast.21, ...), custom_call_target="tpu_custom_call" | custom-call | tf_op jit(solution)/shard_map/point_network/pallas_call | solution.py:556
  45.0 2.2 %collective-permute-start.1 = (f32[3,256,128]{2,1,0:T(8,128)S(1)}, f32[3,256,128]{2,1,0:T(8,128)S(1)}, u32[]{:S(2)}, u32[]{:S(2)}) collective-permute-start(f32[3,256,128]{2,1,0:T(8,128)S(1)} %get-tuple-element.7.far_side), channel_id=1, source_target_pairs={{1,2},{3,4},{5,6},{7,8},{9,10},{11,12},{13,14},{15,16},{17,18},{19... | collective-permute-start | bytes 1179656 | tf_op jit(solution)/shard_map/ppermute | solution.py:602
  47.2 0.1 collective-permute-start
  47.3 1.0 %faces_in_plane.1.partial = f32[256,128]{1,0:T(8,128)S(1)} custom-call(f32[3,256,128]{2,1,0:T(8,128)S(1)} %get-tuple-element.6.side.near_side, s32[256,128]{1,0:T(8,128)S(1)} %bitcast.20, s32[3,256,128]{2,1,0:T(8,128)S(1)} %bitcast.14, f32[8]{0:T(128)S(1)} %copy-done.13), custom_call_target="tpu_custom_call" | custom-call | tf_op jit(solution)/shard_map/faces_in_plane/pallas_call | solution.py:605
  48.3 9.7 %collective-permute-done.1.far_other = f32[3,256,128]{2,1,0:T(8,128)S(1)} collective-permute-done((f32[3,256,128]{2,1,0:T(8,128)S(1)}, f32[3,256,128]{2,1,0:T(8,128)S(1)}, u32[]{:S(2)}, u32[]{:S(2)}) %collective-permute-start.1) | collective-permute-done | bytes 393248 | tf_op jit(solution)/shard_map/ppermute | solution.py:602
  58.0 0.0 collective-permute-done.near_other
  58.0 0.8 %faces_between_planes.1 = f32[256,128]{1,0:T(8,128)} custom-call(f32[256,128]{1,0:T(8,128)S(1)} %faces_in_plane.1.partial, f32[3,256,128]{2,1,0:T(8,128)S(1)} %get-tuple-element.6.side.near_side, f32[3,256,128]{2,1,0:T(8,128)S(1)} %collective-permute-done.near_other, f32[3,256,128]{2,1,0:T(8,128)S(1)} %get-tuple-element.7.far_side, ...), custom_call_target="tpu_custom_call" | custom-call | tf_op jit(solution)/shard_map/faces_between_planes/pallas_call | solution.py:613
Async XLA Ops:
  0.6 20.9 %copy-start.4 = (f32[256,512]{1,0:T(8,128)S(1)}, f32[256,512]{1,0:T(8,128)}, u32[]{:S(2)}) copy-start(f32[256,512]{1,0:T(8,128)} %constant.20.clone.table_back) | copy-start | bytes 1572868
  0.6 20.9 %copy-start.5 = (f32[512,256]{1,0:T(8,128)S(1)}, f32[512,256]{1,0:T(8,128)}, u32[]{:S(2)}) copy-start(f32[512,256]{1,0:T(8,128)} %constant.19.clone.table_x) | copy-start | bytes 1572868
  0.7 20.9 %copy-start.2 = (bf16[2,32,32,256]{3,2,1,0:T(8,128)(2,1)S(1)}, bf16[2,32,32,256]{3,2,1,0:T(8,128)(2,1)}, u32[]{:S(2)}) copy-start(bf16[2,32,32,256]{3,2,1,0:T(8,128)(2,1)} %weight.1) | copy-start | bytes 3145732
  0.7 32.9 %copy-start.3 = (bf16[512,512]{1,0:T(8,128)(2,1)S(1)}, bf16[512,512]{1,0:T(8,128)(2,1)}, u32[]{:S(2)}) copy-start(bf16[512,512]{1,0:T(8,128)(2,1)} %constant.21.clone.table_y) | copy-start | bytes 1572868
  0.7 32.9 %copy-start.8 = (f32[2,48,128]{2,1,0:T(8,128)S(1)}, f32[2,48,128]{2,1,0:T(8,128)}, u32[]{:S(2)}) copy-start(f32[2,48,128]{2,1,0:T(8,128)} %constant.23.clone.turns) | copy-start | bytes 147460
  0.7 32.8 %copy-start.10 = (bf16[128,32]{0,1:T(8,128)(2,1)S(1)}, bf16[128,32]{0,1:T(8,128)(2,1)}, u32[]{:S(2)}) copy-start(bf16[128,32]{0,1:T(8,128)(2,1)} %param.22) | copy-start | bytes 24580
  0.7 32.8 %copy-start.11 = (bf16[32,128]{1,0:T(8,128)(2,1)S(1)}, bf16[32,128]{1,0:T(8,128)(2,1)}, u32[]{:S(2)}) copy-start(bf16[32,128]{1,0:T(8,128)(2,1)} %mlp_out.1) | copy-start | bytes 24580
  6.3 27.2 %copy-start = (bf16[32,1,32768]{2,0,1:T(8,128)(2,1)S(1)}, bf16[32,1,32768]{2,0,1:T(8,128)(2,1)}, u32[]{:S(2)}) copy-start(bf16[32,1,32768]{2,0,1:T(8,128)(2,1)} %param.18) | copy-start | bytes 6291460
  6.3 27.2 %copy-start.1 = (s32[3,1,32768]{2,1,0:T(1,128)S(1)}, s32[3,1,32768]{2,1,0:T(1,128)}, u32[]{:S(2)}) copy-start(s32[3,1,32768]{2,1,0:T(1,128)} %param.26) | copy-start | bytes 1179652
  6.3 27.2 %copy-start.6 = (s32[1,32768]{1,0:T(1,128)S(1)}, s32[1,32768]{1,0:T(1,128)}, u32[]{:S(2)}) copy-start(s32[1,32768]{1,0:T(1,128)} %param.25) | copy-start | bytes 393220
  6.4 27.2 %copy-start.7 = (bf16[256,512]{1,0:T(8,128)(2,1)S(1)}, bf16[256,512]{1,0:T(8,128)(2,1)}, u32[]{:S(2)}) copy-start(bf16[256,512]{1,0:T(8,128)(2,1)} %constant.22.clone.table_z) | copy-start | bytes 786436
  6.4 27.2 %copy-start.9 = (bf16[32,32]{1,0:T(8,128)(2,1)S(1)}, bf16[32,32]{1,0:T(8,128)(2,1)}, u32[]{:S(2)}) copy-start(bf16[32,32]{1,0:T(8,128)(2,1)} %bypass.1) | copy-start | bytes 6148
  6.4 27.2 %copy-start.12 = (f32[32,1]{0,1:T(1,128)S(1)}, f32[32,1]{0,1:T(1,128)}, u32[]{:S(2)}) copy-start(f32[32,1]{0,1:T(1,128)} %param.19) | copy-start | bytes 388
  6.4 27.2 %copy-start.13 = (f32[8]{0:T(128)S(1)}, f32[8]{0:T(128)}, u32[]{:S(2)}) copy-start(f32[8]{0:T(128)} %perm_table.3) | copy-start | bytes 100
  6.4 27.2 %copy-start.14 = (bf16[2,32]{1,0:T(2,128)(2,1)S(1)}, bf16[2,32]{1,0:T(2,128)(2,1)}, u32[]{:S(2)}) copy-start(bf16[2,32]{1,0:T(2,128)(2,1)} %decode.1) | copy-start | bytes 388
  45.0 13.0 %collective-permute-start.1 = (f32[3,256,128]{2,1,0:T(8,128)S(1)}, f32[3,256,128]{2,1,0:T(8,128)S(1)}, u32[]{:S(2)}, u32[]{:S(2)}) collective-permute-start(f32[3,256,128]{2,1,0:T(8,128)S(1)} %get-tuple-element.7.far_side), channel_id=1, source_target_pairs={{1,2},{3,4},{5,6},{7,8},{9,10},{11,12},{13,14},{15,16},{17,18},{19... | collective-permute-start | bytes 1179656 | tf_op jit(solution)/shard_map/ppermute | solution.py:602
  47.2 10.8 %collective-permute-start = (f32[3,256,128]{2,1,0:T(8,128)S(1)}, f32[3,256,128]{2,1,0:T(8,128)S(1)}, u32[]{:S(2)}, u32[]{:S(2)}) collective-permute-start(f32[3,256,128]{2,1,0:T(8,128)S(1)} %get-tuple-element.6.side.near_side), channel_id=1, source_target_pairs={{0,1},{2,3},{4,5},{6,7},{8,9},{10,11},{12,13},{14,15},{16,17},{18,... | collective-permute-start | bytes 1179656 | tf_op jit(solution)/shard_map/ppermute | solution.py:604

commit v2 on v1

--- a/solution.py
+++ b/solution.py
@@ -1,3 +1,4 @@
+import functools
 import math
 
 import jax
@@ -22,6 +23,7 @@
 TILES = 4
 TWO = 2
 HALF = KZ * 2 * TILES
+QUARTER = ROWS // 4
 FOLD = KY // 2
 GELU_A = math.sqrt(2.0 / math.pi)
 GELU_B = GELU_A * 0.044715
@@ -60,24 +62,20 @@
     return halves(table.reshape(TWO * LANES, LANES), 1)
 
 
-def y_forward_table(rows):
-    angle = angles(np.arange(FOLD + 1), np.arange(rows) * PAIRS, NY)
+def y_forward_table():
+    angle = angles(np.arange(FOLD + 1), np.arange(QUARTER) * PAIRS, NY)
     return halves(np.concatenate([spread(np.cos(angle)), spread(np.sin(angle[1:]))], axis=0), 1)
 
 
-def turn_forward_table(rows):
-    freqs = np.arange(FOLD + 1)
-    parity = angles(freqs, np.arange(PAIRS), NY)
+def turn_forward_table():
+    parity = angles(np.arange(FOLD + 1), np.arange(PAIRS), NY)
     parity = np.tile(np.repeat(parity, 2 * TWO, axis=1), (1, 2 * KZ))
-    step = np.repeat(angles(freqs, np.array([rows * PAIRS]), NY), LANES, axis=1)
-    return np.stack([np.cos(parity), np.sin(parity), np.cos(step), np.sin(step)]).astype(np.float32)
-
-
-def turn_back_table(rows):
+    return np.stack([np.cos(parity), np.sin(parity)]).astype(np.float32)
+
+
+def turn_back_table():
     parity = np.repeat(angles(signed(KY), np.array([1]), NY), LANES, axis=1)
-    step = np.repeat(angles(np.arange(1, FOLD + 1), np.array([rows * PAIRS]), NY), LANES, axis=1)
-    both = np.concatenate([parity, step], axis=0)
-    return np.stack([np.cos(both), np.sin(both)]).astype(np.float32)
+    return np.stack([np.cos(parity), np.sin(parity)]).astype(np.float32)
 
 
 def x_forward_table(planes):
@@ -97,8 +95,8 @@
     return np.concatenate([table[0], table[1]], axis=1)
 
 
-def y_back_table(rows):
-    angle = angles(np.arange(1, FOLD + 1), np.arange(rows) * PAIRS, NY)
+def y_back_table():
+    angle = angles(np.arange(1, FOLD + 1), np.arange(QUARTER) * PAIRS, NY)
     return halves(np.concatenate([spread(np.cos(angle).T), spread(np.sin(angle).T)], axis=1), 1)
 
 
@@ -137,6 +135,10 @@
 
 def twice(x):
     return jnp.concatenate([x, x], axis=1)
+
+
+def quarters(real, imag, turns):
+    return ((real, imag), (-imag, real), (-real, -imag), (imag, -real))[turns % 4]
 
 
 def forward_kernel(features, scale, table_z, table_y, turns, lines, total):
@@ -170,12 +172,11 @@
         jnp.concatenate([low, high, high], axis=0),
     )
     n = (FOLD + 1) * SUB
-    cosine = twice(tall(turns[2], 0, FOLD + 1))
-    sine = twice(tall(turns[3], 0, FOLD + 1))
-    first, second = total[0], total[1]
-    total[0] = sums[:n] + cosine * first - sine * second
-    total[1] = sine * first + cosine * second
-    total[1, SUB:] += sums[n:]
+    for k in range(FOLD + 1):
+        at = slice(SUB * k, SUB * (k + 1))
+        real, imag = quarters(total[0, at], total[1, at], k)
+        total[0, at] = real + sums[at]
+        total[1, at] = imag + sums[n + SUB * (k - 1) : n + SUB * k] if k else imag
 
     @pl.when(step == pl.num_programs(0) - 1)
     def _():
@@ -282,6 +283,14 @@
     return x + x * jnp.tanh(x * (GELU_A + GELU_B * (x * x)))
 
 
+def diagonal(block):
+    height, width = block.shape
+    tall_block = jnp.concatenate([block] * SUB, axis=0)
+    rows = lax.broadcasted_iota(jnp.int32, (SUB * height, SUB * width), 0) // height
+    columns = lax.broadcasted_iota(jnp.int32, (SUB * height, SUB * width), 1) // width
+    return jnp.where(rows == columns, jnp.concatenate([tall_block] * SUB, axis=1), 0.0)
+
+
 def point_kernel(
     lines,
     features,
@@ -296,89 +305,71 @@
     table_y,
     table_z,
     turns,
-    fields,
-    near_side,
-    far_side,
-    sides,
-    smooth,
+    *refs,
+    first,
 ):
-    n = FOLD * SUB
-
-    @pl.when(pl.program_id(0) == 0)
-    def _():
-        held = lines[...]
-        other = pltpu.roll(held, HALF, 1)
-        low = lax.broadcasted_iota(jnp.int32, held.shape, 1) < HALF
-        cosine, sine = tall(turns[0], 0, KY), tall(turns[1], 0, KY)
-        straight = jnp.where(low, held, cosine * other + sine * held)
-        turned = jnp.where(low, other, cosine * held - sine * other)
-
-        def at(x, k):
-            return x[SUB * k : SUB * (k + 1)]
-
-        for k in range(1, FOLD):
-            here = slice(SUB * (k - 1), SUB * k)
-            sides[0, here] = at(straight, k) + at(straight, KY - k)
-            sides[1, here] = at(turned, k) - at(turned, KY - k)
-        sides[0, n - SUB : n] = at(straight, FOLD)
-        sides[1, n - SUB : n] = -at(turned, FOLD)
-        sides[0, n:] = at(straight, 0)
-
+    fields, near_side, far_side, smooth = refs[-4:]
     rows = features.shape[1] // LANES
-    width = features.shape[0]
-    even, odd = sides[0, :n], sides[1, :n]
-    high, low = split(jnp.concatenate([even, odd], axis=0))
-    both = jnp.concatenate([high, low], axis=1)
-    both = dot(table_y[...], jnp.concatenate([both, both], axis=0))
-    level = jnp.concatenate([sides[0, n:]] * rows, axis=0)
-    high, low = split(both[:, :LANES] + both[:, LANES:] + level)
-    table = table_z[...]
-    smooth[...] = dot(
-        jnp.concatenate([low, high, high], axis=1),
-        jnp.concatenate([table[:LANES], table], axis=0),
+    held = lines[...]
+    other = pltpu.roll(held, HALF, 1)
+    low_half = lax.broadcasted_iota(jnp.int32, held.shape, 1) < HALF
+    cosine, sine = tall(turns[0], 0, KY), tall(turns[1], 0, KY)
+    straight = jnp.where(low_half, held, cosine * other + sine * held)
+    turned = jnp.where(low_half, other, cosine * held - sine * other)
+
+    def at(x, k):
+        return x[SUB * k : SUB * (k + 1)]
+
+    even = [at(straight, k) + at(straight, KY - k) for k in range(1, FOLD)]
+    odd = [at(turned, k) - at(turned, KY - k) for k in range(1, FOLD)]
+    even.append(at(straight, FOLD))
+    odd.append(-at(turned, FOLD))
+    level = jnp.concatenate([at(straight, 0)] * QUARTER, axis=0)
+    table = jnp.concatenate([table_z[:LANES], table_z[...]], axis=0)
+    for m in range(rows // QUARTER):
+        sides = [
+            quarters(real, -imag, (first // QUARTER + m) * k)
+            for k, (real, imag) in enumerate(zip(even, odd), 1)
+        ]
+        sides = [real for real, _ in sides] + [-imag for _, imag in sides]
+        sides = jnp.concatenate(split(jnp.concatenate(sides, axis=0)), axis=1)
+        both = dot(table_y[...], jnp.concatenate([sides, sides], axis=0))
+        high, low = split(both[:, :LANES] + both[:, LANES:] + level)
+        smooth[QUARTER * SUB * m : QUARTER * SUB * (m + 1)] = dot(
+            jnp.concatenate([low, high, high], axis=1), table
+        )
+
+    wide_bypass = diagonal(bypass[...].astype(F32)).astype(BF16)
+    wide_in = diagonal(0.5 * mlp_in_t[...].astype(F32).T).astype(BF16)
+    heads = 0.5 * dot(decode[...], mlp_out[...])
+    heads = jnp.concatenate([diagonal(heads[k : k + 1]) for k in range(2)], axis=0)
+    wide_out = jnp.concatenate(split(heads), axis=0)
+
+    groups = rows // SUB
+
+    def grouped(tile):
+        return jnp.concatenate(
+            [
+                jnp.concatenate([tile(SUB * a + g) for a in range(groups)], axis=1)
+                for g in range(SUB)
+            ],
+            axis=0,
+        )
+
+    values = features[...].astype(F32) * column(scale[...])
+    values = grouped(lambda j: values[:, LANES * j : LANES * (j + 1)]).astype(BF16)
+    spectral = grouped(
+        lambda j: jnp.concatenate(
+            [
+                smooth[SUB * j : SUB * (j + 1), LANES * t : LANES * (t + 1)]
+                for t in range(TILES)
+            ],
+            axis=0,
+        )
     )
-    cosine, sine = tall(turns[0], KY, FOLD), tall(turns[1], KY, FOLD)
-    sides[0, :n] = cosine * even + sine * odd
-    sides[1, :n] = cosine * odd - sine * even
-
-    values = (features[...].astype(F32) * column(scale[...])).astype(BF16)
-    spectral = jnp.concatenate(
-        [
-            jnp.concatenate(
-                [
-                    smooth[SUB * j : SUB * (j + 1), LANES * t : LANES * (t + 1)]
-                    for t in range(TILES)
-                ],
-                axis=0,
-            )
-            for j in range(rows)
-        ],
-        axis=1,
-    )
-    lifted = gelu_twice(spectral + dot(bypass[...], values)).astype(BF16)
-    inner = (0.5 * mlp_in_t[...].astype(F32)).astype(BF16)
-    hidden = gelu_twice(dot(inner, lifted, ((0,), (0,)))).astype(BF16)
-
-    heads = dot(decode[...], mlp_out[...])
-    count = heads.shape[1]
-    group = lax.broadcasted_iota(jnp.int32, (SUB, SUB * count), 1) // count
-    own = group == lax.broadcasted_iota(jnp.int32, (SUB, SUB * count), 0)
-    wide = jnp.concatenate([heads] * SUB, axis=1)
-    wide = jnp.concatenate([jnp.where(own, wide[k : k + 1], 0.0) for k in range(2)], axis=0)
-    stacked = jnp.concatenate(
-        [
-            jnp.concatenate(
-                [
-                    hidden[:, (SUB * a + g) * LANES : (SUB * a + g + 1) * LANES]
-                    for a in range(rows // SUB)
-                ],
-                axis=1,
-            )
-            for g in range(SUB)
-        ],
-        axis=0,
-    )
-    decoded = dot(jnp.concatenate(split(0.5 * wide), axis=0), stacked)
+    lifted = gelu_twice(spectral + dot(wide_bypass, values)).astype(BF16)
+    hidden = gelu_twice(dot(wide_in, lifted)).astype(BF16)
+    decoded = dot(wide_out, hidden)
     decoded = decoded[: 2 * SUB] + decoded[2 * SUB :]
     even_plane = lax.axis_index("gx") % 2 == 0
     for a in range(rows // SUB):
@@ -440,8 +431,8 @@
     return jnp.where(lane % NZ == 0, 0.0, pltpu.roll(field, 1, 1))
 
 
-def inner_kernel(side, zone, opened, perm_table, partial):
-    pressure, mobility = side[0], side[1]
+def inner_kernel(first, last, zone, opened, perm_table, partial):
+    pressure, mobility = [jnp.concatenate([first[k], last[k]], axis=0) for k in range(2)]
     perm = lookup(zone[...], perm_table)
     residual = jnp.zeros(pressure.shape, F32)
     for axis, ahead, behind in ((1, ahead_y, behind_y), (2, ahead_z, behind_z)):
@@ -451,12 +442,16 @@
     partial[...] = residual
 
 
-def outer_kernel(partial, near_side, near_other, far_side, far_other, residual):
-    total = partial[...]
-    for mine, other in ((near_side, near_other), (far_side, far_other)):
+def outer_kernel(partial, *refs):
+    residual = refs[-1]
+
+    def flow(mine, other):
         link = joined(mine[2], other[2])
-        total = total + link * (mine[1] + other[1]) * (mine[0] - other[0])
-    residual[...] = total
+        return link * (mine[1] + other[1]) * (mine[0] - other[0])
+
+    cut = refs[0].shape[1]
+    for at, sides in ((slice(0, cut), refs[:4]), (slice(cut, ROWS), refs[4:8])):
+        residual[at] = partial[at] + flow(sides[0], sides[3]) + flow(sides[1], sides[2])
 
 
 def near(x):
@@ -496,9 +491,9 @@
 
     fixed = lambda i: (0, 0)
     cubes = lambda i: (0, 0, 0)
-    steps = 4
-    span = cells // steps
-    part = span // LANES
+    steps = ROWS // QUARTER
+    part = QUARTER
+    span = part * LANES
     count = 2 * FOLD + 1
     lines = pl.pallas_call(
         forward_kernel,
@@ -508,7 +503,7 @@
             pl.BlockSpec((1, width), fixed),
             pl.BlockSpec((TWO * LANES, 2 * LANES), fixed),
             pl.BlockSpec((count * SUB, 2 * part * SUB), fixed),
-            pl.BlockSpec((4, FOLD + 1, LANES), cubes),
+            pl.BlockSpec((2, FOLD + 1, LANES), cubes),
         ],
         out_specs=pl.BlockSpec((KY * SUB, LANES), fixed),
         out_shape=jax.ShapeDtypeStruct((KY * SUB, LANES), F32),
@@ -519,8 +514,8 @@
         near(plane),
         near(scale),
         near(jnp.asarray(z_forward_table())),
-        near(jnp.asarray(y_forward_table(part))),
-        near(jnp.asarray(turn_forward_table(part))),
+        near(jnp.asarray(y_forward_table())),
+        near(jnp.asarray(turn_forward_table())),
     )
 
     blocks = lines.reshape(KY, SUB, 2, shares, held * 2 * TILES)
@@ -552,72 +547,86 @@
     blocks = blocks.reshape(KY, shares, SUB, 2, held * 2 * TILES).transpose(0, 2, 3, 1, 4)
     lines = blocks.reshape(KY * SUB, 2 * HALF)
 
-    side = jax.ShapeDtypeStruct((3, ROWS, LANES), F32)
-    fields, near_side, far_side = pl.pallas_call(
-        point_kernel,
-        grid=(steps,),
-        in_specs=[
-            pl.BlockSpec((KY * SUB, LANES), fixed),
-            pl.BlockSpec((width, span), lambda i: (0, i)),
-            pl.BlockSpec((1, width), fixed),
-            pl.BlockSpec(bypass_weight.shape, fixed),
-            pl.BlockSpec(mlp_in.shape[::-1], fixed),
-            pl.BlockSpec(mlp_out.shape, fixed),
-            pl.BlockSpec(decode_weight.shape, fixed),
-            pl.BlockSpec((part, LANES), lambda i: (i, 0)),
-            pl.BlockSpec((1, part, LANES), lambda i: (0, i, 0)),
-            pl.BlockSpec(memory_space=pltpu.SMEM),
-            pl.BlockSpec((part * SUB, 4 * FOLD * SUB), fixed),
-            pl.BlockSpec((2 * LANES, TILES * LANES), fixed),
-            pl.BlockSpec((2, KY + FOLD, LANES), cubes),
-        ],
-        out_specs=[
-            pl.BlockSpec((2, part, LANES), lambda i: (0, i, 0)),
-            pl.BlockSpec((3, part, LANES), lambda i: (0, i, 0)),
-            pl.BlockSpec((3, part, LANES), lambda i: (0, i, 0)),
-        ],
-        out_shape=[jax.ShapeDtypeStruct((2, ROWS, LANES), F32), side, side],
-        scratch_shapes=[
-            pltpu.VMEM((2, (FOLD + 1) * SUB, LANES), F32),
-            pltpu.VMEM((part * SUB, TILES * LANES), F32),
-        ],
-        compiler_params=params(),
-        name="point_network",
-    )(
-        lines,
-        plane,
-        scale,
-        bypass_weight,
-        mlp_in.T,
-        mlp_out,
-        decode_weight,
-        zone,
-        opened,
-        perm_table,
-        jnp.asarray(y_back_table(part)),
-        jnp.asarray(z_back_table(planes * NY * NZ)),
-        jnp.asarray(turn_back_table(part)),
-    )
-    pairs = [(i, i + 1) for i in range(1, devices - 1, 2)]
-    far_other = lax.ppermute(far_side, "gx", pairs + [(b, a) for a, b in pairs])
-    pairs = [(i, i + 1) for i in range(0, devices, 2)]
-    near_other = lax.ppermute(near_side, "gx", pairs + [(b, a) for a, b in pairs])
+    def network(first, count, carried):
+        at = first // count
+        side = jax.ShapeDtypeStruct((3, count, LANES), F32)
+        return pl.pallas_call(
+            functools.partial(point_kernel, first=first),
+            grid=(1,),
+            in_specs=[
+                pl.BlockSpec((KY * SUB, LANES), fixed),
+                pl.BlockSpec((width, count * LANES), lambda i: (0, at)),
+                pl.BlockSpec((1, width), fixed),
+                pl.BlockSpec(bypass_weight.shape, fixed),
+                pl.BlockSpec(mlp_in.shape[::-1], fixed),
+                pl.BlockSpec(mlp_out.shape, fixed),
+                pl.BlockSpec(decode_weight.shape, fixed),
+                pl.BlockSpec((count, LANES), lambda i: (at, 0)),
+                pl.BlockSpec((1, count, LANES), lambda i: (0, at, 0)),
+                pl.BlockSpec(memory_space=pltpu.SMEM),
+                pl.BlockSpec((QUARTER * SUB, 4 * FOLD * SUB), fixed),
+                pl.BlockSpec((2 * LANES, TILES * LANES), fixed),
+                pl.BlockSpec((2, KY, LANES), cubes),
+            ]
+            + [pl.BlockSpec(memory_space=pl.ANY)] * len(carried),
+            out_specs=[
+                pl.BlockSpec((2, count, LANES), lambda i: (0, at, 0)),
+                pl.BlockSpec((3, count, LANES), cubes),
+                pl.BlockSpec((3, count, LANES), cubes),
+            ],
+            out_shape=[
+                jax.ShapeDtypeStruct((2, ROWS, LANES), F32),
+                side,
+                side,
+            ],
+            scratch_shapes=[pltpu.VMEM((count * SUB, TILES * LANES), F32)],
+            input_output_aliases={13 + k: k for k in range(len(carried))},
+            compiler_params=params(),
+            cost_estimate=pl.CostEstimate(
+                flops=count * LANES * 400000, bytes_accessed=count * LANES * 200, transcendentals=0
+            ),
+            name="point_network",
+        )(
+            lines,
+            plane,
+            scale,
+            bypass_weight,
+            mlp_in.T,
+            mlp_out,
+            decode_weight,
+            zone,
+            opened,
+            perm_table,
+            jnp.asarray(y_back_table()),
+            jnp.asarray(z_back_table(planes * NY * NZ)),
+            jnp.asarray(turn_back_table()),
+            *carried,
+        )
+
+    far = [(i, i + 1) for i in range(1, devices - 1, 2)]
+    far = far + [(b, a) for a, b in far]
+    near_by = [(i, i + 1) for i in range(0, devices, 2)]
+    near_by = near_by + [(b, a) for a, b in near_by]
+    fields, *first = network(0, ROWS - QUARTER, ())
+    first_other = [lax.ppermute(first[1], "gx", far), lax.ppermute(first[0], "gx", near_by)]
+    fields, *last = network(ROWS - QUARTER, QUARTER, (fields,))
+    last_other = [lax.ppermute(last[1], "gx", far), lax.ppermute(last[0], "gx", near_by)]
     partial = pl.pallas_call(
         inner_kernel,
-        in_specs=[whole()] * 3 + [pl.BlockSpec(memory_space=pltpu.SMEM)],
+        in_specs=[whole()] * 4 + [pl.BlockSpec(memory_space=pltpu.SMEM)],
         out_specs=whole(),
         out_shape=jax.ShapeDtypeStruct((ROWS, LANES), F32),
         compiler_params=params(),
         name="faces_in_plane",
-    )(near_side, zone, opened, perm_table)
+    )(first[0], last[0], zone, opened, perm_table)
     residual = pl.pallas_call(
         outer_kernel,
-        in_specs=[whole()] * 5,
+        in_specs=[whole()] * 9,
         out_specs=whole(),
         out_shape=jax.ShapeDtypeStruct((ROWS, LANES), F32),
         compiler_params=params(),
         name="faces_between_planes",
-    )(partial, near_side, near_other, far_side, far_other)
+    )(partial, *first, *first_other, *last, *last_other)
     return (fields.reshape(2, 1, cells), residual.reshape(1, cells))
 
 

time: 59 us -> 55.6 us (0.942)
  waiting for transfers between devices: 9.68 us -> 1.97 us
  starting transfers between devices: 2.3 us -> 6.06 us
    ppermute x2 -> x4, waiting for transfers between devices: 9.68 us -> 1.97 us  [the longest x1 1.96 us: body(): lax.ppermute(last[1], 'gx', far)]
    ppermute x2 -> x4, starting transfers between devices: 2.3 us -> 6.06 us  [the longest x1 3.67 us: body(): lax.ppermute(last[1], 'gx', far)]
    pallas_call x3 -> x4, Pallas kernels: 13.1 us -> 13.4 us  [the longest x2 11.6 us: network(): pl.pallas_call(functools.partial(point_kernel, first=first), grid=(1,), i...]
  transfers between devices with their start and end apart: 2 -> 4, of which waited for: 1 -> 1; matrix products, arithmetic and copies ran while one was open for 0% -> 0% of each run, Pallas kernels for 2% -> 9%
where the time goes in v2:
time: 55.6 us; the launch traced here: 55.1 us
  blocking collectives  25.1 us (45%)
  Pallas kernels  21 us (38%)
  starting transfers between devices  6.06 us (11%)
  waiting for transfers between devices  1.97 us (4%)
  between operations  0.89 us (2%)
    all_to_all x2, blocking collectives, body(): blocks = lax.all_to_all(blocks, 'gx', 0, 0, tiled=True)  25.1 us
    pallas_call x2, Pallas kernels, network(): pl.pallas_call(functools.partial(point_kernel, first=first), grid=(1,), i...  11.6 us
    pallas_call x1, Pallas kernels, body(): pl.pallas_call(forward_kernel, grid=(steps,), in_specs=[pl.BlockSpec((wid...  5.62 us
    ppermute x1, starting transfers between devices, body(): lax.ppermute(last[1], 'gx', far)  3.67 us
    ppermute x1, starting transfers between devices, body(): lax.ppermute(first[1], 'gx', far)  2.25 us
    pallas_call x1, Pallas kernels, body(): pl.pallas_call(mix_kernel, in_specs=[whole()] * 4, out_specs=whole(), out...  1.99 us
    ppermute x1, waiting for transfers between devices, body(): lax.ppermute(last[1], 'gx', far)  1.96 us
  transfers between devices with their start and end apart: 4, of which 1 were waited for; matrix products, arithmetic and copies ran while one was open for 0% of the time, Pallas kernels for 9%

profile of v2, /device:TPU:1, one launch (start us, length us, event | category | flops | bytes accessed | tf_op | source)
XLA Modules:
  0.0 55.1 jit_solution(3829936947272248888)
XLA Ops:
  0.6 0.0 copy-start.2
  0.6 0.0 copy-start.3
  0.7 0.0 copy-start.1
  0.7 0.0 copy-start.12
  0.7 0.0 copy-start.13
  0.7 5.6 %forward_yz.1 = f32[256,128]{1,0:T(8,128)S(1)} custom-call(bf16[32,32768]{1,0:T(8,128)(2,1)} %bitcast.11, f32[1,32]{1,0:T(1,128)} %bitcast.25, bf16[256,256]{1,0:T(8,128)(2,1)} %constant.16.clone.table_z, bf16[264,1024]{1,0:T(8,128)(2,1)} %constant.17.clone.table_y, f32[2,17,128]{2,1,0:T(8,128)} %constant.18.clone.turns), custom_call_target="tpu_custom_call" | custom-call | tf_op jit(solution)/shard_map/forward_yz/pallas_call | solution.py:498
  6.3 0.0 copy-start
  6.3 0.0 copy-start.4
  6.3 0.0 copy-start.5
  6.4 0.0 copy-start.6
  6.4 0.0 copy-start.7
  6.4 0.0 copy-start.8
  6.4 0.0 copy-start.9
  6.4 0.0 copy-start.10
  6.4 0.0 copy-start.11
  6.4 0.0 copy-start.14
  6.4 15.1 %all_to_all.10 = f32[32,8,128]{2,1,0:T(8,128)S(1)} all-to-all(f32[32,8,128]{2,1,0:T(8,128)S(1)} %bitcast.14), channel_id=1, replica_groups=mesh['groups'=1,'gx'=32] {'gx'}, dimensions={0} | all-to-all | bytes 262144 | tf_op jit(solution)/shard_map/all_to_all | solution.py:523
  21.5 0.0 copy-done.2
  21.5 0.0 copy-done.3
  21.5 0.0 copy-done.1
  21.5 2.0 %mix_modes.1 = f32[256,128]{1,0:T(8,128)S(1)} custom-call(f32[256,128]{1,0:T(8,128)S(1)} %bitcast.15, bf16[2,32,32,256]{3,2,1,0:T(8,128)(2,1)S(1)} %copy-done.1, f32[512,256]{1,0:T(8,128)S(1)} %copy-done.3, f32[256,512]{1,0:T(8,128)S(1)} %copy-done.2), custom_call_target="tpu_custom_call" | custom-call | tf_op jit(solution)/shard_map/mix_modes/pallas_call | solution.py:527
  23.5 10.0 %all_to_all.11 = f32[32,8,128]{2,1,0:T(8,128)S(1)} all-to-all(f32[32,8,128]{2,1,0:T(8,128)S(1)} %bitcast.16), channel_id=1, replica_groups=mesh['groups'=1,'gx'=32] {'gx'}, dimensions={0} | all-to-all | bytes 262144 | tf_op jit(solution)/shard_map/all_to_all | solution.py:546
  33.5 0.0 copy-done.12
  33.5 0.0 copy-done.13
  33.6 0.0 copy-done
  33.6 0.0 copy-done.4
  33.6 0.0 copy-done.5
  33.6 0.0 copy-done.6
  33.6 0.0 copy-done.7
  33.6 0.0 copy-done.8
  33.6 0.0 copy-done.9
  33.6 0.0 copy-done.10
  33.6 0.0 copy-done.11
  33.6 0.0 copy-done.14
  33.6 7.9 %point_network.2 = (f32[2,256,128]{2,1,0:T(8,128)}, f32[3,192,128]{2,1,0:T(8,128)S(1)}, f32[3,192,128]{2,1,0:T(8,128)S(1)}) custom-call(f32[256,128]{1,0:T(8,128)S(1)} %bitcast.20, bf16[32,32768]{1,0:T(8,128)(2,1)S(1)} %bitcast.12, f32[1,32]{1,0:T(1,128)S(1)} %bitcast.26, bf16[32,32]{1,0:T(8,128)(2,1)S(1)} %copy-done.8, bf16[32,128]{1,0:T(8,128)(2,1)S(1)} %bitcast.28, ...), custom_call_target="tpu_custom_call" | custom-call | flops 9830400000 | bytes 4915200 | tf_op jit(solution)/shard_map/point_network/pallas_call | solution.py:553
  41.6 2.2 %collective-permute-start = (f32[3,192,128]{2,1,0:T(8,128)S(1)}, f32[3,192,128]{2,1,0:T(8,128)S(1)}, u32[]{:S(2)}, u32[]{:S(2)}) collective-permute-start(f32[3,192,128]{2,1,0:T(8,128)S(1)} %get-tuple-element.12.refs_1_), channel_id=1, source_target_pairs={{1,2},{3,4},{5,6},{7,8},{9,10},{11,12},{13,14},{15,16},{17,18},{19... | collective-permute-start | bytes 884744 | tf_op jit(solution)/shard_map/ppermute | solution.py:611
  43.8 0.1 collective-permute-start.1
  43.9 3.7 %point_network.3 = (f32[2,256,128]{2,1,0:T(8,128)}, f32[3,64,128]{2,1,0:T(8,128)S(1)}, f32[3,64,128]{2,1,0:T(8,128)S(1)}) custom-call(f32[256,128]{1,0:T(8,128)S(1)} %bitcast.21, bf16[32,32768]{1,0:T(8,128)(2,1)S(1)} %bitcast.13, f32[1,32]{1,0:T(1,128)S(1)} %bitcast.27, bf16[32,32]{1,0:T(8,128)(2,1)S(1)} %copy-done.8, ...), custom_call_target="tpu_custom_call", output_to_operand_aliasing={{0}: (13, {})} | custom-call | flops 3276800000 | bytes 1638400 | tf_op jit(solution)/shard_map/point_network/pallas_call | solution.py:553
  47.6 3.7 %collective-permute-start.2 = (f32[3,64,128]{2,1,0:T(8,128)S(1)}, f32[3,64,128]{2,1,0:T(8,128)S(1)}, u32[]{:S(2)}, u32[]{:S(2)}) collective-permute-start(f32[3,64,128]{2,1,0:T(8,128)S(1)} %get-tuple-element.13.refs_5_), channel_id=1, source_target_pairs={{1,2},{3,4},{5,6},{7,8},{9,10},{11,12},{13,14},{15,16},{17,18},{19... | collective-permute-start | bytes 294920 | tf_op jit(solution)/shard_map/ppermute | solution.py:613
  51.3 0.1 collective-permute-start.3
  51.4 1.0 %faces_in_plane.1.partial = f32[256,128]{1,0:T(8,128)S(1)} custom-call(f32[3,192,128]{2,1,0:T(8,128)S(1)} %get-tuple-element.10.first.refs_0_, f32[3,64,128]{2,1,0:T(8,128)S(1)} %get-tuple-element.11.last.refs_4_, s32[256,128]{1,0:T(8,128)S(1)} %bitcast.24, s32[3,256,128]{2,1,0:T(8,128)S(1)} %bitcast.19, f32[8]{0:T(128)S(1)} %copy-done.7), custom_call_target="tpu_custom_call" | custom-call | tf_op jit(solution)/shard_map/faces_in_plane/pallas_call | solution.py:614
  52.4 2.0 %collective-permute-done.2.refs_6_ = f32[3,64,128]{2,1,0:T(8,128)S(1)} collective-permute-done((f32[3,64,128]{2,1,0:T(8,128)S(1)}, f32[3,64,128]{2,1,0:T(8,128)S(1)}, u32[]{:S(2)}, u32[]{:S(2)}) %collective-permute-start.2) | collective-permute-done | bytes 98336 | tf_op jit(solution)/shard_map/ppermute | solution.py:613
  54.3 0.0 collective-permute-done.3.refs_7_
  54.3 0.0 collective-permute-done.refs_2_
  54.3 0.0 collective-permute-done.1.refs_3_
  54.4 0.8 %faces_between_planes.1 = f32[256,128]{1,0:T(8,128)} custom-call(f32[256,128]{1,0:T(8,128)S(1)} %faces_in_plane.1.partial, f32[3,192,128]{2,1,0:T(8,128)S(1)} %get-tuple-element.10.first.refs_0_, f32[3,192,128]{2,1,0:T(8,128)S(1)} %get-tuple-element.12.refs_1_, f32[3,192,128]{2,1,0:T(8,128)S(1)} %collective-permute-done.refs_2_, ...), custom_call_target="tpu_custom_call" | custom-call | tf_op jit(solution)/shard_map/faces_between_planes/pallas_call | solution.py:622
Async XLA Ops:
  0.6 20.9 %copy-start.2 = (f32[256,512]{1,0:T(8,128)S(1)}, f32[256,512]{1,0:T(8,128)}, u32[]{:S(2)}) copy-start(f32[256,512]{1,0:T(8,128)} %constant.20.clone.table_back) | copy-start | bytes 1572868
  0.6 20.9 %copy-start.3 = (f32[512,256]{1,0:T(8,128)S(1)}, f32[512,256]{1,0:T(8,128)}, u32[]{:S(2)}) copy-start(f32[512,256]{1,0:T(8,128)} %constant.19.clone.table_x) | copy-start | bytes 1572868
  0.7 20.9 %copy-start.1 = (bf16[2,32,32,256]{3,2,1,0:T(8,128)(2,1)S(1)}, bf16[2,32,32,256]{3,2,1,0:T(8,128)(2,1)}, u32[]{:S(2)}) copy-start(bf16[2,32,32,256]{3,2,1,0:T(8,128)(2,1)} %weight.1) | copy-start | bytes 3145732
  0.7 32.9 %copy-start.12 = (bf16[512,512]{1,0:T(8,128)(2,1)S(1)}, bf16[512,512]{1,0:T(8,128)(2,1)}, u32[]{:S(2)}) copy-start(bf16[512,512]{1,0:T(8,128)(2,1)} %constant.21.clone.table_y) | copy-start | bytes 1572868
  0.7 32.9 %copy-start.13 = (bf16[256,512]{1,0:T(8,128)(2,1)S(1)}, bf16[256,512]{1,0:T(8,128)(2,1)}, u32[]{:S(2)}) copy-start(bf16[256,512]{1,0:T(8,128)(2,1)} %constant.22.clone.table_z) | copy-start | bytes 786436
  6.3 27.2 %copy-start = (bf16[32,1,32768]{2,0,1:T(8,128)(2,1)S(1)}, bf16[32,1,32768]{2,0,1:T(8,128)(2,1)}, u32[]{:S(2)}) copy-start(bf16[32,1,32768]{2,0,1:T(8,128)(2,1)} %param.21) | copy-start | bytes 6291460
  6.3 27.2 %copy-start.4 = (s32[3,1,32768]{2,1,0:T(1,128)S(1)}, s32[3,1,32768]{2,1,0:T(1,128)}, u32[]{:S(2)}) copy-start(s32[3,1,32768]{2,1,0:T(1,128)} %param.29) | copy-start | bytes 1179652
  6.3 27.2 %copy-start.5 = (s32[1,32768]{1,0:T(1,128)S(1)}, s32[1,32768]{1,0:T(1,128)}, u32[]{:S(2)}) copy-start(s32[1,32768]{1,0:T(1,128)} %param.28) | copy-start | bytes 393220
  6.4 27.2 %copy-start.6 = (f32[32,1]{0,1:T(1,128)S(1)}, f32[32,1]{0,1:T(1,128)}, u32[]{:S(2)}) copy-start(f32[32,1]{0,1:T(1,128)} %param.22) | copy-start | bytes 388
  6.4 27.2 %copy-start.7 = (f32[8]{0:T(128)S(1)}, f32[8]{0:T(128)}, u32[]{:S(2)}) copy-start(f32[8]{0:T(128)} %perm_table.5) | copy-start | bytes 100
  6.4 27.2 %copy-start.8 = (bf16[32,32]{1,0:T(8,128)(2,1)S(1)}, bf16[32,32]{1,0:T(8,128)(2,1)}, u32[]{:S(2)}) copy-start(bf16[32,32]{1,0:T(8,128)(2,1)} %bypass.3) | copy-start | bytes 6148
  6.4 27.2 %copy-start.9 = (bf16[128,32]{0,1:T(8,128)(2,1)S(1)}, bf16[128,32]{0,1:T(8,128)(2,1)}, u32[]{:S(2)}) copy-start(bf16[128,32]{0,1:T(8,128)(2,1)} %param.25) | copy-start | bytes 24580
  6.4 27.2 %copy-start.10 = (bf16[32,128]{1,0:T(8,128)(2,1)S(1)}, bf16[32,128]{1,0:T(8,128)(2,1)}, u32[]{:S(2)}) copy-start(bf16[32,128]{1,0:T(8,128)(2,1)} %mlp_out.3) | copy-start | bytes 24580
  6.4 27.2 %copy-start.11 = (bf16[2,32]{1,0:T(2,128)(2,1)S(1)}, bf16[2,32]{1,0:T(2,128)(2,1)}, u32[]{:S(2)}) copy-start(bf16[2,32]{1,0:T(2,128)(2,1)} %decode.3) | copy-start | bytes 388
  6.4 27.2 %copy-start.14 = (f32[2,32,128]{2,1,0:T(8,128)S(1)}, f32[2,32,128]{2,1,0:T(8,128)}, u32[]{:S(2)}) copy-start(f32[2,32,128]{2,1,0:T(8,128)} %constant.23.clone.turns) | copy-start | bytes 98308
  41.6 12.8 %collective-permute-start = (f32[3,192,128]{2,1,0:T(8,128)S(1)}, f32[3,192,128]{2,1,0:T(8,128)S(1)}, u32[]{:S(2)}, u32[]{:S(2)}) collective-permute-start(f32[3,192,128]{2,1,0:T(8,128)S(1)} %get-tuple-element.12.refs_1_), channel_id=1, source_target_pairs={{1,2},{3,4},{5,6},{7,8},{9,10},{11,12},{13,14},{15,16},{17,18},{19... | collective-permute-start | bytes 884744 | tf_op jit(solution)/shard_map/ppermute | solution.py:611
  43.8 10.5 %collective-permute-start.1 = (f32[3,192,128]{2,1,0:T(8,128)S(1)}, f32[3,192,128]{2,1,0:T(8,128)S(1)}, u32[]{:S(2)}, u32[]{:S(2)}) collective-permute-start(f32[3,192,128]{2,1,0:T(8,128)S(1)} %get-tuple-element.10.first.refs_0_), channel_id=1, source_target_pairs={{0,1},{2,3},{4,5},{6,7},{8,9},{10,11},{12,13},{14,15},{16,17},{18,... | collective-permute-start | bytes 884744 | tf_op jit(solution)/shard_map/ppermute | solution.py:611
  47.6 6.7 %collective-permute-start.2 = (f32[3,64,128]{2,1,0:T(8,128)S(1)}, f32[3,64,128]{2,1,0:T(8,128)S(1)}, u32[]{:S(2)}, u32[]{:S(2)}) collective-permute-start(f32[3,64,128]{2,1,0:T(8,128)S(1)} %get-tuple-element.13.refs_5_), channel_id=1, source_target_pairs={{1,2},{3,4},{5,6},{7,8},{9,10},{11,12},{13,14},{15,16},{17,18},{19... | collective-permute-start | bytes 294920 | tf_op jit(solution)/shard_map/ppermute | solution.py:613
  51.3 3.1 %collective-permute-start.3 = (f32[3,64,128]{2,1,0:T(8,128)S(1)}, f32[3,64,128]{2,1,0:T(8,128)S(1)}, u32[]{:S(2)}, u32[]{:S(2)}) collective-permute-start(f32[3,64,128]{2,1,0:T(8,128)S(1)} %get-tuple-element.11.last.refs_4_), channel_id=1, source_target_pairs={{0,1},{2,3},{4,5},{6,7},{8,9},{10,11},{12,13},{14,15},{16,17},{18,... | collective-permute-start | bytes 294920 | tf_op jit(solution)/shard_map/ppermute | solution.py:613

commit v3 on v2

--- a/solution.py
+++ b/solution.py
@@ -82,9 +82,9 @@
     angle = angles(signed(KX), np.arange(planes), planes)
 
     def one(small):
-        wide = np.zeros((planes, SUB, SUB, KX))
+        wide = np.zeros((2, planes, SUB // 2, SUB, KX))
         for s in range(SUB):
-            wide[:, s, s, :] = small.T
+            wide[s // (SUB // 2), :, s % (SUB // 2), s, :] = small.T
         return wide.reshape(planes * SUB, SUB * KX)
 
     return np.concatenate([one(np.cos(angle)), one(np.sin(angle))], axis=0).astype(np.float32)
@@ -141,67 +141,88 @@
     return ((real, imag), (-imag, real), (-real, -imag), (imag, -real))[turns % 4]
 
 
-def forward_kernel(features, scale, table_z, table_y, turns, lines, total):
-    step = pl.program_id(0)
-    rows = features.shape[1] // LANES
-
-    @pl.when(step == 0)
-    def _():
-        total[...] = jnp.zeros_like(total)
-
-    values = features[...].astype(F32) * column(scale[...])
-
-    def tile(t, j):
-        return values[SUB * t : SUB * (t + 1), LANES * j : LANES * (j + 1)]
-
-    cells = jnp.concatenate(
-        [
-            jnp.concatenate([tile(t, j), tile(t + 1, j)], axis=1)
-            for t in range(0, TILES, TWO)
-            for j in range(rows)
-        ],
-        axis=0,
-    ).astype(BF16)
-    part = dot(cells, table_z[...])
-    part = part[:, :LANES] + part[:, LANES:]
-    high, low = split(jnp.concatenate([part[: SUB * rows], part[SUB * rows :]], axis=1))
-    table = table_y[...]
-    inner = table.shape[1] // 2
-    sums = dot(
-        jnp.concatenate([table[:, :inner], table], axis=1),
-        jnp.concatenate([low, high, high], axis=0),
-    )
+def forward_kernel(
+    features, scale, table_z, table_y, turns, lines, values, held, factor, own_z, own_y, own_turns, done
+):
+    span = QUARTER * LANES
+    chunks = features.shape[1] // span
+    loads = [(scale, factor), (features.at[:, :span], held.at[0]), (table_z, own_z)]
+    loads += [(table_y, own_y), (turns, own_turns)]
+    loads += [(features.at[:, span * m : span * (m + 1)], held.at[m]) for m in range(1, chunks)]
+    loads = [pltpu.make_async_copy(*pair, done.at[k]) for k, pair in enumerate(loads)]
+    for load in loads:
+        load.start()
+
     n = (FOLD + 1) * SUB
-    for k in range(FOLD + 1):
-        at = slice(SUB * k, SUB * (k + 1))
-        real, imag = quarters(total[0, at], total[1, at], k)
-        total[0, at] = real + sums[at]
-        total[1, at] = imag + sums[n + SUB * (k - 1) : n + SUB * k] if k else imag
-
-    @pl.when(step == pl.num_programs(0) - 1)
-    def _():
-        cosine = twice(tall(turns[0], 0, FOLD + 1))
-        sine = twice(tall(turns[1], 0, FOLD + 1))
-        even = cosine * total[0] - sine * total[1]
-        odd = sine * total[0] + cosine * total[1]
-        lane = lax.broadcasted_iota(jnp.int32, (n, LANES), 1)
-        own = lane // (2 * TWO) % 2 == 0
-
-        def packed(sign):
-            sides = []
-            for k in range(2):
-                at = slice(LANES * k, LANES * (k + 1))
-                turned = pltpu.roll(odd[:, at], HALF, 1)
-                whole_line = even[:, at] + jnp.where(lane < HALF, sign, -sign) * turned
-                shift = LANES - 2 * TWO if k == 0 else 2 * TWO
-                sides.append(whole_line + pltpu.roll(whole_line, shift, 1))
-            return jnp.where(own, sides[0], sides[1])
-
-        up, down = packed(1.0), packed(-1.0)
-        lines[: FOLD * SUB] = up[: FOLD * SUB]
-        for k in range(FOLD, 0, -1):
-            at = (KY - k) * SUB
-            lines[at : at + SUB] = down[SUB * k : SUB * (k + 1)]
+    even, odd = [None] * (FOLD + 1), [None] * (FOLD + 1)
+    for m in range(chunks):
+        if m == 0:
+            for load in loads[:3]:
+                load.wait()
+            gain = column(factor[...])
+        elif m == 1:
+            for load in loads[5:]:
+                load.wait()
+        scaled = held[m].astype(F32) * gain
+        values[:, span * m : span * (m + 1)] = scaled.astype(BF16)
+
+        def tile(t, j):
+            return scaled[SUB * t : SUB * (t + 1), LANES * j : LANES * (j + 1)]
+
+        cells = jnp.concatenate(
+            [
+                jnp.concatenate([tile(t, j), tile(t + 1, j)], axis=1)
+                for t in range(0, TILES, TWO)
+                for j in range(QUARTER)
+            ],
+            axis=0,
+        ).astype(BF16)
+        part = dot(cells, own_z[...])
+        part = part[:, :LANES] + part[:, LANES:]
+        high, low = split(
+            jnp.concatenate([part[: SUB * QUARTER], part[SUB * QUARTER :]], axis=1)
+        )
+        if m == 0:
+            for load in loads[3:5]:
+                load.wait()
+        table = own_y[...]
+        inner = table.shape[1] // 2
+        sums = dot(
+            jnp.concatenate([table[:, :inner], table], axis=1),
+            jnp.concatenate([low, high, high], axis=0),
+        )
+        for k in range(FOLD + 1):
+            real = sums[SUB * k : SUB * (k + 1)]
+            imag = sums[n + SUB * (k - 1) : n + SUB * k] if k else jnp.zeros_like(real)
+            real, imag = quarters(real, imag, m * k)
+            even[k] = real if even[k] is None else even[k] + real
+            odd[k] = imag if odd[k] is None else odd[k] + imag
+
+    first, second = jnp.concatenate(even, axis=0), jnp.concatenate(odd, axis=0)
+    cosine = twice(tall(own_turns[0], 0, FOLD + 1))
+    sine = twice(tall(own_turns[1], 0, FOLD + 1))
+    even = cosine * first - sine * second
+    odd = sine * first + cosine * second
+    lane = lax.broadcasted_iota(jnp.int32, (n, LANES), 1)
+    own = (lane & (2 * TWO)) == 0
+
+    def packed(sign):
+        sides = []
+        for k in range(2):
+            at = slice(LANES * k, LANES * (k + 1))
+            line = even[:, at] + sign * pltpu.roll(odd[:, at], HALF, 1)
+            shift = LANES - 2 * TWO if k == 0 else 2 * TWO
+            sides.append(line + pltpu.roll(line, shift, 1))
+        line = jnp.where(own, sides[0], sides[1])
+        raised = pltpu.roll(pltpu.roll(line, HALF, 1), n - SUB // 2, 0)
+        return jnp.where(lane < HALF, line, raised)
+
+    up, down = packed(1.0), packed(-1.0)
+    for k in range(FOLD):
+        lines[SUB // 2 * k : SUB // 2 * (k + 1)] = up[SUB * k : SUB * k + SUB // 2]
+    for k in range(FOLD, 0, -1):
+        at = (KY - k) * SUB // 2
+        lines[at : at + SUB // 2] = down[SUB * k : SUB * k + SUB // 2]
 
 
 def swap_blocks(pieces):
@@ -216,13 +237,63 @@
     return out
 
 
-def mix_kernel(lines, weight, table_x, table_back, back, modes, mixed):
+def diagonal(block):
+    width = block.shape[1]
+    wide = (1, SUB * width)
+    if width % LANES:
+        row = lax.broadcasted_iota(jnp.int32, (width, SUB * width), 0)
+        lane = lax.broadcasted_iota(jnp.int32, (width, SUB * width), 1)
+        spread_out = (lax.rem(lane, width) == row).astype(F32).astype(BF16)
+        block = dot(block.astype(BF16), spread_out)
+    else:
+        block = jnp.concatenate([block] * SUB, axis=1)
+    lane = lax.broadcasted_iota(jnp.int32, wide, 1)
+    return jnp.concatenate(
+        [
+            jnp.where((lane >= width * g) & (lane < width * (g + 1)), block, 0.0)
+            for g in range(SUB)
+        ],
+        axis=0,
+    )
+
+
+def turned_by_i(x, axis):
+    size = x.shape[axis]
+    place = lax.broadcasted_iota(jnp.int32, x.shape, axis)
+    after = pltpu.roll(x, size - TWO, axis)
+    before = pltpu.roll(x, TWO, axis)
+    return jnp.where((place & TWO) == 0, -after, before)
+
+
+def mix_kernel(
+    lines,
+    weight,
+    table_x,
+    table_back,
+    bypass,
+    mlp_in_t,
+    mlp_out,
+    decode,
+    back,
+    wide_bypass,
+    wide_in,
+    wide_out,
+    modes,
+    mixed,
+):
+    wide_bypass[...] = diagonal(bypass[...].astype(F32)).astype(BF16)
+    wide_in[...] = diagonal(0.5 * mlp_in_t[...].astype(F32).T).astype(BF16)
+    heads = 0.5 * dot(decode[...], mlp_out[...])
+    heads = jnp.concatenate([diagonal(heads[k : k + 1]) for k in range(2)], axis=0)
+    wide_out[...] = jnp.concatenate(split(heads), axis=0)
+
     highest = lax.Precision.HIGHEST
     half = lines.shape[1] // 2
     count = half // (2 * TILES)
     groups = count // 4
     flipped = lines[...].T
-    pair = jnp.concatenate([flipped[:half], flipped[half:]], axis=1)
+    straight = jnp.concatenate([flipped[:half], flipped[half:]], axis=1)
+    pair = jnp.concatenate([straight, -turned_by_i(straight, 0)], axis=1)
     spectrum = dot(pair, table_x[...], precision=highest)
     for c in range(SUB // 4):
         for a in range(groups):
@@ -268,54 +339,47 @@
                 for b in range(4):
                     parts[4 * a + b][c] = got[b]
         rows.append(jnp.concatenate([jnp.concatenate(p, axis=1) for p in parts], axis=0))
-    straight, turned = rows
-    sides = jnp.concatenate(
-        [
-            jnp.concatenate([straight, turned], axis=1),
-            jnp.concatenate([turned, -straight], axis=1),
-        ],
-        axis=0,
-    )
-    back[...] = dot(table_back[...], sides, ((1,), (1,)), precision=highest)
+    got = dot(table_back[...], jnp.concatenate(rows, axis=1), ((1,), (1,)), precision=highest)
+    count = got.shape[0] // 2
+    back[...] = jnp.concatenate([got[:count], got[count:]], axis=1)
 
 
 def gelu_twice(x):
     return x + x * jnp.tanh(x * (GELU_A + GELU_B * (x * x)))
 
 
-def diagonal(block):
-    height, width = block.shape
-    tall_block = jnp.concatenate([block] * SUB, axis=0)
-    rows = lax.broadcasted_iota(jnp.int32, (SUB * height, SUB * width), 0) // height
-    columns = lax.broadcasted_iota(jnp.int32, (SUB * height, SUB * width), 1) // width
-    return jnp.where(rows == columns, jnp.concatenate([tall_block] * SUB, axis=1), 0.0)
-
-
 def point_kernel(
     lines,
-    features,
-    scale,
-    bypass,
-    mlp_in_t,
-    mlp_out,
-    decode,
+    values,
+    wide_bypass,
+    wide_in,
+    wide_out,
     zone,
     opened,
     perm_table,
-    table_y,
-    table_z,
+    tables,
     turns,
-    *refs,
+    near_side,
+    far_side,
+    filled,
+    smooth,
     first,
 ):
-    fields, near_side, far_side, smooth = refs[-4:]
-    rows = features.shape[1] // LANES
-    held = lines[...]
-    other = pltpu.roll(held, HALF, 1)
+    rows = near_side.shape[1]
+    sent = lines[...]
+    rolled = pltpu.roll(sent, HALF, 1)
+    top = lax.broadcasted_iota(jnp.int32, sent.shape, 0) % SUB < SUB // 2
+    of_even = jnp.where(top, sent, pltpu.roll(rolled, SUB // 2, 0))
+    of_odd = jnp.where(top, pltpu.roll(sent, sent.shape[0] - SUB // 2, 0), rolled)
+    held = jnp.concatenate(
+        [x[SUB * k : SUB * (k + 1)] for k in range(KY // 2) for x in (of_even, of_odd)], axis=0
+    )
     low_half = lax.broadcasted_iota(jnp.int32, held.shape, 1) < HALF
+    held = jnp.where(low_half, held, pltpu.roll(held, HALF, 1))
+    other = turned_by_i(held, 1)
     cosine, sine = tall(turns[0], 0, KY), tall(turns[1], 0, KY)
-    straight = jnp.where(low_half, held, cosine * other + sine * held)
-    turned = jnp.where(low_half, other, cosine * held - sine * other)
+    straight = jnp.where(low_half, held, cosine * held + sine * other)
+    turned = jnp.where(low_half, other, cosine * other - sine * held)
 
     def at(x, k):
         return x[SUB * k : SUB * (k + 1)]
@@ -325,7 +389,8 @@
     even.append(at(straight, FOLD))
     odd.append(-at(turned, FOLD))
     level = jnp.concatenate([at(straight, 0)] * QUARTER, axis=0)
-    table = jnp.concatenate([table_z[:LANES], table_z[...]], axis=0)
+    count = QUARTER * SUB
+    table = jnp.concatenate([tables[count : count + LANES], tables[count:]], axis=0)
     for m in range(rows // QUARTER):
         sides = [
             quarters(real, -imag, (first // QUARTER + m) * k)
@@ -333,17 +398,11 @@
         ]
         sides = [real for real, _ in sides] + [-imag for _, imag in sides]
         sides = jnp.concatenate(split(jnp.concatenate(sides, axis=0)), axis=1)
-        both = dot(table_y[...], jnp.concatenate([sides, sides], axis=0))
+        both = dot(tables[:count], jnp.concatenate([sides, sides], axis=0))
         high, low = split(both[:, :LANES] + both[:, LANES:] + level)
         smooth[QUARTER * SUB * m : QUARTER * SUB * (m + 1)] = dot(
             jnp.concatenate([low, high, high], axis=1), table
         )
-
-    wide_bypass = diagonal(bypass[...].astype(F32)).astype(BF16)
-    wide_in = diagonal(0.5 * mlp_in_t[...].astype(F32).T).astype(BF16)
-    heads = 0.5 * dot(decode[...], mlp_out[...])
-    heads = jnp.concatenate([diagonal(heads[k : k + 1]) for k in range(2)], axis=0)
-    wide_out = jnp.concatenate(split(heads), axis=0)
 
     groups = rows // SUB
 
@@ -356,8 +415,7 @@
             axis=0,
         )
 
-    values = features[...].astype(F32) * column(scale[...])
-    values = grouped(lambda j: values[:, LANES * j : LANES * (j + 1)]).astype(BF16)
+    own = grouped(lambda j: values[:, LANES * (first + j) : LANES * (first + j + 1)])
     spectral = grouped(
         lambda j: jnp.concatenate(
             [
@@ -367,9 +425,9 @@
             axis=0,
         )
     )
-    lifted = gelu_twice(spectral + dot(wide_bypass, values)).astype(BF16)
-    hidden = gelu_twice(dot(wide_in, lifted)).astype(BF16)
-    decoded = dot(wide_out, hidden)
+    lifted = gelu_twice(spectral + dot(wide_bypass[...], own)).astype(BF16)
+    hidden = gelu_twice(dot(wide_in[...], lifted)).astype(BF16)
+    decoded = dot(wide_out[...], hidden)
     decoded = decoded[: 2 * SUB] + decoded[2 * SUB :]
     even_plane = lax.axis_index("gx") % 2 == 0
     for a in range(rows // SUB):
@@ -378,11 +436,11 @@
         square = saturation * saturation
         rest = 1.0 - saturation
         at = slice(SUB * a, SUB * (a + 1))
-        fields[0, at] = pressure
-        fields[1, at] = saturation
+        here = slice(first + SUB * a, first + SUB * (a + 1))
+        filled[at] = saturation
         mobility = square / (square + 0.5 * rest * rest)
-        perm = lookup(zone[at], perm_table)
-        gated = perm * opened[0, at].astype(F32)
+        perm = lookup(zone[here], perm_table)
+        gated = perm * opened[0, here].astype(F32)
         near_side[0, at] = pressure
         near_side[1, at] = mobility
         near_side[2, at] = jnp.where(even_plane, gated, perm)
@@ -431,8 +489,12 @@
     return jnp.where(lane % NZ == 0, 0.0, pltpu.roll(field, 1, 1))
 
 
-def inner_kernel(first, last, zone, opened, perm_table, partial):
+def inner_kernel(
+    first, last, first_filled, last_filled, zone, opened, perm_table, fields, partial
+):
     pressure, mobility = [jnp.concatenate([first[k], last[k]], axis=0) for k in range(2)]
+    fields[0] = pressure
+    fields[1] = jnp.concatenate([first_filled[...], last_filled[...]], axis=0)
     perm = lookup(zone[...], perm_table)
     residual = jnp.zeros(pressure.shape, F32)
     for axis, ahead, behind in ((1, ahead_y, behind_y), (2, ahead_z, behind_z)):
@@ -489,46 +551,48 @@
     shares = devices // KY
     held = KZ // shares
 
-    fixed = lambda i: (0, 0)
-    cubes = lambda i: (0, 0, 0)
-    steps = ROWS // QUARTER
-    part = QUARTER
-    span = part * LANES
-    count = 2 * FOLD + 1
-    lines = pl.pallas_call(
+    span = QUARTER * LANES
+    chunks = cells // span
+    table_z, table_y, turns = z_forward_table(), y_forward_table(), turn_forward_table()
+    lines, values = pl.pallas_call(
         forward_kernel,
-        grid=(steps,),
-        in_specs=[
-            pl.BlockSpec((width, span), lambda i: (0, steps - 1 - i)),
-            pl.BlockSpec((1, width), fixed),
-            pl.BlockSpec((TWO * LANES, 2 * LANES), fixed),
-            pl.BlockSpec((count * SUB, 2 * part * SUB), fixed),
-            pl.BlockSpec((2, FOLD + 1, LANES), cubes),
+        in_specs=[pl.BlockSpec(memory_space=pl.ANY)] * 5,
+        out_specs=[whole()] * 2,
+        out_shape=[
+            jax.ShapeDtypeStruct((KY * SUB // 2, LANES), F32),
+            jax.ShapeDtypeStruct((width, cells), BF16),
         ],
-        out_specs=pl.BlockSpec((KY * SUB, LANES), fixed),
-        out_shape=jax.ShapeDtypeStruct((KY * SUB, LANES), F32),
-        scratch_shapes=[pltpu.VMEM((2, (FOLD + 1) * SUB, 2 * LANES), F32)],
+        scratch_shapes=[
+            pltpu.VMEM((chunks, width, span), BF16),
+            pltpu.VMEM((1, width), F32),
+            pltpu.VMEM(table_z.shape, BF16),
+            pltpu.VMEM(table_y.shape, BF16),
+            pltpu.VMEM(turns.shape, F32),
+            pltpu.SemaphoreType.DMA((4 + chunks,)),
+        ],
         compiler_params=params(),
         name="forward_yz",
-    )(
-        near(plane),
-        near(scale),
-        near(jnp.asarray(z_forward_table())),
-        near(jnp.asarray(y_forward_table())),
-        near(jnp.asarray(turn_forward_table())),
-    )
-
-    blocks = lines.reshape(KY, SUB, 2, shares, held * 2 * TILES)
-    blocks = blocks.transpose(0, 3, 1, 2, 4).reshape(devices, SUB, 2 * held * 2 * TILES)
+    )(*map(near, (plane, scale, jnp.asarray(table_z), jnp.asarray(table_y), jnp.asarray(turns))))
+
+    part = SUB // 2
+    share = held * 2 * TILES
+    blocks = lines.reshape(KY, part, 2, shares, share)
+    blocks = blocks.transpose(0, 3, 1, 2, 4).reshape(devices, part, 2 * share)
     blocks = lax.all_to_all(blocks, "gx", 0, 0, tiled=True)
-    lines = blocks.reshape(planes * SUB, 2 * held * 2 * TILES)
+    lines = blocks.reshape(planes * part, 2 * share)
 
     modes = spec_weight.shape[3]
-    back = pl.pallas_call(
+    hidden = mlp_in.shape[0]
+    back, *wide = pl.pallas_call(
         mix_kernel,
-        in_specs=[whole()] * 4,
-        out_specs=whole(),
-        out_shape=jax.ShapeDtypeStruct((planes * SUB, 2 * held * 2 * TILES), F32),
+        in_specs=[whole()] * 8,
+        out_specs=[whole()] * 4,
+        out_shape=[
+            jax.ShapeDtypeStruct((planes * part, 2 * share), F32),
+            jax.ShapeDtypeStruct((SUB * width, SUB * width), BF16),
+            jax.ShapeDtypeStruct((SUB * hidden, SUB * width), BF16),
+            jax.ShapeDtypeStruct((4 * SUB, SUB * hidden), BF16),
+        ],
         scratch_shapes=[
             pltpu.VMEM((SUB, 2 * TILES, modes), F32),
             pltpu.VMEM((2, modes // LANES, 2 * width, LANES), F32),
@@ -540,47 +604,29 @@
         spec_weight,
         jnp.asarray(x_forward_table(planes)),
         jnp.asarray(x_back_table(planes)),
+        bypass_weight,
+        mlp_in.T,
+        mlp_out,
+        decode_weight,
     )
 
-    blocks = back.reshape(devices, SUB, 2 * held * 2 * TILES)
+    blocks = back.reshape(devices, part, 2 * share)
     blocks = lax.all_to_all(blocks, "gx", 0, 0, tiled=True)
-    blocks = blocks.reshape(KY, shares, SUB, 2, held * 2 * TILES).transpose(0, 2, 3, 1, 4)
-    lines = blocks.reshape(KY * SUB, 2 * HALF)
-
-    def network(first, count, carried):
-        at = first // count
+    blocks = blocks.reshape(KY, shares, part, 2, share).transpose(0, 2, 3, 1, 4)
+    lines = blocks.reshape(KY * part, 2 * HALF)
+
+    tables = np.concatenate([y_back_table(), z_back_table(planes * NY * NZ)], axis=0)
+    tables = jnp.asarray(tables)
+
+    def network(first, count):
         side = jax.ShapeDtypeStruct((3, count, LANES), F32)
+        smem = pl.BlockSpec(memory_space=pltpu.SMEM)
         return pl.pallas_call(
             functools.partial(point_kernel, first=first),
-            grid=(1,),
-            in_specs=[
-                pl.BlockSpec((KY * SUB, LANES), fixed),
-                pl.BlockSpec((width, count * LANES), lambda i: (0, at)),
-                pl.BlockSpec((1, width), fixed),
-                pl.BlockSpec(bypass_weight.shape, fixed),
-                pl.BlockSpec(mlp_in.shape[::-1], fixed),
-                pl.BlockSpec(mlp_out.shape, fixed),
-                pl.BlockSpec(decode_weight.shape, fixed),
-                pl.BlockSpec((count, LANES), lambda i: (at, 0)),
-                pl.BlockSpec((1, count, LANES), lambda i: (0, at, 0)),
-                pl.BlockSpec(memory_space=pltpu.SMEM),
-                pl.BlockSpec((QUARTER * SUB, 4 * FOLD * SUB), fixed),
-                pl.BlockSpec((2 * LANES, TILES * LANES), fixed),
-                pl.BlockSpec((2, KY, LANES), cubes),
-            ]
-            + [pl.BlockSpec(memory_space=pl.ANY)] * len(carried),
-            out_specs=[
-                pl.BlockSpec((2, count, LANES), lambda i: (0, at, 0)),
-                pl.BlockSpec((3, count, LANES), cubes),
-                pl.BlockSpec((3, count, LANES), cubes),
-            ],
-            out_shape=[
-                jax.ShapeDtypeStruct((2, ROWS, LANES), F32),
-                side,
-                side,
-            ],
+            in_specs=[whole()] * 7 + [smem] + [whole()] * 2,
+            out_specs=[whole()] * 3,
+            out_shape=[side, side, jax.ShapeDtypeStruct((count, LANES), F32)],
             scratch_shapes=[pltpu.VMEM((count * SUB, TILES * LANES), F32)],
-            input_output_aliases={13 + k: k for k in range(len(carried))},
             compiler_params=params(),
             cost_estimate=pl.CostEstimate(
                 flops=count * LANES * 400000, bytes_accessed=count * LANES * 200, transcendentals=0
@@ -588,37 +634,34 @@
             name="point_network",
         )(
             lines,
-            plane,
-            scale,
-            bypass_weight,
-            mlp_in.T,
-            mlp_out,
-            decode_weight,
+            values,
+            *wide,
             zone,
             opened,
             perm_table,
-            jnp.asarray(y_back_table()),
-            jnp.asarray(z_back_table(planes * NY * NZ)),
+            tables,
             jnp.asarray(turn_back_table()),
-            *carried,
         )
 
     far = [(i, i + 1) for i in range(1, devices - 1, 2)]
     far = far + [(b, a) for a, b in far]
     near_by = [(i, i + 1) for i in range(0, devices, 2)]
     near_by = near_by + [(b, a) for a, b in near_by]
-    fields, *first = network(0, ROWS - QUARTER, ())
+    *first, first_filled = network(0, ROWS - QUARTER)
     first_other = [lax.ppermute(first[1], "gx", far), lax.ppermute(first[0], "gx", near_by)]
-    fields, *last = network(ROWS - QUARTER, QUARTER, (fields,))
+    *last, last_filled = network(ROWS - QUARTER, QUARTER)
     last_other = [lax.ppermute(last[1], "gx", far), lax.ppermute(last[0], "gx", near_by)]
-    partial = pl.pallas_call(
+    fields, partial = pl.pallas_call(
         inner_kernel,
-        in_specs=[whole()] * 4 + [pl.BlockSpec(memory_space=pltpu.SMEM)],
-        out_specs=whole(),
-        out_shape=jax.ShapeDtypeStruct((ROWS, LANES), F32),
+        in_specs=[whole()] * 6 + [pl.BlockSpec(memory_space=pltpu.SMEM)],
+        out_specs=[whole()] * 2,
+        out_shape=[
+            jax.ShapeDtypeStruct((2, ROWS, LANES), F32),
+            jax.ShapeDtypeStruct((ROWS, LANES), F32),
+        ],
         compiler_params=params(),
         name="faces_in_plane",
-    )(first[0], last[0], zone, opened, perm_table)
+    )(first[0], last[0], first_filled, last_filled, zone, opened, perm_table)
     residual = pl.pallas_call(
         outer_kernel,
         in_specs=[whole()] * 9,

time: 55.6 us -> 51.9 us (0.933)
  Pallas kernels: 21 us -> 19.2 us
  blocking collectives: 25.1 us -> 23.3 us
    all_to_all x2, blocking collectives: 25.1 us -> 23.3 us  [body(): blocks = lax.all_to_all(blocks, 'gx', 0, 0, tiled=True)]
    pallas_call x5, Pallas kernels: 20.2 us -> 18.4 us  [the longest x2 10.4 us: network(): pl.pallas_call(functools.partial(point_kernel, first=first), in_specs=[wh...]
where the time goes in v3:
time: 51.9 us; the launch traced here: 51.6 us
  blocking collectives  23.3 us (45%)
  Pallas kernels  19.2 us (37%)
  starting transfers between devices  6.29 us (12%)
  waiting for transfers between devices  1.96 us (4%)
  between operations  0.85 us (2%)
    all_to_all x2, blocking collectives, body(): blocks = lax.all_to_all(blocks, 'gx', 0, 0, tiled=True)  23.3 us
    pallas_call x2, Pallas kernels, network(): pl.pallas_call(functools.partial(point_kernel, first=first), in_specs=[wh...  10.4 us
    pallas_call x1, Pallas kernels, body(): pl.pallas_call(forward_kernel, in_specs=[pl.BlockSpec(memory_space=pl.ANY...  4.29 us
    ppermute x1, starting transfers between devices, body(): lax.ppermute(last[1], 'gx', far)  3.63 us
    ppermute x1, starting transfers between devices, body(): lax.ppermute(first[1], 'gx', far)  2.52 us
    pallas_call x1, Pallas kernels, body(): pl.pallas_call(mix_kernel, in_specs=[whole()] * 8, out_specs=[whole()] *...  2.08 us
    ppermute x1, waiting for transfers between devices, body(): lax.ppermute(last[1], 'gx', far)  1.95 us
    pallas_call x1, Pallas kernels, body(): pl.pallas_call(inner_kernel, in_specs=[whole()] * 6 + [pl.BlockSpec(memor...  1.65 us
  transfers between devices with their start and end apart: 4, of which 1 were waited for; matrix products, arithmetic and copies ran while one was open for 0% of the time, Pallas kernels for 9%

profile of v3, /device:TPU:1, one launch (start us, length us, event | category | flops | bytes accessed | tf_op | source)
XLA Modules:
  0.0 51.6 jit_solution(4493063197793962342)
XLA Ops:
  0.6 0.0 copy-start.1
  0.6 0.0 copy-start.2
  0.7 0.0 copy-start.8
  0.7 0.0 copy-start.7
  0.7 0.0 copy-start.6
  0.7 0.0 copy-start.5
  0.7 0.0 copy-start
  0.7 0.0 copy-start.3
  0.7 0.0 copy-start.4
  0.7 0.0 copy-start.9
  0.7 0.0 copy-start.10
  0.8 0.0 copy-start.11
  0.8 4.3 %forward_yz.1 = (f32[128,128]{1,0:T(8,128)S(1)}, bf16[32,32768]{1,0:T(8,128)(2,1)S(1)}) custom-call(bf16[32,32768]{1,0:T(8,128)(2,1)} %bitcast.23, f32[1,32]{1,0:T(1,128)} %bitcast.25, bf16[256,256]{1,0:T(8,128)(2,1)} %constant.14.clone.table_z, bf16[264,1024]{1,0:T(8,128)(2,1)} %constant.15.clone.table_y, f32[2,17,128]{2,1,0:T(8,128)} %constant.16.clone.turns), custom_call_target="tpu_custom_call" | custom-call | tf_op jit(solution)/shard_map/forward_yz/pallas_call | solution.py:557
  5.1 14.2 %all_to_all.10 = f32[32,4,128]{2,1,0:T(4,128)S(1)} all-to-all(f32[32,4,128]{2,1,0:T(4,128)S(1)} %bitcast.21), channel_id=1, replica_groups=mesh['groups'=1,'gx'=32] {'gx'}, dimensions={0} | all-to-all | bytes 131072 | tf_op jit(solution)/shard_map/all_to_all | solution.py:581
  19.2 0.0 copy-done.1
  19.2 0.0 copy-done.2
  19.2 0.0 copy-done.8
  19.2 0.0 copy-done.7
  19.2 0.0 copy-done.6
  19.3 0.0 copy-done.5
  19.3 0.0 copy-done
  19.3 2.1 %mix_modes.1 = (f32[128,128]{1,0:T(8,128)S(1)}, bf16[256,256]{1,0:T(8,128)(2,1)S(1)}, bf16[1024,256]{1,0:T(8,128)(2,1)S(1)}, bf16[32,1024]{1,0:T(8,128)(2,1)S(1)}) custom-call(f32[128,128]{1,0:T(8,128)S(1)} %bitcast.14, bf16[2,32,32,256]{3,2,1,0:T(8,128)(2,1)S(1)} %copy-done, f32[512,256]{1,0:T(8,128)S(1)} %copy-done.2, f32[256,512]{1,0:T(8,128)S(1)} %copy-done.1, ...), custom_call_target="tpu_custom_call" | custom-call | tf_op jit(solution)/shard_map/mix_modes/pallas_call | solution.py:586
  21.4 9.1 %all_to_all.11 = f32[32,4,128]{2,1,0:T(4,128)S(1)} all-to-all(f32[32,4,128]{2,1,0:T(4,128)S(1)} %bitcast.20), channel_id=1, replica_groups=mesh['groups'=1,'gx'=32] {'gx'}, dimensions={0} | all-to-all | bytes 131072 | tf_op jit(solution)/shard_map/all_to_all | solution.py:614
  30.5 0.0 copy-done.3
  30.5 0.0 copy-done.4
  30.5 0.0 copy-done.9
  30.5 0.0 copy-done.10
  30.5 0.0 copy-done.11
  30.5 7.3 %point_network.2 = (f32[3,192,128]{2,1,0:T(8,128)S(1)}, f32[3,192,128]{2,1,0:T(8,128)S(1)}, f32[192,128]{1,0:T(8,128)S(1)}) custom-call(f32[128,128]{1,0:T(8,128)S(1)} %bitcast.18, bf16[32,32768]{1,0:T(8,128)(2,1)S(1)} %get-tuple-element.18.values, bf16[256,256]{1,0:T(8,128)(2,1)S(1)} %get-tuple-element.19.wide_bypass, ...), custom_call_target="tpu_custom_call" | custom-call | flops 9830400000 | bytes 4915200 | tf_op jit(solution)/shard_map/point_network/pallas_call | solution.py:624
  37.8 2.5 %collective-permute-start = (f32[3,192,128]{2,1,0:T(8,128)S(1)}, f32[3,192,128]{2,1,0:T(8,128)S(1)}, u32[]{:S(2)}, u32[]{:S(2)}) collective-permute-start(f32[3,192,128]{2,1,0:T(8,128)S(1)} %get-tuple-element.28.refs_1_), channel_id=1, source_target_pairs={{1,2},{3,4},{5,6},{7,8},{9,10},{11,12},{13,14},{15,16},{17,18},{19... | collective-permute-start | bytes 884744 | tf_op jit(solution)/shard_map/ppermute | solution.py:651
  40.4 0.1 collective-permute-start.1
  40.4 3.1 %point_network.3 = (f32[3,64,128]{2,1,0:T(8,128)S(1)}, f32[3,64,128]{2,1,0:T(8,128)S(1)}, f32[64,128]{1,0:T(8,128)S(1)}) custom-call(f32[128,128]{1,0:T(8,128)S(1)} %bitcast.19, bf16[32,32768]{1,0:T(8,128)(2,1)S(1)} %get-tuple-element.18.values, bf16[256,256]{1,0:T(8,128)(2,1)S(1)} %get-tuple-element.19.wide_bypass, ...), custom_call_target="tpu_custom_call" | custom-call | flops 3276800000 | bytes 1638400 | tf_op jit(solution)/shard_map/point_network/pallas_call | solution.py:624
  43.5 3.6 %collective-permute-start.2 = (f32[3,64,128]{2,1,0:T(8,128)S(1)}, f32[3,64,128]{2,1,0:T(8,128)S(1)}, u32[]{:S(2)}, u32[]{:S(2)}) collective-permute-start(f32[3,64,128]{2,1,0:T(8,128)S(1)} %get-tuple-element.29.refs_5_), channel_id=1, source_target_pairs={{1,2},{3,4},{5,6},{7,8},{9,10},{11,12},{13,14},{15,16},{17,18},{19... | collective-permute-start | bytes 294920 | tf_op jit(solution)/shard_map/ppermute | solution.py:653
  47.2 0.1 collective-permute-start.3
  47.2 1.6 %faces_in_plane.1 = (f32[2,256,128]{2,1,0:T(8,128)}, f32[256,128]{1,0:T(8,128)S(1)}) custom-call(f32[3,192,128]{2,1,0:T(8,128)S(1)} %get-tuple-element.22.first.refs_0_, f32[3,64,128]{2,1,0:T(8,128)S(1)} %get-tuple-element.23.last.refs_4_, f32[192,128]{1,0:T(8,128)S(1)} %get-tuple-element.24.first_filled, f32[64,128]{1,0:T(8,128)S(1)} %get-tuple-element.25.last_filled, ...), custom_call_target="tpu_custom_call" | custom-call | tf_op jit(solution)/shard_map/faces_in_plane/pallas_call | solution.py:654
  48.9 1.9 %collective-permute-done.2.refs_6_ = f32[3,64,128]{2,1,0:T(8,128)S(1)} collective-permute-done((f32[3,64,128]{2,1,0:T(8,128)S(1)}, f32[3,64,128]{2,1,0:T(8,128)S(1)}, u32[]{:S(2)}, u32[]{:S(2)}) %collective-permute-start.2) | collective-permute-done | bytes 98336 | tf_op jit(solution)/shard_map/ppermute | solution.py:653
  50.8 0.0 collective-permute-done.3.refs_7_
  50.9 0.0 collective-permute-done.refs_2_
  50.9 0.0 collective-permute-done.1.refs_3_
  50.9 0.8 %faces_between_planes.1 = f32[256,128]{1,0:T(8,128)} custom-call(f32[256,128]{1,0:T(8,128)S(1)} %get-tuple-element.27.partial, f32[3,192,128]{2,1,0:T(8,128)S(1)} %get-tuple-element.22.first.refs_0_, f32[3,192,128]{2,1,0:T(8,128)S(1)} %get-tuple-element.28.refs_1_, f32[3,192,128]{2,1,0:T(8,128)S(1)} %collective-permute-done.refs_2_, ...), custom_call_target="tpu_custom_call" | custom-call | tf_op jit(solution)/shard_map/faces_between_planes/pallas_call | solution.py:665
Async XLA Ops:
  0.6 18.6 %copy-start.1 = (f32[256,512]{1,0:T(8,128)S(1)}, f32[256,512]{1,0:T(8,128)}, u32[]{:S(2)}) copy-start(f32[256,512]{1,0:T(8,128)} %constant.18.clone.table_back) | copy-start | bytes 1572868
  0.6 18.6 %copy-start.2 = (f32[512,256]{1,0:T(8,128)S(1)}, f32[512,256]{1,0:T(8,128)}, u32[]{:S(2)}) copy-start(f32[512,256]{1,0:T(8,128)} %constant.17.clone.table_x) | copy-start | bytes 1572868
  0.7 18.6 %copy-start.8 = (bf16[2,32]{1,0:T(2,128)(2,1)S(1)}, bf16[2,32]{1,0:T(2,128)(2,1)}, u32[]{:S(2)}) copy-start(bf16[2,32]{1,0:T(2,128)(2,1)} %decode.1) | copy-start | bytes 388
  0.7 18.6 %copy-start.7 = (bf16[32,128]{1,0:T(8,128)(2,1)S(1)}, bf16[32,128]{1,0:T(8,128)(2,1)}, u32[]{:S(2)}) copy-start(bf16[32,128]{1,0:T(8,128)(2,1)} %mlp_out.1) | copy-start | bytes 24580
  0.7 18.6 %copy-start.6 = (bf16[128,32]{0,1:T(8,128)(2,1)S(1)}, bf16[128,32]{0,1:T(8,128)(2,1)}, u32[]{:S(2)}) copy-start(bf16[128,32]{0,1:T(8,128)(2,1)} %param.22) | copy-start | bytes 24580
  0.7 18.6 %copy-start.5 = (bf16[32,32]{1,0:T(8,128)(2,1)S(1)}, bf16[32,32]{1,0:T(8,128)(2,1)}, u32[]{:S(2)}) copy-start(bf16[32,32]{1,0:T(8,128)(2,1)} %bypass.1) | copy-start | bytes 6148
  0.7 18.6 %copy-start = (bf16[2,32,32,256]{3,2,1,0:T(8,128)(2,1)S(1)}, bf16[2,32,32,256]{3,2,1,0:T(8,128)(2,1)}, u32[]{:S(2)}) copy-start(bf16[2,32,32,256]{3,2,1,0:T(8,128)(2,1)} %weight.1) | copy-start | bytes 3145732
  0.7 29.8 %copy-start.3 = (s32[3,1,32768]{2,1,0:T(1,128)S(1)}, s32[3,1,32768]{2,1,0:T(1,128)}, u32[]{:S(2)}) copy-start(s32[3,1,32768]{2,1,0:T(1,128)} %param.26) | copy-start | bytes 1179652
  0.7 29.8 %copy-start.4 = (s32[1,32768]{1,0:T(1,128)S(1)}, s32[1,32768]{1,0:T(1,128)}, u32[]{:S(2)}) copy-start(s32[1,32768]{1,0:T(1,128)} %param.25) | copy-start | bytes 393220
  0.7 29.7 %copy-start.9 = (f32[8]{0:T(128)S(1)}, f32[8]{0:T(128)}, u32[]{:S(2)}) copy-start(f32[8]{0:T(128)} %perm_table.5) | copy-start | bytes 100
  0.7 29.7 %copy-start.10 = (bf16[768,512]{1,0:T(8,128)(2,1)S(1)}, bf16[768,512]{1,0:T(8,128)(2,1)}, u32[]{:S(2)}) copy-start(bf16[768,512]{1,0:T(8,128)(2,1)} %constant.19.clone.tables) | copy-start | bytes 2359300
  0.8 29.7 %copy-start.11 = (f32[2,32,128]{2,1,0:T(8,128)S(1)}, f32[2,32,128]{2,1,0:T(8,128)}, u32[]{:S(2)}) copy-start(f32[2,32,128]{2,1,0:T(8,128)} %constant.20.clone.turns) | copy-start | bytes 98308
  37.8 13.0 %collective-permute-start = (f32[3,192,128]{2,1,0:T(8,128)S(1)}, f32[3,192,128]{2,1,0:T(8,128)S(1)}, u32[]{:S(2)}, u32[]{:S(2)}) collective-permute-start(f32[3,192,128]{2,1,0:T(8,128)S(1)} %get-tuple-element.28.refs_1_), channel_id=1, source_target_pairs={{1,2},{3,4},{5,6},{7,8},{9,10},{11,12},{13,14},{15,16},{17,18},{19... | collective-permute-start | bytes 884744 | tf_op jit(solution)/shard_map/ppermute | solution.py:651
  40.4 10.5 %collective-permute-start.1 = (f32[3,192,128]{2,1,0:T(8,128)S(1)}, f32[3,192,128]{2,1,0:T(8,128)S(1)}, u32[]{:S(2)}, u32[]{:S(2)}) collective-permute-start(f32[3,192,128]{2,1,0:T(8,128)S(1)} %get-tuple-element.22.first.refs_0_), channel_id=1, source_target_pairs={{0,1},{2,3},{4,5},{6,7},{8,9},{10,11},{12,13},{14,15},{16,17},{18,... | collective-permute-start | bytes 884744 | tf_op jit(solution)/shard_map/ppermute | solution.py:651
  43.5 7.3 %collective-permute-start.2 = (f32[3,64,128]{2,1,0:T(8,128)S(1)}, f32[3,64,128]{2,1,0:T(8,128)S(1)}, u32[]{:S(2)}, u32[]{:S(2)}) collective-permute-start(f32[3,64,128]{2,1,0:T(8,128)S(1)} %get-tuple-element.29.refs_5_), channel_id=1, source_target_pairs={{1,2},{3,4},{5,6},{7,8},{9,10},{11,12},{13,14},{15,16},{17,18},{19... | collective-permute-start | bytes 294920 | tf_op jit(solution)/shard_map/ppermute | solution.py:653
  47.2 3.7 %collective-permute-start.3 = (f32[3,64,128]{2,1,0:T(8,128)S(1)}, f32[3,64,128]{2,1,0:T(8,128)S(1)}, u32[]{:S(2)}, u32[]{:S(2)}) collective-permute-start(f32[3,64,128]{2,1,0:T(8,128)S(1)} %get-tuple-element.23.last.refs_4_), channel_id=1, source_target_pairs={{0,1},{2,3},{4,5},{6,7},{8,9},{10,11},{12,13},{14,15},{16,17},{18,... | collective-permute-start | bytes 294920 | tf_op jit(solution)/shard_map/ppermute | solution.py:653

commit v4 on v3

--- a/solution.py
+++ b/solution.py
@@ -87,7 +87,7 @@
             wide[s // (SUB // 2), :, s % (SUB // 2), s, :] = small.T
         return wide.reshape(planes * SUB, SUB * KX)
 
-    return np.concatenate([one(np.cos(angle)), one(np.sin(angle))], axis=0).astype(np.float32)
+    return np.concatenate([one(np.cos(angle)), one(np.sin(angle))], axis=0)
 
 
 def x_back_table(planes):
@@ -155,14 +155,8 @@
 
     n = (FOLD + 1) * SUB
     even, odd = [None] * (FOLD + 1), [None] * (FOLD + 1)
-    for m in range(chunks):
-        if m == 0:
-            for load in loads[:3]:
-                load.wait()
-            gain = column(factor[...])
-        elif m == 1:
-            for load in loads[5:]:
-                load.wait()
+
+    def along_z(m):
         scaled = held[m].astype(F32) * gain
         values[:, span * m : span * (m + 1)] = scaled.astype(BF16)
 
@@ -182,21 +176,31 @@
         high, low = split(
             jnp.concatenate([part[: SUB * QUARTER], part[SUB * QUARTER :]], axis=1)
         )
-        if m == 0:
-            for load in loads[3:5]:
-                load.wait()
+        return jnp.concatenate([low, high, high], axis=0)
+
+    def along_y(m, part):
         table = own_y[...]
         inner = table.shape[1] // 2
-        sums = dot(
-            jnp.concatenate([table[:, :inner], table], axis=1),
-            jnp.concatenate([low, high, high], axis=0),
-        )
+        sums = dot(jnp.concatenate([table[:, :inner], table], axis=1), part)
         for k in range(FOLD + 1):
             real = sums[SUB * k : SUB * (k + 1)]
             imag = sums[n + SUB * (k - 1) : n + SUB * k] if k else jnp.zeros_like(real)
             real, imag = quarters(real, imag, m * k)
             even[k] = real if even[k] is None else even[k] + real
             odd[k] = imag if odd[k] is None else odd[k] + imag
+
+    for load in loads[:3]:
+        load.wait()
+    gain = column(factor[...])
+    part = along_z(0)
+    for load in loads[3:5]:
+        load.wait()
+    along_y(0, part)
+    for load in loads[5:]:
+        load.wait()
+    parts = [along_z(m) for m in range(1, chunks)]
+    for m, part in enumerate(parts, 1):
+        along_y(m, part)
 
     first, second = jnp.concatenate(even, axis=0), jnp.concatenate(odd, axis=0)
     cosine = twice(tall(own_turns[0], 0, FOLD + 1))
@@ -244,13 +248,13 @@
         row = lax.broadcasted_iota(jnp.int32, (width, SUB * width), 0)
         lane = lax.broadcasted_iota(jnp.int32, (width, SUB * width), 1)
         spread_out = (lax.rem(lane, width) == row).astype(F32).astype(BF16)
-        block = dot(block.astype(BF16), spread_out)
+        block = dot(block, spread_out)
     else:
-        block = jnp.concatenate([block] * SUB, axis=1)
+        block = jnp.concatenate([block.astype(F32)] * SUB, axis=1)
     lane = lax.broadcasted_iota(jnp.int32, wide, 1)
     return jnp.concatenate(
         [
-            jnp.where((lane >= width * g) & (lane < width * (g + 1)), block, 0.0)
+            jnp.where((lane >= width * g) & (lane < width * (g + 1)), block, 0.0).astype(BF16)
             for g in range(SUB)
         ],
         axis=0,
@@ -281,20 +285,32 @@
     modes,
     mixed,
 ):
-    wide_bypass[...] = diagonal(bypass[...].astype(F32)).astype(BF16)
-    wide_in[...] = diagonal(0.5 * mlp_in_t[...].astype(F32).T).astype(BF16)
+    wide_bypass[...] = diagonal(bypass[...])
+    inner = 0.5 * mlp_in_t[...].astype(F32)
+    count = wide_out.shape[1]
+    wide_in[:count] = diagonal(inner.T.astype(BF16))
     heads = 0.5 * dot(decode[...], mlp_out[...])
-    heads = jnp.concatenate([diagonal(heads[k : k + 1]) for k in range(2)], axis=0)
-    wide_out[...] = jnp.concatenate(split(heads), axis=0)
-
-    highest = lax.Precision.HIGHEST
+    through = dot(heads, inner, ((1,), (1,)), precision=lax.Precision.HIGHEST)
+    def rows_of(x):
+        rows = [part[k : k + 1] for part in split(x) for k in range(2)]
+        return jnp.concatenate([diagonal(row).astype(F32) for row in rows], axis=0).astype(BF16)
+
+    wide_out[...] = rows_of(heads)
+    wide_in[count:] = rows_of(through)
+
     half = lines.shape[1] // 2
     count = half // (2 * TILES)
     groups = count // 4
     flipped = lines[...].T
     straight = jnp.concatenate([flipped[:half], flipped[half:]], axis=1)
     pair = jnp.concatenate([straight, -turned_by_i(straight, 0)], axis=1)
-    spectrum = dot(pair, table_x[...], precision=highest)
+    high, low = split(pair)
+    table = table_x[...]
+    inner = table.shape[0] // 2
+    spectrum = dot(
+        jnp.concatenate([low, high, high], axis=1),
+        jnp.concatenate([table[:inner], table], axis=0),
+    )
     for c in range(SUB // 4):
         for a in range(groups):
             got = swap_blocks(
@@ -339,7 +355,14 @@
                 for b in range(4):
                     parts[4 * a + b][c] = got[b]
         rows.append(jnp.concatenate([jnp.concatenate(p, axis=1) for p in parts], axis=0))
-    got = dot(table_back[...], jnp.concatenate(rows, axis=1), ((1,), (1,)), precision=highest)
+    high, low = split(jnp.concatenate(rows, axis=1))
+    table = table_back[...]
+    inner = table.shape[1] // 2
+    got = dot(
+        jnp.concatenate([table[:, :inner], table], axis=1),
+        jnp.concatenate([low, high, high], axis=1),
+        ((1,), (1,)),
+    )
     count = got.shape[0] // 2
     back[...] = jnp.concatenate([got[:count], got[count:]], axis=1)
 
@@ -426,8 +449,9 @@
         )
     )
     lifted = gelu_twice(spectral + dot(wide_bypass[...], own)).astype(BF16)
-    hidden = gelu_twice(dot(wide_in[...], lifted)).astype(BF16)
-    decoded = dot(wide_out[...], hidden)
+    inner = dot(wide_in[...], lifted)
+    count = wide_out.shape[1]
+    decoded = dot(wide_out[...], curved(inner[:count])) + inner[count:]
     decoded = decoded[: 2 * SUB] + decoded[2 * SUB :]
     even_plane = lax.axis_index("gx") % 2 == 0
     for a in range(rows // SUB):
@@ -454,6 +478,11 @@
     for k in range(ZONES):
         perm = jnp.where(zones == k, perm_table[k], perm)
     return perm
+
+
+def curved(x):
+    x = x.astype(BF16)
+    return x * jnp.tanh(x * (BF16(GELU_A) + BF16(GELU_B) * (x * x)))
 
 
 def joined(first, second):
@@ -590,7 +619,7 @@
         out_shape=[
             jax.ShapeDtypeStruct((planes * part, 2 * share), F32),
             jax.ShapeDtypeStruct((SUB * width, SUB * width), BF16),
-            jax.ShapeDtypeStruct((SUB * hidden, SUB * width), BF16),
+            jax.ShapeDtypeStruct((SUB * hidden + 4 * SUB, SUB * width), BF16),
             jax.ShapeDtypeStruct((4 * SUB, SUB * hidden), BF16),
         ],
         scratch_shapes=[
@@ -602,8 +631,8 @@
     )(
         lines,
         spec_weight,
-        jnp.asarray(x_forward_table(planes)),
-        jnp.asarray(x_back_table(planes)),
+        jnp.asarray(halves(x_forward_table(planes), 0)),
+        jnp.asarray(halves(x_back_table(planes), 1)),
         bypass_weight,
         mlp_in.T,
         mlp_out,

time: 51.9 us -> 50.4 us (0.971)
  Pallas kernels: 19.2 us -> 17.4 us
  waiting for transfers between devices: 1.96 us -> 2.55 us
    pallas_call x2, Pallas kernels: 10.4 us -> 8.88 us  [network(): pl.pallas_call(functools.partial(point_kernel, first=first), in_specs=[wh...]
    ppermute x1, waiting for transfers between devices: 1.95 us -> 2.54 us  [body(): lax.ppermute(last[1], 'gx', far)]
where the time goes in v4:
time: 50.4 us; the launch traced here: 50.3 us
  blocking collectives  23.3 us (46%)
  Pallas kernels  17.4 us (35%)
  starting transfers between devices  6.11 us (12%)
  waiting for transfers between devices  2.55 us (5%)
  between operations  0.85 us (2%)
    all_to_all x2, blocking collectives, body(): blocks = lax.all_to_all(blocks, 'gx', 0, 0, tiled=True)  23.3 us
    pallas_call x2, Pallas kernels, network(): pl.pallas_call(functools.partial(point_kernel, first=first), in_specs=[wh...  8.88 us
    pallas_call x1, Pallas kernels, body(): pl.pallas_call(forward_kernel, in_specs=[pl.BlockSpec(memory_space=pl.ANY...  4.28 us
    ppermute x1, starting transfers between devices, body(): lax.ppermute(last[1], 'gx', far)  3.63 us
    ppermute x1, waiting for transfers between devices, body(): lax.ppermute(last[1], 'gx', far)  2.54 us
    ppermute x1, starting transfers between devices, body(): lax.ppermute(first[1], 'gx', far)  2.34 us
    pallas_call x1, Pallas kernels, body(): pl.pallas_call(mix_kernel, in_specs=[whole()] * 8, out_specs=[whole()] *...  1.79 us
    pallas_call x1, Pallas kernels, body(): pl.pallas_call(inner_kernel, in_specs=[whole()] * 6 + [pl.BlockSpec(memor...  1.65 us
  transfers between devices with their start and end apart: 4, of which 1 were waited for; matrix products, arithmetic and copies ran while one was open for 0% of the time, Pallas kernels for 9%

profile of v4, /device:TPU:1, one launch (start us, length us, event | category | flops | bytes accessed | tf_op | source)
XLA Modules:
  0.0 50.3 jit_solution(6462862655612580696)
XLA Ops:
  0.6 0.0 copy-start.1
  0.6 0.0 copy-start.2
  0.7 0.0 copy-start.8
  0.7 0.0 copy-start.7
  0.7 0.0 copy-start.6
  0.7 0.0 copy-start.5
  0.7 0.0 copy-start
  0.7 0.0 copy-start.3
  0.7 0.0 copy-start.4
  0.7 0.0 copy-start.9
  0.7 0.0 copy-start.10
  0.8 0.0 copy-start.11
  0.8 4.3 %forward_yz.1 = (f32[128,128]{1,0:T(8,128)S(1)}, bf16[32,32768]{1,0:T(8,128)(2,1)S(1)}) custom-call(bf16[32,32768]{1,0:T(8,128)(2,1)} %bitcast.23, f32[1,32]{1,0:T(1,128)} %bitcast.25, bf16[256,256]{1,0:T(8,128)(2,1)} %constant.14.clone.table_z, bf16[264,1024]{1,0:T(8,128)(2,1)} %constant.15.clone.table_y, f32[2,17,128]{2,1,0:T(8,128)} %constant.16.clone.turns), custom_call_target="tpu_custom_call" | custom-call | tf_op jit(solution)/shard_map/forward_yz/pallas_call | solution.py:586
  5.1 14.2 %all_to_all.10 = f32[32,4,128]{2,1,0:T(4,128)S(1)} all-to-all(f32[32,4,128]{2,1,0:T(4,128)S(1)} %bitcast.21), channel_id=1, replica_groups=mesh['groups'=1,'gx'=32] {'gx'}, dimensions={0} | all-to-all | bytes 131072 | tf_op jit(solution)/shard_map/all_to_all | solution.py:610
  19.2 0.0 copy-done.1
  19.2 0.0 copy-done.2
  19.2 0.0 copy-done.8
  19.2 0.0 copy-done.7
  19.3 0.0 copy-done.6
  19.3 0.0 copy-done.5
  19.3 0.0 copy-done
  19.3 1.8 %mix_modes.1 = (f32[128,128]{1,0:T(8,128)S(1)}, bf16[256,256]{1,0:T(8,128)(2,1)S(1)}, bf16[1056,256]{1,0:T(8,128)(2,1)S(1)}, bf16[32,1024]{1,0:T(8,128)(2,1)S(1)}) custom-call(f32[128,128]{1,0:T(8,128)S(1)} %bitcast.14, bf16[2,32,32,256]{3,2,1,0:T(8,128)(2,1)S(1)} %copy-done, bf16[1024,256]{1,0:T(8,128)(2,1)S(1)} %copy-done.2, ...), custom_call_target="tpu_custom_call" | custom-call | tf_op jit(solution)/shard_map/mix_modes/pallas_call | solution.py:615
  21.1 9.1 %all_to_all.11 = f32[32,4,128]{2,1,0:T(4,128)S(1)} all-to-all(f32[32,4,128]{2,1,0:T(4,128)S(1)} %bitcast.20), channel_id=1, replica_groups=mesh['groups'=1,'gx'=32] {'gx'}, dimensions={0} | all-to-all | bytes 131072 | tf_op jit(solution)/shard_map/all_to_all | solution.py:643
  30.2 0.0 copy-done.3
  30.2 0.0 copy-done.4
  30.2 0.0 copy-done.9
  30.2 0.0 copy-done.10
  30.2 0.0 copy-done.11
  30.2 6.2 %point_network.2 = (f32[3,192,128]{2,1,0:T(8,128)S(1)}, f32[3,192,128]{2,1,0:T(8,128)S(1)}, f32[192,128]{1,0:T(8,128)S(1)}) custom-call(f32[128,128]{1,0:T(8,128)S(1)} %bitcast.18, bf16[32,32768]{1,0:T(8,128)(2,1)S(1)} %get-tuple-element.18.values, bf16[256,256]{1,0:T(8,128)(2,1)S(1)} %get-tuple-element.19.wide_bypass, ...), custom_call_target="tpu_custom_call" | custom-call | flops 9830400000 | bytes 4915200 | tf_op jit(solution)/shard_map/point_network/pallas_call | solution.py:653
  36.4 2.3 %collective-permute-start = (f32[3,192,128]{2,1,0:T(8,128)S(1)}, f32[3,192,128]{2,1,0:T(8,128)S(1)}, u32[]{:S(2)}, u32[]{:S(2)}) collective-permute-start(f32[3,192,128]{2,1,0:T(8,128)S(1)} %get-tuple-element.28.refs_1_), channel_id=1, source_target_pairs={{1,2},{3,4},{5,6},{7,8},{9,10},{11,12},{13,14},{15,16},{17,18},{19... | collective-permute-start | bytes 884744 | tf_op jit(solution)/shard_map/ppermute | solution.py:680
  38.8 0.1 collective-permute-start.1
  38.8 2.7 %point_network.3 = (f32[3,64,128]{2,1,0:T(8,128)S(1)}, f32[3,64,128]{2,1,0:T(8,128)S(1)}, f32[64,128]{1,0:T(8,128)S(1)}) custom-call(f32[128,128]{1,0:T(8,128)S(1)} %bitcast.19, bf16[32,32768]{1,0:T(8,128)(2,1)S(1)} %get-tuple-element.18.values, bf16[256,256]{1,0:T(8,128)(2,1)S(1)} %get-tuple-element.19.wide_bypass, ...), custom_call_target="tpu_custom_call" | custom-call | flops 3276800000 | bytes 1638400 | tf_op jit(solution)/shard_map/point_network/pallas_call | solution.py:653
  41.5 3.6 %collective-permute-start.2 = (f32[3,64,128]{2,1,0:T(8,128)S(1)}, f32[3,64,128]{2,1,0:T(8,128)S(1)}, u32[]{:S(2)}, u32[]{:S(2)}) collective-permute-start(f32[3,64,128]{2,1,0:T(8,128)S(1)} %get-tuple-element.29.refs_5_), channel_id=1, source_target_pairs={{1,2},{3,4},{5,6},{7,8},{9,10},{11,12},{13,14},{15,16},{17,18},{19... | collective-permute-start | bytes 294920 | tf_op jit(solution)/shard_map/ppermute | solution.py:682
  45.2 0.1 collective-permute-start.3
  45.3 1.6 %faces_in_plane.1 = (f32[2,256,128]{2,1,0:T(8,128)}, f32[256,128]{1,0:T(8,128)S(1)}) custom-call(f32[3,192,128]{2,1,0:T(8,128)S(1)} %get-tuple-element.22.first.refs_0_, f32[3,64,128]{2,1,0:T(8,128)S(1)} %get-tuple-element.23.last.refs_4_, f32[192,128]{1,0:T(8,128)S(1)} %get-tuple-element.24.first_filled, f32[64,128]{1,0:T(8,128)S(1)} %get-tuple-element.25.last_filled, ...), custom_call_target="tpu_custom_call" | custom-call | tf_op jit(solution)/shard_map/faces_in_plane/pallas_call | solution.py:683
  46.9 2.5 %collective-permute-done.2.refs_6_ = f32[3,64,128]{2,1,0:T(8,128)S(1)} collective-permute-done((f32[3,64,128]{2,1,0:T(8,128)S(1)}, f32[3,64,128]{2,1,0:T(8,128)S(1)}, u32[]{:S(2)}, u32[]{:S(2)}) %collective-permute-start.2) | collective-permute-done | bytes 98336 | tf_op jit(solution)/shard_map/ppermute | solution.py:682
  49.5 0.0 collective-permute-done.3.refs_7_
  49.5 0.0 collective-permute-done.refs_2_
  49.5 0.0 collective-permute-done.1.refs_3_
  49.5 0.8 %faces_between_planes.1 = f32[256,128]{1,0:T(8,128)} custom-call(f32[256,128]{1,0:T(8,128)S(1)} %get-tuple-element.27.partial, f32[3,192,128]{2,1,0:T(8,128)S(1)} %get-tuple-element.22.first.refs_0_, f32[3,192,128]{2,1,0:T(8,128)S(1)} %get-tuple-element.28.refs_1_, f32[3,192,128]{2,1,0:T(8,128)S(1)} %collective-permute-done.refs_2_, ...), custom_call_target="tpu_custom_call" | custom-call | tf_op jit(solution)/shard_map/faces_between_planes/pallas_call | solution.py:694
Async XLA Ops:
  0.6 18.6 %copy-start.1 = (bf16[256,1024]{1,0:T(8,128)(2,1)S(1)}, bf16[256,1024]{1,0:T(8,128)(2,1)}, u32[]{:S(2)}) copy-start(bf16[256,1024]{1,0:T(8,128)(2,1)} %constant.18.clone.table_back) | copy-start | bytes 1572868
  0.6 18.6 %copy-start.2 = (bf16[1024,256]{1,0:T(8,128)(2,1)S(1)}, bf16[1024,256]{1,0:T(8,128)(2,1)}, u32[]{:S(2)}) copy-start(bf16[1024,256]{1,0:T(8,128)(2,1)} %constant.17.clone.table_x) | copy-start | bytes 1572868
  0.7 18.6 %copy-start.8 = (bf16[2,32]{1,0:T(2,128)(2,1)S(1)}, bf16[2,32]{1,0:T(2,128)(2,1)}, u32[]{:S(2)}) copy-start(bf16[2,32]{1,0:T(2,128)(2,1)} %decode.1) | copy-start | bytes 388
  0.7 18.6 %copy-start.7 = (bf16[32,128]{1,0:T(8,128)(2,1)S(1)}, bf16[32,128]{1,0:T(8,128)(2,1)}, u32[]{:S(2)}) copy-start(bf16[32,128]{1,0:T(8,128)(2,1)} %mlp_out.1) | copy-start | bytes 24580
  0.7 18.6 %copy-start.6 = (bf16[128,32]{0,1:T(8,128)(2,1)S(1)}, bf16[128,32]{0,1:T(8,128)(2,1)}, u32[]{:S(2)}) copy-start(bf16[128,32]{0,1:T(8,128)(2,1)} %param.22) | copy-start | bytes 24580
  0.7 18.6 %copy-start.5 = (bf16[32,32]{1,0:T(8,128)(2,1)S(1)}, bf16[32,32]{1,0:T(8,128)(2,1)}, u32[]{:S(2)}) copy-start(bf16[32,32]{1,0:T(8,128)(2,1)} %bypass.1) | copy-start | bytes 6148
  0.7 18.6 %copy-start = (bf16[2,32,32,256]{3,2,1,0:T(8,128)(2,1)S(1)}, bf16[2,32,32,256]{3,2,1,0:T(8,128)(2,1)}, u32[]{:S(2)}) copy-start(bf16[2,32,32,256]{3,2,1,0:T(8,128)(2,1)} %weight.1) | copy-start | bytes 3145732
  0.7 29.5 %copy-start.3 = (s32[3,1,32768]{2,1,0:T(1,128)S(1)}, s32[3,1,32768]{2,1,0:T(1,128)}, u32[]{:S(2)}) copy-start(s32[3,1,32768]{2,1,0:T(1,128)} %param.26) | copy-start | bytes 1179652
  0.7 29.5 %copy-start.4 = (s32[1,32768]{1,0:T(1,128)S(1)}, s32[1,32768]{1,0:T(1,128)}, u32[]{:S(2)}) copy-start(s32[1,32768]{1,0:T(1,128)} %param.25) | copy-start | bytes 393220
  0.7 29.5 %copy-start.9 = (f32[8]{0:T(128)S(1)}, f32[8]{0:T(128)}, u32[]{:S(2)}) copy-start(f32[8]{0:T(128)} %perm_table.5) | copy-start | bytes 100
  0.7 29.5 %copy-start.10 = (bf16[768,512]{1,0:T(8,128)(2,1)S(1)}, bf16[768,512]{1,0:T(8,128)(2,1)}, u32[]{:S(2)}) copy-start(bf16[768,512]{1,0:T(8,128)(2,1)} %constant.19.clone.tables) | copy-start | bytes 2359300
  0.8 29.5 %copy-start.11 = (f32[2,32,128]{2,1,0:T(8,128)S(1)}, f32[2,32,128]{2,1,0:T(8,128)}, u32[]{:S(2)}) copy-start(f32[2,32,128]{2,1,0:T(8,128)} %constant.20.clone.turns) | copy-start | bytes 98308
  36.4 13.1 %collective-permute-start = (f32[3,192,128]{2,1,0:T(8,128)S(1)}, f32[3,192,128]{2,1,0:T(8,128)S(1)}, u32[]{:S(2)}, u32[]{:S(2)}) collective-permute-start(f32[3,192,128]{2,1,0:T(8,128)S(1)} %get-tuple-element.28.refs_1_), channel_id=1, source_target_pairs={{1,2},{3,4},{5,6},{7,8},{9,10},{11,12},{13,14},{15,16},{17,18},{19... | collective-permute-start | bytes 884744 | tf_op jit(solution)/shard_map/ppermute | solution.py:680
  38.8 10.7 %collective-permute-start.1 = (f32[3,192,128]{2,1,0:T(8,128)S(1)}, f32[3,192,128]{2,1,0:T(8,128)S(1)}, u32[]{:S(2)}, u32[]{:S(2)}) collective-permute-start(f32[3,192,128]{2,1,0:T(8,128)S(1)} %get-tuple-element.22.first.refs_0_), channel_id=1, source_target_pairs={{0,1},{2,3},{4,5},{6,7},{8,9},{10,11},{12,13},{14,15},{16,17},{18,... | collective-permute-start | bytes 884744 | tf_op jit(solution)/shard_map/ppermute | solution.py:680
  41.5 7.9 %collective-permute-start.2 = (f32[3,64,128]{2,1,0:T(8,128)S(1)}, f32[3,64,128]{2,1,0:T(8,128)S(1)}, u32[]{:S(2)}, u32[]{:S(2)}) collective-permute-start(f32[3,64,128]{2,1,0:T(8,128)S(1)} %get-tuple-element.29.refs_5_), channel_id=1, source_target_pairs={{1,2},{3,4},{5,6},{7,8},{9,10},{11,12},{13,14},{15,16},{17,18},{19... | collective-permute-start | bytes 294920 | tf_op jit(solution)/shard_map/ppermute | solution.py:682
  45.2 4.3 %collective-permute-start.3 = (f32[3,64,128]{2,1,0:T(8,128)S(1)}, f32[3,64,128]{2,1,0:T(8,128)S(1)}, u32[]{:S(2)}, u32[]{:S(2)}) collective-permute-start(f32[3,64,128]{2,1,0:T(8,128)S(1)} %get-tuple-element.23.last.refs_4_), channel_id=1, source_target_pairs={{0,1},{2,3},{4,5},{6,7},{8,9},{10,11},{12,13},{14,15},{16,17},{18,... | collective-permute-start | bytes 294920 | tf_op jit(solution)/shard_map/ppermute | solution.py:682

commit v5 on v4

--- a/solution.py
+++ b/solution.py
@@ -25,6 +25,11 @@
 HALF = KZ * 2 * TILES
 QUARTER = ROWS // 4
 FOLD = KY // 2
+CLASSES = (
+    list(range(1, FOLD + 1, 2)),
+    list(range(0, FOLD + 1, 4)),
+    list(range(2, FOLD + 1, 4)),
+)
 GELU_A = math.sqrt(2.0 / math.pi)
 GELU_B = GELU_A * 0.044715
 F32 = jnp.float32
@@ -64,7 +69,10 @@
 
 def y_forward_table():
     angle = angles(np.arange(FOLD + 1), np.arange(QUARTER) * PAIRS, NY)
-    return halves(np.concatenate([spread(np.cos(angle)), spread(np.sin(angle[1:]))], axis=0), 1)
+    parts = []
+    for group in CLASSES:
+        parts += [np.cos(angle[group]), np.sin(angle[[k for k in group if k]])]
+    return halves(spread(np.concatenate(parts, axis=0)), 1)
 
 
 def turn_forward_table():
@@ -146,16 +154,13 @@
 ):
     span = QUARTER * LANES
     chunks = features.shape[1] // span
-    loads = [(scale, factor), (features.at[:, :span], held.at[0]), (table_z, own_z)]
-    loads += [(table_y, own_y), (turns, own_turns)]
-    loads += [(features.at[:, span * m : span * (m + 1)], held.at[m]) for m in range(1, chunks)]
+    loads = [(scale, factor), (table_z, own_z), (table_y, own_y), (turns, own_turns)]
+    loads += [(features.at[:, span * m : span * (m + 1)], held.at[m]) for m in range(chunks)]
     loads = [pltpu.make_async_copy(*pair, done.at[k]) for k, pair in enumerate(loads)]
     for load in loads:
         load.start()
 
     n = (FOLD + 1) * SUB
-    even, odd = [None] * (FOLD + 1), [None] * (FOLD + 1)
-
     def along_z(m):
         scaled = held[m].astype(F32) * gain
         values[:, span * m : span * (m + 1)] = scaled.astype(BF16)
@@ -173,34 +178,40 @@
         ).astype(BF16)
         part = dot(cells, own_z[...])
         part = part[:, :LANES] + part[:, LANES:]
-        high, low = split(
-            jnp.concatenate([part[: SUB * QUARTER], part[SUB * QUARTER :]], axis=1)
+        return jnp.concatenate([part[: SUB * QUARTER], part[SUB * QUARTER :]], axis=1)
+
+    def along_y(place, group, x):
+        table = own_y[SUB * place : SUB * (place + 2 * len(group) - (0 in group))]
+        inner = table.shape[1] // 2
+        high, low = split(x)
+        sums = dot(
+            jnp.concatenate([table[:, :inner], table], axis=1),
+            jnp.concatenate([low, high, high], axis=0),
         )
-        return jnp.concatenate([low, high, high], axis=0)
-
-    def along_y(m, part):
-        table = own_y[...]
-        inner = table.shape[1] // 2
-        sums = dot(jnp.concatenate([table[:, :inner], table], axis=1), part)
-        for k in range(FOLD + 1):
-            real = sums[SUB * k : SUB * (k + 1)]
-            imag = sums[n + SUB * (k - 1) : n + SUB * k] if k else jnp.zeros_like(real)
-            real, imag = quarters(real, imag, m * k)
-            even[k] = real if even[k] is None else even[k] + real
-            odd[k] = imag if odd[k] is None else odd[k] + imag
-
-    for load in loads[:3]:
+        tiles = [sums[SUB * k : SUB * (k + 1)] for k in range(sums.shape[0] // SUB)]
+        cosines, sines = tiles[: len(group)], tiles[len(group) :]
+        return cosines, ([jnp.zeros_like(tiles[0])] if 0 in group else []) + sines
+
+    for load in loads:
         load.wait()
     gain = column(factor[...])
-    part = along_z(0)
-    for load in loads[3:5]:
-        load.wait()
-    along_y(0, part)
-    for load in loads[5:]:
-        load.wait()
-    parts = [along_z(m) for m in range(1, chunks)]
-    for m, part in enumerate(parts, 1):
-        along_y(m, part)
+    q = [along_z(m) for m in range(chunks)]
+    sums, differences = [q[0] + q[2], q[1] + q[3]], [q[0] - q[2], q[1] - q[3]]
+    even, odd = [None] * (FOLD + 1), [None] * (FOLD + 1)
+    place = 0
+    for group in CLASSES:
+        if group[0] % 2:
+            cosines, sines = along_y(place, group, jnp.concatenate(differences, axis=1))
+            half = cosines[0].shape[1] // 2
+            for k, c, s in zip(group, cosines, sines):
+                sign = 1.0 if k % 4 == 1 else -1.0
+                even[k] = c[:, :half] - sign * s[:, half:]
+                odd[k] = s[:, :half] + sign * c[:, half:]
+        else:
+            x = sums[0] + sums[1] if group[0] % 4 == 0 else sums[0] - sums[1]
+            for k, c, s in zip(group, *along_y(place, group, x)):
+                even[k], odd[k] = c, s
+        place += 2 * len(group) - (0 in group)
 
     first, second = jnp.concatenate(even, axis=0), jnp.concatenate(odd, axis=0)
     cosine = twice(tall(own_turns[0], 0, FOLD + 1))

time: 50.4 us -> 49.8 us (0.988)
  Pallas kernels: 17.4 us -> 16.8 us
    pallas_call x1, Pallas kernels: 4.28 us -> 3.65 us  [body(): pl.pallas_call(forward_kernel, in_specs=[pl.BlockSpec(memory_space=pl.ANY...]
where the time goes in v5:
time: 49.8 us; the launch traced here: 49.6 us
  blocking collectives  23.3 us (47%)
  Pallas kernels  16.8 us (34%)
  starting transfers between devices  6.11 us (12%)
  waiting for transfers between devices  2.55 us (5%)
  between operations  0.85 us (2%)
    all_to_all x2, blocking collectives, body(): blocks = lax.all_to_all(blocks, 'gx', 0, 0, tiled=True)  23.3 us
    pallas_call x2, Pallas kernels, network(): pl.pallas_call(functools.partial(point_kernel, first=first), in_specs=[wh...  8.89 us
    pallas_call x1, Pallas kernels, body(): pl.pallas_call(forward_kernel, in_specs=[pl.BlockSpec(memory_space=pl.ANY...  3.65 us
    ppermute x1, starting transfers between devices, body(): lax.ppermute(last[1], 'gx', far)  3.63 us
    ppermute x1, waiting for transfers between devices, body(): lax.ppermute(last[1], 'gx', far)  2.54 us
    ppermute x1, starting transfers between devices, body(): lax.ppermute(first[1], 'gx', far)  2.34 us
    pallas_call x1, Pallas kernels, body(): pl.pallas_call(mix_kernel, in_specs=[whole()] * 8, out_specs=[whole()] *...  1.79 us
    pallas_call x1, Pallas kernels, body(): pl.pallas_call(inner_kernel, in_specs=[whole()] * 6 + [pl.BlockSpec(memor...  1.65 us
  transfers between devices with their start and end apart: 4, of which 1 were waited for; matrix products, arithmetic and copies ran while one was open for 0% of the time, Pallas kernels for 9%

profile of v5, /device:TPU:1, one launch (start us, length us, event | category | flops | bytes accessed | tf_op | source)
XLA Modules:
  0.0 49.6 jit_solution(3716211958187208133)
XLA Ops:
  0.6 0.0 copy-start.1
  0.6 0.0 copy-start.2
  0.7 0.0 copy-start.8
  0.7 0.0 copy-start.7
  0.7 0.0 copy-start.6
  0.7 0.0 copy-start.5
  0.7 0.0 copy-start
  0.7 0.0 copy-start.3
  0.7 0.0 copy-start.4
  0.7 0.0 copy-start.9
  0.7 0.0 copy-start.10
  0.8 0.0 copy-start.11
  0.8 3.6 %forward_yz.1 = (f32[128,128]{1,0:T(8,128)S(1)}, bf16[32,32768]{1,0:T(8,128)(2,1)S(1)}) custom-call(bf16[32,32768]{1,0:T(8,128)(2,1)} %bitcast.23, f32[1,32]{1,0:T(1,128)} %bitcast.25, bf16[256,256]{1,0:T(8,128)(2,1)} %constant.14.clone.table_z, bf16[264,1024]{1,0:T(8,128)(2,1)} %constant.15.clone.table_y, f32[2,17,128]{2,1,0:T(8,128)} %constant.16.clone.turns), custom_call_target="tpu_custom_call" | custom-call | tf_op jit(solution)/shard_map/forward_yz/pallas_call | solution.py:597
  4.4 14.2 %all_to_all.10 = f32[32,4,128]{2,1,0:T(4,128)S(1)} all-to-all(f32[32,4,128]{2,1,0:T(4,128)S(1)} %bitcast.21), channel_id=1, replica_groups=mesh['groups'=1,'gx'=32] {'gx'}, dimensions={0} | all-to-all | bytes 131072 | tf_op jit(solution)/shard_map/all_to_all | solution.py:621
  18.6 0.0 copy-done.1
  18.6 0.0 copy-done.2
  18.6 0.0 copy-done.8
  18.6 0.0 copy-done.7
  18.6 0.0 copy-done.6
  18.6 0.0 copy-done.5
  18.6 0.0 copy-done
  18.6 1.8 %mix_modes.1 = (f32[128,128]{1,0:T(8,128)S(1)}, bf16[256,256]{1,0:T(8,128)(2,1)S(1)}, bf16[1056,256]{1,0:T(8,128)(2,1)S(1)}, bf16[32,1024]{1,0:T(8,128)(2,1)S(1)}) custom-call(f32[128,128]{1,0:T(8,128)S(1)} %bitcast.14, bf16[2,32,32,256]{3,2,1,0:T(8,128)(2,1)S(1)} %copy-done, bf16[1024,256]{1,0:T(8,128)(2,1)S(1)} %copy-done.2, ...), custom_call_target="tpu_custom_call" | custom-call | tf_op jit(solution)/shard_map/mix_modes/pallas_call | solution.py:626
  20.4 9.1 %all_to_all.11 = f32[32,4,128]{2,1,0:T(4,128)S(1)} all-to-all(f32[32,4,128]{2,1,0:T(4,128)S(1)} %bitcast.20), channel_id=1, replica_groups=mesh['groups'=1,'gx'=32] {'gx'}, dimensions={0} | all-to-all | bytes 131072 | tf_op jit(solution)/shard_map/all_to_all | solution.py:654
  29.6 0.0 copy-done.3
  29.6 0.0 copy-done.4
  29.6 0.0 copy-done.9
  29.6 0.0 copy-done.10
  29.6 0.0 copy-done.11
  29.6 6.2 %point_network.2 = (f32[3,192,128]{2,1,0:T(8,128)S(1)}, f32[3,192,128]{2,1,0:T(8,128)S(1)}, f32[192,128]{1,0:T(8,128)S(1)}) custom-call(f32[128,128]{1,0:T(8,128)S(1)} %bitcast.18, bf16[32,32768]{1,0:T(8,128)(2,1)S(1)} %get-tuple-element.18.values, bf16[256,256]{1,0:T(8,128)(2,1)S(1)} %get-tuple-element.19.wide_bypass, ...), custom_call_target="tpu_custom_call" | custom-call | flops 9830400000 | bytes 4915200 | tf_op jit(solution)/shard_map/point_network/pallas_call | solution.py:664
  35.8 2.3 %collective-permute-start = (f32[3,192,128]{2,1,0:T(8,128)S(1)}, f32[3,192,128]{2,1,0:T(8,128)S(1)}, u32[]{:S(2)}, u32[]{:S(2)}) collective-permute-start(f32[3,192,128]{2,1,0:T(8,128)S(1)} %get-tuple-element.28.refs_1_), channel_id=1, source_target_pairs={{1,2},{3,4},{5,6},{7,8},{9,10},{11,12},{13,14},{15,16},{17,18},{19... | collective-permute-start | bytes 884744 | tf_op jit(solution)/shard_map/ppermute | solution.py:691
  38.1 0.1 collective-permute-start.1
  38.2 2.7 %point_network.3 = (f32[3,64,128]{2,1,0:T(8,128)S(1)}, f32[3,64,128]{2,1,0:T(8,128)S(1)}, f32[64,128]{1,0:T(8,128)S(1)}) custom-call(f32[128,128]{1,0:T(8,128)S(1)} %bitcast.19, bf16[32,32768]{1,0:T(8,128)(2,1)S(1)} %get-tuple-element.18.values, bf16[256,256]{1,0:T(8,128)(2,1)S(1)} %get-tuple-element.19.wide_bypass, ...), custom_call_target="tpu_custom_call" | custom-call | flops 3276800000 | bytes 1638400 | tf_op jit(solution)/shard_map/point_network/pallas_call | solution.py:664
  40.9 3.6 %collective-permute-start.2 = (f32[3,64,128]{2,1,0:T(8,128)S(1)}, f32[3,64,128]{2,1,0:T(8,128)S(1)}, u32[]{:S(2)}, u32[]{:S(2)}) collective-permute-start(f32[3,64,128]{2,1,0:T(8,128)S(1)} %get-tuple-element.29.refs_5_), channel_id=1, source_target_pairs={{1,2},{3,4},{5,6},{7,8},{9,10},{11,12},{13,14},{15,16},{17,18},{19... | collective-permute-start | bytes 294920 | tf_op jit(solution)/shard_map/ppermute | solution.py:693
  44.5 0.1 collective-permute-start.3
  44.6 1.6 %faces_in_plane.1 = (f32[2,256,128]{2,1,0:T(8,128)}, f32[256,128]{1,0:T(8,128)S(1)}) custom-call(f32[3,192,128]{2,1,0:T(8,128)S(1)} %get-tuple-element.22.first.refs_0_, f32[3,64,128]{2,1,0:T(8,128)S(1)} %get-tuple-element.23.last.refs_4_, f32[192,128]{1,0:T(8,128)S(1)} %get-tuple-element.24.first_filled, f32[64,128]{1,0:T(8,128)S(1)} %get-tuple-element.25.last_filled, ...), custom_call_target="tpu_custom_call" | custom-call | tf_op jit(solution)/shard_map/faces_in_plane/pallas_call | solution.py:694
  46.3 2.5 %collective-permute-done.2.refs_6_ = f32[3,64,128]{2,1,0:T(8,128)S(1)} collective-permute-done((f32[3,64,128]{2,1,0:T(8,128)S(1)}, f32[3,64,128]{2,1,0:T(8,128)S(1)}, u32[]{:S(2)}, u32[]{:S(2)}) %collective-permute-start.2) | collective-permute-done | bytes 98336 | tf_op jit(solution)/shard_map/ppermute | solution.py:693
  48.8 0.0 collective-permute-done.3.refs_7_
  48.8 0.0 collective-permute-done.refs_2_
  48.8 0.0 collective-permute-done.1.refs_3_
  48.8 0.8 %faces_between_planes.1 = f32[256,128]{1,0:T(8,128)} custom-call(f32[256,128]{1,0:T(8,128)S(1)} %get-tuple-element.27.partial, f32[3,192,128]{2,1,0:T(8,128)S(1)} %get-tuple-element.22.first.refs_0_, f32[3,192,128]{2,1,0:T(8,128)S(1)} %get-tuple-element.28.refs_1_, f32[3,192,128]{2,1,0:T(8,128)S(1)} %collective-permute-done.refs_2_, ...), custom_call_target="tpu_custom_call" | custom-call | tf_op jit(solution)/shard_map/faces_between_planes/pallas_call | solution.py:705
Async XLA Ops:
  0.6 18.0 %copy-start.1 = (bf16[256,1024]{1,0:T(8,128)(2,1)S(1)}, bf16[256,1024]{1,0:T(8,128)(2,1)}, u32[]{:S(2)}) copy-start(bf16[256,1024]{1,0:T(8,128)(2,1)} %constant.18.clone.table_back) | copy-start | bytes 1572868
  0.6 18.0 %copy-start.2 = (bf16[1024,256]{1,0:T(8,128)(2,1)S(1)}, bf16[1024,256]{1,0:T(8,128)(2,1)}, u32[]{:S(2)}) copy-start(bf16[1024,256]{1,0:T(8,128)(2,1)} %constant.17.clone.table_x) | copy-start | bytes 1572868
  0.7 17.9 %copy-start.8 = (bf16[2,32]{1,0:T(2,128)(2,1)S(1)}, bf16[2,32]{1,0:T(2,128)(2,1)}, u32[]{:S(2)}) copy-start(bf16[2,32]{1,0:T(2,128)(2,1)} %decode.1) | copy-start | bytes 388
  0.7 17.9 %copy-start.7 = (bf16[32,128]{1,0:T(8,128)(2,1)S(1)}, bf16[32,128]{1,0:T(8,128)(2,1)}, u32[]{:S(2)}) copy-start(bf16[32,128]{1,0:T(8,128)(2,1)} %mlp_out.1) | copy-start | bytes 24580
  0.7 17.9 %copy-start.6 = (bf16[128,32]{0,1:T(8,128)(2,1)S(1)}, bf16[128,32]{0,1:T(8,128)(2,1)}, u32[]{:S(2)}) copy-start(bf16[128,32]{0,1:T(8,128)(2,1)} %param.22) | copy-start | bytes 24580
  0.7 17.9 %copy-start.5 = (bf16[32,32]{1,0:T(8,128)(2,1)S(1)}, bf16[32,32]{1,0:T(8,128)(2,1)}, u32[]{:S(2)}) copy-start(bf16[32,32]{1,0:T(8,128)(2,1)} %bypass.1) | copy-start | bytes 6148
  0.7 17.9 %copy-start = (bf16[2,32,32,256]{3,2,1,0:T(8,128)(2,1)S(1)}, bf16[2,32,32,256]{3,2,1,0:T(8,128)(2,1)}, u32[]{:S(2)}) copy-start(bf16[2,32,32,256]{3,2,1,0:T(8,128)(2,1)} %weight.1) | copy-start | bytes 3145732
  0.7 28.8 %copy-start.3 = (s32[3,1,32768]{2,1,0:T(1,128)S(1)}, s32[3,1,32768]{2,1,0:T(1,128)}, u32[]{:S(2)}) copy-start(s32[3,1,32768]{2,1,0:T(1,128)} %param.26) | copy-start | bytes 1179652
  0.7 28.8 %copy-start.4 = (s32[1,32768]{1,0:T(1,128)S(1)}, s32[1,32768]{1,0:T(1,128)}, u32[]{:S(2)}) copy-start(s32[1,32768]{1,0:T(1,128)} %param.25) | copy-start | bytes 393220
  0.7 28.8 %copy-start.9 = (f32[8]{0:T(128)S(1)}, f32[8]{0:T(128)}, u32[]{:S(2)}) copy-start(f32[8]{0:T(128)} %perm_table.5) | copy-start | bytes 100
  0.7 28.8 %copy-start.10 = (bf16[768,512]{1,0:T(8,128)(2,1)S(1)}, bf16[768,512]{1,0:T(8,128)(2,1)}, u32[]{:S(2)}) copy-start(bf16[768,512]{1,0:T(8,128)(2,1)} %constant.19.clone.tables) | copy-start | bytes 2359300
  0.8 28.8 %copy-start.11 = (f32[2,32,128]{2,1,0:T(8,128)S(1)}, f32[2,32,128]{2,1,0:T(8,128)}, u32[]{:S(2)}) copy-start(f32[2,32,128]{2,1,0:T(8,128)} %constant.20.clone.turns) | copy-start | bytes 98308
  35.8 13.0 %collective-permute-start = (f32[3,192,128]{2,1,0:T(8,128)S(1)}, f32[3,192,128]{2,1,0:T(8,128)S(1)}, u32[]{:S(2)}, u32[]{:S(2)}) collective-permute-start(f32[3,192,128]{2,1,0:T(8,128)S(1)} %get-tuple-element.28.refs_1_), channel_id=1, source_target_pairs={{1,2},{3,4},{5,6},{7,8},{9,10},{11,12},{13,14},{15,16},{17,18},{19... | collective-permute-start | bytes 884744 | tf_op jit(solution)/shard_map/ppermute | solution.py:691
  38.1 10.7 %collective-permute-start.1 = (f32[3,192,128]{2,1,0:T(8,128)S(1)}, f32[3,192,128]{2,1,0:T(8,128)S(1)}, u32[]{:S(2)}, u32[]{:S(2)}) collective-permute-start(f32[3,192,128]{2,1,0:T(8,128)S(1)} %get-tuple-element.22.first.refs_0_), channel_id=1, source_target_pairs={{0,1},{2,3},{4,5},{6,7},{8,9},{10,11},{12,13},{14,15},{16,17},{18,... | collective-permute-start | bytes 884744 | tf_op jit(solution)/shard_map/ppermute | solution.py:691
  40.9 7.9 %collective-permute-start.2 = (f32[3,64,128]{2,1,0:T(8,128)S(1)}, f32[3,64,128]{2,1,0:T(8,128)S(1)}, u32[]{:S(2)}, u32[]{:S(2)}) collective-permute-start(f32[3,64,128]{2,1,0:T(8,128)S(1)} %get-tuple-element.29.refs_5_), channel_id=1, source_target_pairs={{1,2},{3,4},{5,6},{7,8},{9,10},{11,12},{13,14},{15,16},{17,18},{19... | collective-permute-start | bytes 294920 | tf_op jit(solution)/shard_map/ppermute | solution.py:693
  44.5 4.3 %collective-permute-start.3 = (f32[3,64,128]{2,1,0:T(8,128)S(1)}, f32[3,64,128]{2,1,0:T(8,128)S(1)}, u32[]{:S(2)}, u32[]{:S(2)}) collective-permute-start(f32[3,64,128]{2,1,0:T(8,128)S(1)} %get-tuple-element.23.last.refs_4_), channel_id=1, source_target_pairs={{0,1},{2,3},{4,5},{6,7},{8,9},{10,11},{12,13},{14,15},{16,17},{18,... | collective-permute-start | bytes 294920 | tf_op jit(solution)/shard_map/ppermute | solution.py:693

commit v6 on v5

--- a/solution.py
+++ b/solution.py
@@ -30,6 +30,7 @@
     list(range(0, FOLD + 1, 4)),
     list(range(2, FOLD + 1, 4)),
 )
+EVENS, ODDS = list(range(2, FOLD + 1, 2)), list(range(1, FOLD + 1, 2))
 GELU_A = math.sqrt(2.0 / math.pi)
 GELU_B = GELU_A * 0.044715
 F32 = jnp.float32
@@ -104,19 +105,27 @@
 
 
 def y_back_table():
-    angle = angles(np.arange(1, FOLD + 1), np.arange(QUARTER) * PAIRS, NY)
-    return halves(np.concatenate([spread(np.cos(angle).T), spread(np.sin(angle).T)], axis=1), 1)
+    sides = []
+    for freqs in (EVENS, ODDS):
+        angle = angles(np.array(freqs), np.arange(QUARTER) * PAIRS, NY)
+        sides.append(halves(spread(np.concatenate([np.cos(angle).T, np.sin(angle).T], axis=1)), 1))
+    return np.concatenate(sides, axis=1)
 
 
 def z_back_table(total):
     angle = angles(np.arange(KZ), np.arange(NZ), NZ)
     weight = np.where(np.arange(KZ) == 0, 1.0, 2.0)[:, None] / total
-    table = np.zeros((PAIRS, KZ, TILES // TWO, 2, TWO, TILES, PAIRS, NZ))
-    for t in range(TILES):
+    table = np.zeros((PAIRS, KZ, TILES // TWO, 2, TWO, TWO, PAIRS, NZ))
+    for t in range(TWO):
         for p in range(PAIRS):
-            table[p, :, t // TWO, 0, t % TWO, t, p, :] = weight * np.cos(angle)
-            table[p, :, t // TWO, 1, t % TWO, t, p, :] = -weight * np.sin(angle)
-    return halves(table.reshape(PAIRS * HALF, TILES * LANES), 0)
+            table[p, :, :, 0, t, t, p, :] = (weight * np.cos(angle))[:, None]
+            table[p, :, :, 1, t, t, p, :] = (-weight * np.sin(angle))[:, None]
+    high, low = np.split(halves(table, 0), 2)
+    blocks = [high, low.copy(), low.copy(), np.zeros_like(low)]
+    blocks[1][:, :, 1] = 0
+    blocks[2][:, :, 0] = 0
+    blocks = [block.reshape(LANES, TWO * LANES) for block in blocks]
+    return np.concatenate([np.concatenate(blocks[k : k + 2], axis=1) for k in (0, 2)], axis=0)
 
 
 def dot(a, b, dims=((1,), (0,)), precision=None):
@@ -424,19 +433,36 @@
     odd.append(-at(turned, FOLD))
     level = jnp.concatenate([at(straight, 0)] * QUARTER, axis=0)
     count = QUARTER * SUB
-    table = jnp.concatenate([tables[count : count + LANES], tables[count:]], axis=0)
-    for m in range(rows // QUARTER):
-        sides = [
-            quarters(real, -imag, (first // QUARTER + m) * k)
-            for k, (real, imag) in enumerate(zip(even, odd), 1)
-        ]
+    quarter = first // QUARTER
+
+    def along_y(freqs, place, turns_of):
+        sides = [quarters(even[k - 1], -odd[k - 1], turns_of * k) for k in freqs]
         sides = [real for real, _ in sides] + [-imag for _, imag in sides]
         sides = jnp.concatenate(split(jnp.concatenate(sides, axis=0)), axis=1)
-        both = dot(tables[:count], jnp.concatenate([sides, sides], axis=0))
-        high, low = split(both[:, :LANES] + both[:, LANES:] + level)
-        smooth[QUARTER * SUB * m : QUARTER * SUB * (m + 1)] = dot(
-            jnp.concatenate([low, high, high], axis=1), table
-        )
+        both = dot(tables[:count, place : place + 2 * LANES], jnp.concatenate([sides] * 2, axis=0))
+        return both[:, :LANES] + both[:, LANES:]
+
+    wanted = sorted({(quarter + m) % 2 for m in range(rows // QUARTER)})
+    even_sums = {m: along_y(EVENS, 0, m) + level for m in wanted}
+    odd_sums = {m: along_y(ODDS, 2 * LANES, m) for m in wanted}
+    high_table = tables[count : count + LANES, : 2 * LANES]
+    low_tables = tables[count : count + LANES, 2 * LANES :], tables[count + LANES :, : 2 * LANES]
+    lane = lax.broadcasted_iota(jnp.int32, (count, LANES), 1)
+    second_pair = (lane & (2 * TWO)) != 0
+    for m in range(rows // QUARTER):
+        side = (quarter + m) % 2
+        minus = (quarter + m) // 2 % 2
+        gained = even_sums[side] - odd_sums[side] if minus else even_sums[side] + odd_sums[side]
+        high = gained.astype(BF16)
+        rounded = high.astype(F32)
+        rest = gained - rounded
+        for k, shift in enumerate((2 * TWO, LANES - 2 * TWO)):
+            moved = pltpu.roll(rest, shift, 1)
+            own = jnp.where(second_pair, *((rounded, moved) if k else (moved, rounded)))
+            smooth[count * m : count * (m + 1), 2 * LANES * k : 2 * LANES * (k + 1)] = dot(
+                jnp.concatenate([own.astype(BF16), high], axis=1),
+                jnp.concatenate([high_table, low_tables[k]], axis=0),
+            )
 
     groups = rows // SUB
 

time: 49.8 us -> 49.3 us (0.990)
  Pallas kernels: 16.8 us -> 16.1 us
    pallas_call x2, Pallas kernels: 8.89 us -> 8.26 us  [network(): pl.pallas_call(functools.partial(point_kernel, first=first), in_specs=[wh...]
where the time goes in v6:
time: 49.3 us; the launch traced here: 49.1 us
  blocking collectives  23.3 us (47%)
  Pallas kernels  16.1 us (33%)
  starting transfers between devices  6.13 us (12%)
  waiting for transfers between devices  2.62 us (5%)
  between operations  0.85 us (2%)
    all_to_all x2, blocking collectives, body(): blocks = lax.all_to_all(blocks, 'gx', 0, 0, tiled=True)  23.3 us
    pallas_call x2, Pallas kernels, network(): pl.pallas_call(functools.partial(point_kernel, first=first), in_specs=[wh...  8.26 us
    pallas_call x1, Pallas kernels, body(): pl.pallas_call(forward_kernel, in_specs=[pl.BlockSpec(memory_space=pl.ANY...  3.65 us
    ppermute x1, starting transfers between devices, body(): lax.ppermute(last[1], 'gx', far)  3.64 us
    ppermute x1, waiting for transfers between devices, body(): lax.ppermute(last[1], 'gx', far)  2.62 us
    ppermute x1, starting transfers between devices, body(): lax.ppermute(first[1], 'gx', far)  2.35 us
    pallas_call x1, Pallas kernels, body(): pl.pallas_call(mix_kernel, in_specs=[whole()] * 8, out_specs=[whole()] *...  1.79 us
    pallas_call x1, Pallas kernels, body(): pl.pallas_call(inner_kernel, in_specs=[whole()] * 6 + [pl.BlockSpec(memor...  1.65 us
  transfers between devices with their start and end apart: 4, of which 1 were waited for; matrix products, arithmetic and copies ran while one was open for 0% of the time, Pallas kernels for 9%

profile of v6, /device:TPU:1, one launch (start us, length us, event | category | flops | bytes accessed | tf_op | source)
XLA Modules:
  0.0 49.1 jit_solution(1395272876823715467)
XLA Ops:
  0.6 0.0 copy-start.1
  0.6 0.0 copy-start.2
  0.7 0.0 copy-start.8
  0.7 0.0 copy-start.7
  0.7 0.0 copy-start.6
  0.7 0.0 copy-start.5
  0.7 0.0 copy-start
  0.7 0.0 copy-start.3
  0.7 0.0 copy-start.4
  0.7 0.0 copy-start.9
  0.7 0.0 copy-start.10
  0.8 0.0 copy-start.11
  0.8 3.6 %forward_yz.1 = (f32[128,128]{1,0:T(8,128)S(1)}, bf16[32,32768]{1,0:T(8,128)(2,1)S(1)}) custom-call(bf16[32,32768]{1,0:T(8,128)(2,1)} %bitcast.23, f32[1,32]{1,0:T(1,128)} %bitcast.25, bf16[256,256]{1,0:T(8,128)(2,1)} %constant.14.clone.table_z, bf16[264,1024]{1,0:T(8,128)(2,1)} %constant.15.clone.table_y, f32[2,17,128]{2,1,0:T(8,128)} %constant.16.clone.turns), custom_call_target="tpu_custom_call" | custom-call | tf_op jit(solution)/shard_map/forward_yz/pallas_call | solution.py:623
  4.4 14.2 %all_to_all.10 = f32[32,4,128]{2,1,0:T(4,128)S(1)} all-to-all(f32[32,4,128]{2,1,0:T(4,128)S(1)} %bitcast.21), channel_id=1, replica_groups=mesh['groups'=1,'gx'=32] {'gx'}, dimensions={0} | all-to-all | bytes 131072 | tf_op jit(solution)/shard_map/all_to_all | solution.py:647
  18.6 0.0 copy-done.1
  18.6 0.0 copy-done.2
  18.6 0.0 copy-done.8
  18.6 0.0 copy-done.7
  18.6 0.0 copy-done.6
  18.6 0.0 copy-done.5
  18.6 0.0 copy-done
  18.6 1.8 %mix_modes.1 = (f32[128,128]{1,0:T(8,128)S(1)}, bf16[256,256]{1,0:T(8,128)(2,1)S(1)}, bf16[1056,256]{1,0:T(8,128)(2,1)S(1)}, bf16[32,1024]{1,0:T(8,128)(2,1)S(1)}) custom-call(f32[128,128]{1,0:T(8,128)S(1)} %bitcast.14, bf16[2,32,32,256]{3,2,1,0:T(8,128)(2,1)S(1)} %copy-done, bf16[1024,256]{1,0:T(8,128)(2,1)S(1)} %copy-done.2, ...), custom_call_target="tpu_custom_call" | custom-call | tf_op jit(solution)/shard_map/mix_modes/pallas_call | solution.py:652
  20.4 9.1 %all_to_all.11 = f32[32,4,128]{2,1,0:T(4,128)S(1)} all-to-all(f32[32,4,128]{2,1,0:T(4,128)S(1)} %bitcast.20), channel_id=1, replica_groups=mesh['groups'=1,'gx'=32] {'gx'}, dimensions={0} | all-to-all | bytes 131072 | tf_op jit(solution)/shard_map/all_to_all | solution.py:680
  29.6 0.0 copy-done.3
  29.6 0.0 copy-done.4
  29.6 0.0 copy-done.9
  29.6 0.0 copy-done.10
  29.6 0.0 copy-done.11
  29.6 5.6 %point_network.2 = (f32[3,192,128]{2,1,0:T(8,128)S(1)}, f32[3,192,128]{2,1,0:T(8,128)S(1)}, f32[192,128]{1,0:T(8,128)S(1)}) custom-call(f32[128,128]{1,0:T(8,128)S(1)} %bitcast.18, bf16[32,32768]{1,0:T(8,128)(2,1)S(1)} %get-tuple-element.18.values, bf16[256,256]{1,0:T(8,128)(2,1)S(1)} %get-tuple-element.19.wide_bypass, ...), custom_call_target="tpu_custom_call" | custom-call | flops 9830400000 | bytes 4915200 | tf_op jit(solution)/shard_map/point_network/pallas_call | solution.py:690
  35.2 2.3 %collective-permute-start = (f32[3,192,128]{2,1,0:T(8,128)S(1)}, f32[3,192,128]{2,1,0:T(8,128)S(1)}, u32[]{:S(2)}, u32[]{:S(2)}) collective-permute-start(f32[3,192,128]{2,1,0:T(8,128)S(1)} %get-tuple-element.28.refs_1_), channel_id=1, source_target_pairs={{1,2},{3,4},{5,6},{7,8},{9,10},{11,12},{13,14},{15,16},{17,18},{19... | collective-permute-start | bytes 884744 | tf_op jit(solution)/shard_map/ppermute | solution.py:717
  37.6 0.1 collective-permute-start.1
  37.7 2.6 %point_network.3 = (f32[3,64,128]{2,1,0:T(8,128)S(1)}, f32[3,64,128]{2,1,0:T(8,128)S(1)}, f32[64,128]{1,0:T(8,128)S(1)}) custom-call(f32[128,128]{1,0:T(8,128)S(1)} %bitcast.19, bf16[32,32768]{1,0:T(8,128)(2,1)S(1)} %get-tuple-element.18.values, bf16[256,256]{1,0:T(8,128)(2,1)S(1)} %get-tuple-element.19.wide_bypass, ...), custom_call_target="tpu_custom_call" | custom-call | flops 3276800000 | bytes 1638400 | tf_op jit(solution)/shard_map/point_network/pallas_call | solution.py:690
  40.3 3.6 %collective-permute-start.2 = (f32[3,64,128]{2,1,0:T(8,128)S(1)}, f32[3,64,128]{2,1,0:T(8,128)S(1)}, u32[]{:S(2)}, u32[]{:S(2)}) collective-permute-start(f32[3,64,128]{2,1,0:T(8,128)S(1)} %get-tuple-element.29.refs_5_), channel_id=1, source_target_pairs={{1,2},{3,4},{5,6},{7,8},{9,10},{11,12},{13,14},{15,16},{17,18},{19... | collective-permute-start | bytes 294920 | tf_op jit(solution)/shard_map/ppermute | solution.py:719
  43.9 0.1 collective-permute-start.3
  44.0 1.6 %faces_in_plane.1 = (f32[2,256,128]{2,1,0:T(8,128)}, f32[256,128]{1,0:T(8,128)S(1)}) custom-call(f32[3,192,128]{2,1,0:T(8,128)S(1)} %get-tuple-element.22.first.refs_0_, f32[3,64,128]{2,1,0:T(8,128)S(1)} %get-tuple-element.23.last.refs_4_, f32[192,128]{1,0:T(8,128)S(1)} %get-tuple-element.24.first_filled, f32[64,128]{1,0:T(8,128)S(1)} %get-tuple-element.25.last_filled, ...), custom_call_target="tpu_custom_call" | custom-call | tf_op jit(solution)/shard_map/faces_in_plane/pallas_call | solution.py:720
  45.7 2.6 %collective-permute-done.2.refs_6_ = f32[3,64,128]{2,1,0:T(8,128)S(1)} collective-permute-done((f32[3,64,128]{2,1,0:T(8,128)S(1)}, f32[3,64,128]{2,1,0:T(8,128)S(1)}, u32[]{:S(2)}, u32[]{:S(2)}) %collective-permute-start.2) | collective-permute-done | bytes 98336 | tf_op jit(solution)/shard_map/ppermute | solution.py:719
  48.3 0.0 collective-permute-done.3.refs_7_
  48.3 0.0 collective-permute-done.refs_2_
  48.3 0.0 collective-permute-done.1.refs_3_
  48.3 0.8 %faces_between_planes.1 = f32[256,128]{1,0:T(8,128)} custom-call(f32[256,128]{1,0:T(8,128)S(1)} %get-tuple-element.27.partial, f32[3,192,128]{2,1,0:T(8,128)S(1)} %get-tuple-element.22.first.refs_0_, f32[3,192,128]{2,1,0:T(8,128)S(1)} %get-tuple-element.28.refs_1_, f32[3,192,128]{2,1,0:T(8,128)S(1)} %collective-permute-done.refs_2_, ...), custom_call_target="tpu_custom_call" | custom-call | tf_op jit(solution)/shard_map/faces_between_planes/pallas_call | solution.py:731
Async XLA Ops:
  0.6 18.0 %copy-start.1 = (bf16[256,1024]{1,0:T(8,128)(2,1)S(1)}, bf16[256,1024]{1,0:T(8,128)(2,1)}, u32[]{:S(2)}) copy-start(bf16[256,1024]{1,0:T(8,128)(2,1)} %constant.18.clone.table_back) | copy-start | bytes 1572868
  0.6 18.0 %copy-start.2 = (bf16[1024,256]{1,0:T(8,128)(2,1)S(1)}, bf16[1024,256]{1,0:T(8,128)(2,1)}, u32[]{:S(2)}) copy-start(bf16[1024,256]{1,0:T(8,128)(2,1)} %constant.17.clone.table_x) | copy-start | bytes 1572868
  0.7 17.9 %copy-start.8 = (bf16[2,32]{1,0:T(2,128)(2,1)S(1)}, bf16[2,32]{1,0:T(2,128)(2,1)}, u32[]{:S(2)}) copy-start(bf16[2,32]{1,0:T(2,128)(2,1)} %decode.1) | copy-start | bytes 388
  0.7 17.9 %copy-start.7 = (bf16[32,128]{1,0:T(8,128)(2,1)S(1)}, bf16[32,128]{1,0:T(8,128)(2,1)}, u32[]{:S(2)}) copy-start(bf16[32,128]{1,0:T(8,128)(2,1)} %mlp_out.1) | copy-start | bytes 24580
  0.7 17.9 %copy-start.6 = (bf16[128,32]{0,1:T(8,128)(2,1)S(1)}, bf16[128,32]{0,1:T(8,128)(2,1)}, u32[]{:S(2)}) copy-start(bf16[128,32]{0,1:T(8,128)(2,1)} %param.22) | copy-start | bytes 24580
  0.7 17.9 %copy-start.5 = (bf16[32,32]{1,0:T(8,128)(2,1)S(1)}, bf16[32,32]{1,0:T(8,128)(2,1)}, u32[]{:S(2)}) copy-start(bf16[32,32]{1,0:T(8,128)(2,1)} %bypass.1) | copy-start | bytes 6148
  0.7 17.9 %copy-start = (bf16[2,32,32,256]{3,2,1,0:T(8,128)(2,1)S(1)}, bf16[2,32,32,256]{3,2,1,0:T(8,128)(2,1)}, u32[]{:S(2)}) copy-start(bf16[2,32,32,256]{3,2,1,0:T(8,128)(2,1)} %weight.1) | copy-start | bytes 3145732
  0.7 28.8 %copy-start.3 = (s32[3,1,32768]{2,1,0:T(1,128)S(1)}, s32[3,1,32768]{2,1,0:T(1,128)}, u32[]{:S(2)}) copy-start(s32[3,1,32768]{2,1,0:T(1,128)} %param.26) | copy-start | bytes 1179652
  0.7 28.8 %copy-start.4 = (s32[1,32768]{1,0:T(1,128)S(1)}, s32[1,32768]{1,0:T(1,128)}, u32[]{:S(2)}) copy-start(s32[1,32768]{1,0:T(1,128)} %param.25) | copy-start | bytes 393220
  0.7 28.8 %copy-start.9 = (f32[8]{0:T(128)S(1)}, f32[8]{0:T(128)}, u32[]{:S(2)}) copy-start(f32[8]{0:T(128)} %perm_table.5) | copy-start | bytes 100
  0.7 28.8 %copy-start.10 = (bf16[768,512]{1,0:T(8,128)(2,1)S(1)}, bf16[768,512]{1,0:T(8,128)(2,1)}, u32[]{:S(2)}) copy-start(bf16[768,512]{1,0:T(8,128)(2,1)} %constant.19.clone.tables) | copy-start | bytes 2359300
  0.8 28.8 %copy-start.11 = (f32[2,32,128]{2,1,0:T(8,128)S(1)}, f32[2,32,128]{2,1,0:T(8,128)}, u32[]{:S(2)}) copy-start(f32[2,32,128]{2,1,0:T(8,128)} %constant.20.clone.turns) | copy-start | bytes 98308
  35.2 13.1 %collective-permute-start = (f32[3,192,128]{2,1,0:T(8,128)S(1)}, f32[3,192,128]{2,1,0:T(8,128)S(1)}, u32[]{:S(2)}, u32[]{:S(2)}) collective-permute-start(f32[3,192,128]{2,1,0:T(8,128)S(1)} %get-tuple-element.28.refs_1_), channel_id=1, source_target_pairs={{1,2},{3,4},{5,6},{7,8},{9,10},{11,12},{13,14},{15,16},{17,18},{19... | collective-permute-start | bytes 884744 | tf_op jit(solution)/shard_map/ppermute | solution.py:717
  37.6 10.7 %collective-permute-start.1 = (f32[3,192,128]{2,1,0:T(8,128)S(1)}, f32[3,192,128]{2,1,0:T(8,128)S(1)}, u32[]{:S(2)}, u32[]{:S(2)}) collective-permute-start(f32[3,192,128]{2,1,0:T(8,128)S(1)} %get-tuple-element.22.first.refs_0_), channel_id=1, source_target_pairs={{0,1},{2,3},{4,5},{6,7},{8,9},{10,11},{12,13},{14,15},{16,17},{18,... | collective-permute-start | bytes 884744 | tf_op jit(solution)/shard_map/ppermute | solution.py:717
  40.3 8.0 %collective-permute-start.2 = (f32[3,64,128]{2,1,0:T(8,128)S(1)}, f32[3,64,128]{2,1,0:T(8,128)S(1)}, u32[]{:S(2)}, u32[]{:S(2)}) collective-permute-start(f32[3,64,128]{2,1,0:T(8,128)S(1)} %get-tuple-element.29.refs_5_), channel_id=1, source_target_pairs={{1,2},{3,4},{5,6},{7,8},{9,10},{11,12},{13,14},{15,16},{17,18},{19... | collective-permute-start | bytes 294920 | tf_op jit(solution)/shard_map/ppermute | solution.py:719
  43.9 4.3 %collective-permute-start.3 = (f32[3,64,128]{2,1,0:T(8,128)S(1)}, f32[3,64,128]{2,1,0:T(8,128)S(1)}, u32[]{:S(2)}, u32[]{:S(2)}) collective-permute-start(f32[3,64,128]{2,1,0:T(8,128)S(1)} %get-tuple-element.23.last.refs_4_), channel_id=1, source_target_pairs={{0,1},{2,3},{4,5},{6,7},{8,9},{10,11},{12,13},{14,15},{16,17},{18,... | collective-permute-start | bytes 294920 | tf_op jit(solution)/shard_map/ppermute | solution.py:719

commit v7 on v6

--- a/solution.py
+++ b/solution.py
@@ -306,17 +306,10 @@
     mixed,
 ):
     wide_bypass[...] = diagonal(bypass[...])
-    inner = 0.5 * mlp_in_t[...].astype(F32)
-    count = wide_out.shape[1]
-    wide_in[:count] = diagonal(inner.T.astype(BF16))
-    heads = 0.5 * dot(decode[...], mlp_out[...])
-    through = dot(heads, inner, ((1,), (1,)), precision=lax.Precision.HIGHEST)
-    def rows_of(x):
-        rows = [part[k : k + 1] for part in split(x) for k in range(2)]
-        return jnp.concatenate([diagonal(row).astype(F32) for row in rows], axis=0).astype(BF16)
-
-    wide_out[...] = rows_of(heads)
-    wide_in[count:] = rows_of(through)
+    wide_in[...] = diagonal((0.5 * mlp_in_t[...].astype(F32)).T.astype(BF16))
+    heads = split(0.5 * dot(decode[...], mlp_out[...]))
+    rows = [diagonal(part[k : k + 1]).astype(F32) for part in heads for k in range(2)]
+    wide_out[...] = jnp.concatenate(rows, axis=0).astype(BF16)
 
     half = lines.shape[1] // 2
     count = half // (2 * TILES)
@@ -486,9 +479,8 @@
         )
     )
     lifted = gelu_twice(spectral + dot(wide_bypass[...], own)).astype(BF16)
-    inner = dot(wide_in[...], lifted)
-    count = wide_out.shape[1]
-    decoded = dot(wide_out[...], curved(inner[:count])) + inner[count:]
+    hidden = gelu_twice(dot(wide_in[...], lifted)).astype(BF16)
+    decoded = dot(wide_out[...], hidden)
     decoded = decoded[: 2 * SUB] + decoded[2 * SUB :]
     even_plane = lax.axis_index("gx") % 2 == 0
     for a in range(rows // SUB):
@@ -515,11 +507,6 @@
     for k in range(ZONES):
         perm = jnp.where(zones == k, perm_table[k], perm)
     return perm
-
-
-def curved(x):
-    x = x.astype(BF16)
-    return x * jnp.tanh(x * (BF16(GELU_A) + BF16(GELU_B) * (x * x)))
 
 
 def joined(first, second):
@@ -656,7 +643,7 @@
         out_shape=[
             jax.ShapeDtypeStruct((planes * part, 2 * share), F32),
             jax.ShapeDtypeStruct((SUB * width, SUB * width), BF16),
-            jax.ShapeDtypeStruct((SUB * hidden + 4 * SUB, SUB * width), BF16),
+            jax.ShapeDtypeStruct((SUB * hidden, SUB * width), BF16),
             jax.ShapeDtypeStruct((4 * SUB, SUB * hidden), BF16),
         ],
         scratch_shapes=[

time: 49.3 us -> 49.9 us (1.012)
  Pallas kernels: 16.1 us -> 17.1 us
    pallas_call x2, Pallas kernels: 8.26 us -> 9.45 us  [network(): pl.pallas_call(functools.partial(point_kernel, first=first), in_specs=[wh...]
where the time goes in v7:
time: 49.9 us; the launch traced here: 49.7 us
  blocking collectives  23.3 us (47%)
  Pallas kernels  17.1 us (34%)
  starting transfers between devices  6.12 us (12%)
  waiting for transfers between devices  2.3 us (5%)
  between operations  0.85 us (2%)
    all_to_all x2, blocking collectives, body(): blocks = lax.all_to_all(blocks, 'gx', 0, 0, tiled=True)  23.3 us
    pallas_call x2, Pallas kernels, network(): pl.pallas_call(functools.partial(point_kernel, first=first), in_specs=[wh...  9.45 us
    pallas_call x1, Pallas kernels, body(): pl.pallas_call(forward_kernel, in_specs=[pl.BlockSpec(memory_space=pl.ANY...  3.65 us
    ppermute x1, starting transfers between devices, body(): lax.ppermute(last[1], 'gx', far)  3.63 us
    ppermute x1, starting transfers between devices, body(): lax.ppermute(first[1], 'gx', far)  2.35 us
    ppermute x1, waiting for transfers between devices, body(): lax.ppermute(last[1], 'gx', far)  2.29 us
    pallas_call x1, Pallas kernels, body(): pl.pallas_call(inner_kernel, in_specs=[whole()] * 6 + [pl.BlockSpec(memor...  1.65 us
    pallas_call x1, Pallas kernels, body(): pl.pallas_call(mix_kernel, in_specs=[whole()] * 8, out_specs=[whole()] *...  1.54 us
  transfers between devices with their start and end apart: 4, of which 1 were waited for; matrix products, arithmetic and copies ran while one was open for 0% of the time, Pallas kernels for 9%

profile of v7, /device:TPU:1, one launch (start us, length us, event | category | flops | bytes accessed | tf_op | source)
XLA Modules:
  0.0 49.7 jit_solution(2021544924462461023)
XLA Ops:
  0.6 0.0 copy-start.1
  0.6 0.0 copy-start.2
  0.7 0.0 copy-start.8
  0.7 0.0 copy-start.7
  0.7 0.0 copy-start.6
  0.7 0.0 copy-start.5
  0.7 0.0 copy-start
  0.7 0.0 copy-start.3
  0.7 0.0 copy-start.4
  0.7 0.0 copy-start.9
  0.7 0.0 copy-start.10
  0.8 0.0 copy-start.11
  0.8 3.6 %forward_yz.1 = (f32[128,128]{1,0:T(8,128)S(1)}, bf16[32,32768]{1,0:T(8,128)(2,1)S(1)}) custom-call(bf16[32,32768]{1,0:T(8,128)(2,1)} %bitcast.23, f32[1,32]{1,0:T(1,128)} %bitcast.25, bf16[256,256]{1,0:T(8,128)(2,1)} %constant.14.clone.table_z, bf16[264,1024]{1,0:T(8,128)(2,1)} %constant.15.clone.table_y, f32[2,17,128]{2,1,0:T(8,128)} %constant.16.clone.turns), custom_call_target="tpu_custom_call" | custom-call | tf_op jit(solution)/shard_map/forward_yz/pallas_call | solution.py:610
  4.4 14.2 %all_to_all.10 = f32[32,4,128]{2,1,0:T(4,128)S(1)} all-to-all(f32[32,4,128]{2,1,0:T(4,128)S(1)} %bitcast.21), channel_id=1, replica_groups=mesh['groups'=1,'gx'=32] {'gx'}, dimensions={0} | all-to-all | bytes 131072 | tf_op jit(solution)/shard_map/all_to_all | solution.py:634
  18.6 0.0 copy-done.1
  18.6 0.0 copy-done.2
  18.6 0.0 copy-done.8
  18.6 0.0 copy-done.7
  18.6 0.0 copy-done.6
  18.6 0.0 copy-done.5
  18.6 0.0 copy-done
  18.6 1.5 %mix_modes.1 = (f32[128,128]{1,0:T(8,128)S(1)}, bf16[256,256]{1,0:T(8,128)(2,1)S(1)}, bf16[1024,256]{1,0:T(8,128)(2,1)S(1)}, bf16[32,1024]{1,0:T(8,128)(2,1)S(1)}) custom-call(f32[128,128]{1,0:T(8,128)S(1)} %bitcast.14, bf16[2,32,32,256]{3,2,1,0:T(8,128)(2,1)S(1)} %copy-done, bf16[1024,256]{1,0:T(8,128)(2,1)S(1)} %copy-done.2, ...), custom_call_target="tpu_custom_call" | custom-call | tf_op jit(solution)/shard_map/mix_modes/pallas_call | solution.py:639
  20.2 9.1 %all_to_all.11 = f32[32,4,128]{2,1,0:T(4,128)S(1)} all-to-all(f32[32,4,128]{2,1,0:T(4,128)S(1)} %bitcast.20), channel_id=1, replica_groups=mesh['groups'=1,'gx'=32] {'gx'}, dimensions={0} | all-to-all | bytes 131072 | tf_op jit(solution)/shard_map/all_to_all | solution.py:667
  29.3 0.0 copy-done.3
  29.3 0.0 copy-done.4
  29.3 0.0 copy-done.9
  29.3 0.0 copy-done.10
  29.3 0.0 copy-done.11
  29.3 6.5 %point_network.2 = (f32[3,192,128]{2,1,0:T(8,128)S(1)}, f32[3,192,128]{2,1,0:T(8,128)S(1)}, f32[192,128]{1,0:T(8,128)S(1)}) custom-call(f32[128,128]{1,0:T(8,128)S(1)} %bitcast.18, bf16[32,32768]{1,0:T(8,128)(2,1)S(1)} %get-tuple-element.18.values, bf16[256,256]{1,0:T(8,128)(2,1)S(1)} %get-tuple-element.19.wide_bypass, ...), custom_call_target="tpu_custom_call" | custom-call | flops 9830400000 | bytes 4915200 | tf_op jit(solution)/shard_map/point_network/pallas_call | solution.py:677
  35.8 2.3 %collective-permute-start = (f32[3,192,128]{2,1,0:T(8,128)S(1)}, f32[3,192,128]{2,1,0:T(8,128)S(1)}, u32[]{:S(2)}, u32[]{:S(2)}) collective-permute-start(f32[3,192,128]{2,1,0:T(8,128)S(1)} %get-tuple-element.28.refs_1_), channel_id=1, source_target_pairs={{1,2},{3,4},{5,6},{7,8},{9,10},{11,12},{13,14},{15,16},{17,18},{19... | collective-permute-start | bytes 884744 | tf_op jit(solution)/shard_map/ppermute | solution.py:704
  38.2 0.1 collective-permute-start.1
  38.3 3.0 %point_network.3 = (f32[3,64,128]{2,1,0:T(8,128)S(1)}, f32[3,64,128]{2,1,0:T(8,128)S(1)}, f32[64,128]{1,0:T(8,128)S(1)}) custom-call(f32[128,128]{1,0:T(8,128)S(1)} %bitcast.19, bf16[32,32768]{1,0:T(8,128)(2,1)S(1)} %get-tuple-element.18.values, bf16[256,256]{1,0:T(8,128)(2,1)S(1)} %get-tuple-element.19.wide_bypass, ...), custom_call_target="tpu_custom_call" | custom-call | flops 3276800000 | bytes 1638400 | tf_op jit(solution)/shard_map/point_network/pallas_call | solution.py:677
  41.2 3.6 %collective-permute-start.2 = (f32[3,64,128]{2,1,0:T(8,128)S(1)}, f32[3,64,128]{2,1,0:T(8,128)S(1)}, u32[]{:S(2)}, u32[]{:S(2)}) collective-permute-start(f32[3,64,128]{2,1,0:T(8,128)S(1)} %get-tuple-element.29.refs_5_), channel_id=1, source_target_pairs={{1,2},{3,4},{5,6},{7,8},{9,10},{11,12},{13,14},{15,16},{17,18},{19... | collective-permute-start | bytes 294920 | tf_op jit(solution)/shard_map/ppermute | solution.py:706
  44.9 0.1 collective-permute-start.3
  44.9 1.6 %faces_in_plane.1 = (f32[2,256,128]{2,1,0:T(8,128)}, f32[256,128]{1,0:T(8,128)S(1)}) custom-call(f32[3,192,128]{2,1,0:T(8,128)S(1)} %get-tuple-element.22.first.refs_0_, f32[3,64,128]{2,1,0:T(8,128)S(1)} %get-tuple-element.23.last.refs_4_, f32[192,128]{1,0:T(8,128)S(1)} %get-tuple-element.24.first_filled, f32[64,128]{1,0:T(8,128)S(1)} %get-tuple-element.25.last_filled, ...), custom_call_target="tpu_custom_call" | custom-call | tf_op jit(solution)/shard_map/faces_in_plane/pallas_call | solution.py:707
  46.6 2.3 %collective-permute-done.2.refs_6_ = f32[3,64,128]{2,1,0:T(8,128)S(1)} collective-permute-done((f32[3,64,128]{2,1,0:T(8,128)S(1)}, f32[3,64,128]{2,1,0:T(8,128)S(1)}, u32[]{:S(2)}, u32[]{:S(2)}) %collective-permute-start.2) | collective-permute-done | bytes 98336 | tf_op jit(solution)/shard_map/ppermute | solution.py:706
  48.9 0.0 collective-permute-done.3.refs_7_
  48.9 0.0 collective-permute-done.refs_2_
  48.9 0.0 collective-permute-done.1.refs_3_
  48.9 0.8 %faces_between_planes.1 = f32[256,128]{1,0:T(8,128)} custom-call(f32[256,128]{1,0:T(8,128)S(1)} %get-tuple-element.27.partial, f32[3,192,128]{2,1,0:T(8,128)S(1)} %get-tuple-element.22.first.refs_0_, f32[3,192,128]{2,1,0:T(8,128)S(1)} %get-tuple-element.28.refs_1_, f32[3,192,128]{2,1,0:T(8,128)S(1)} %collective-permute-done.refs_2_, ...), custom_call_target="tpu_custom_call" | custom-call | tf_op jit(solution)/shard_map/faces_between_planes/pallas_call | solution.py:718
Async XLA Ops:
  0.6 18.0 %copy-start.1 = (bf16[256,1024]{1,0:T(8,128)(2,1)S(1)}, bf16[256,1024]{1,0:T(8,128)(2,1)}, u32[]{:S(2)}) copy-start(bf16[256,1024]{1,0:T(8,128)(2,1)} %constant.18.clone.table_back) | copy-start | bytes 1572868
  0.6 18.0 %copy-start.2 = (bf16[1024,256]{1,0:T(8,128)(2,1)S(1)}, bf16[1024,256]{1,0:T(8,128)(2,1)}, u32[]{:S(2)}) copy-start(bf16[1024,256]{1,0:T(8,128)(2,1)} %constant.17.clone.table_x) | copy-start | bytes 1572868
  0.7 17.9 %copy-start.8 = (bf16[2,32]{1,0:T(2,128)(2,1)S(1)}, bf16[2,32]{1,0:T(2,128)(2,1)}, u32[]{:S(2)}) copy-start(bf16[2,32]{1,0:T(2,128)(2,1)} %decode.1) | copy-start | bytes 388
  0.7 17.9 %copy-start.7 = (bf16[32,128]{1,0:T(8,128)(2,1)S(1)}, bf16[32,128]{1,0:T(8,128)(2,1)}, u32[]{:S(2)}) copy-start(bf16[32,128]{1,0:T(8,128)(2,1)} %mlp_out.1) | copy-start | bytes 24580
  0.7 17.9 %copy-start.6 = (bf16[128,32]{0,1:T(8,128)(2,1)S(1)}, bf16[128,32]{0,1:T(8,128)(2,1)}, u32[]{:S(2)}) copy-start(bf16[128,32]{0,1:T(8,128)(2,1)} %param.22) | copy-start | bytes 24580
  0.7 17.9 %copy-start.5 = (bf16[32,32]{1,0:T(8,128)(2,1)S(1)}, bf16[32,32]{1,0:T(8,128)(2,1)}, u32[]{:S(2)}) copy-start(bf16[32,32]{1,0:T(8,128)(2,1)} %bypass.1) | copy-start | bytes 6148
  0.7 17.9 %copy-start = (bf16[2,32,32,256]{3,2,1,0:T(8,128)(2,1)S(1)}, bf16[2,32,32,256]{3,2,1,0:T(8,128)(2,1)}, u32[]{:S(2)}) copy-start(bf16[2,32,32,256]{3,2,1,0:T(8,128)(2,1)} %weight.1) | copy-start | bytes 3145732
  0.7 28.6 %copy-start.3 = (s32[3,1,32768]{2,1,0:T(1,128)S(1)}, s32[3,1,32768]{2,1,0:T(1,128)}, u32[]{:S(2)}) copy-start(s32[3,1,32768]{2,1,0:T(1,128)} %param.26) | copy-start | bytes 1179652
  0.7 28.6 %copy-start.4 = (s32[1,32768]{1,0:T(1,128)S(1)}, s32[1,32768]{1,0:T(1,128)}, u32[]{:S(2)}) copy-start(s32[1,32768]{1,0:T(1,128)} %param.25) | copy-start | bytes 393220
  0.7 28.6 %copy-start.9 = (f32[8]{0:T(128)S(1)}, f32[8]{0:T(128)}, u32[]{:S(2)}) copy-start(f32[8]{0:T(128)} %perm_table.5) | copy-start | bytes 100
  0.7 28.6 %copy-start.10 = (bf16[768,512]{1,0:T(8,128)(2,1)S(1)}, bf16[768,512]{1,0:T(8,128)(2,1)}, u32[]{:S(2)}) copy-start(bf16[768,512]{1,0:T(8,128)(2,1)} %constant.19.clone.tables) | copy-start | bytes 2359300
  0.8 28.6 %copy-start.11 = (f32[2,32,128]{2,1,0:T(8,128)S(1)}, f32[2,32,128]{2,1,0:T(8,128)}, u32[]{:S(2)}) copy-start(f32[2,32,128]{2,1,0:T(8,128)} %constant.20.clone.turns) | copy-start | bytes 98308
  35.8 13.1 %collective-permute-start = (f32[3,192,128]{2,1,0:T(8,128)S(1)}, f32[3,192,128]{2,1,0:T(8,128)S(1)}, u32[]{:S(2)}, u32[]{:S(2)}) collective-permute-start(f32[3,192,128]{2,1,0:T(8,128)S(1)} %get-tuple-element.28.refs_1_), channel_id=1, source_target_pairs={{1,2},{3,4},{5,6},{7,8},{9,10},{11,12},{13,14},{15,16},{17,18},{19... | collective-permute-start | bytes 884744 | tf_op jit(solution)/shard_map/ppermute | solution.py:704
  38.2 10.7 %collective-permute-start.1 = (f32[3,192,128]{2,1,0:T(8,128)S(1)}, f32[3,192,128]{2,1,0:T(8,128)S(1)}, u32[]{:S(2)}, u32[]{:S(2)}) collective-permute-start(f32[3,192,128]{2,1,0:T(8,128)S(1)} %get-tuple-element.22.first.refs_0_), channel_id=1, source_target_pairs={{0,1},{2,3},{4,5},{6,7},{8,9},{10,11},{12,13},{14,15},{16,17},{18,... | collective-permute-start | bytes 884744 | tf_op jit(solution)/shard_map/ppermute | solution.py:704
  41.2 7.7 %collective-permute-start.2 = (f32[3,64,128]{2,1,0:T(8,128)S(1)}, f32[3,64,128]{2,1,0:T(8,128)S(1)}, u32[]{:S(2)}, u32[]{:S(2)}) collective-permute-start(f32[3,64,128]{2,1,0:T(8,128)S(1)} %get-tuple-element.29.refs_5_), channel_id=1, source_target_pairs={{1,2},{3,4},{5,6},{7,8},{9,10},{11,12},{13,14},{15,16},{17,18},{19... | collective-permute-start | bytes 294920 | tf_op jit(solution)/shard_map/ppermute | solution.py:706
  44.9 4.0 %collective-permute-start.3 = (f32[3,64,128]{2,1,0:T(8,128)S(1)}, f32[3,64,128]{2,1,0:T(8,128)S(1)}, u32[]{:S(2)}, u32[]{:S(2)}) collective-permute-start(f32[3,64,128]{2,1,0:T(8,128)S(1)} %get-tuple-element.23.last.refs_4_), channel_id=1, source_target_pairs={{0,1},{2,3},{4,5},{6,7},{8,9},{10,11},{12,13},{14,15},{16,17},{18,... | collective-permute-start | bytes 294920 | tf_op jit(solution)/shard_map/ppermute | solution.py:706

commit v8 on v7

--- a/solution.py
+++ b/solution.py
@@ -479,7 +479,8 @@
         )
     )
     lifted = gelu_twice(spectral + dot(wide_bypass[...], own)).astype(BF16)
-    hidden = gelu_twice(dot(wide_in[...], lifted)).astype(BF16)
+    inner = dot(wide_in[...], lifted).astype(BF16)
+    hidden = inner + inner * jnp.tanh(inner * (BF16(GELU_A) + BF16(GELU_B) * (inner * inner)))
     decoded = dot(wide_out[...], hidden)
     decoded = decoded[: 2 * SUB] + decoded[2 * SUB :]
     even_plane = lax.axis_index("gx") % 2 == 0

time: 49.9 us -> 48.9 us (0.980)
  Pallas kernels: 17.1 us -> 15.7 us
    pallas_call x2, Pallas kernels: 9.45 us -> 8.05 us  [network(): pl.pallas_call(functools.partial(point_kernel, first=first), in_specs=[wh...]
where the time goes in v8:
time: 48.9 us; the launch traced here: 48.7 us
  blocking collectives  23.3 us (48%)
  Pallas kernels  15.7 us (32%)
  starting transfers between devices  6.11 us (12%)
  waiting for transfers between devices  2.71 us (6%)
  between operations  0.85 us (2%)
    all_to_all x2, blocking collectives, body(): blocks = lax.all_to_all(blocks, 'gx', 0, 0, tiled=True)  23.3 us
    pallas_call x2, Pallas kernels, network(): pl.pallas_call(functools.partial(point_kernel, first=first), in_specs=[wh...  8.05 us
    pallas_call x1, Pallas kernels, body(): pl.pallas_call(forward_kernel, in_specs=[pl.BlockSpec(memory_space=pl.ANY...  3.65 us
    ppermute x1, starting transfers between devices, body(): lax.ppermute(last[1], 'gx', far)  3.63 us
    ppermute x1, waiting for transfers between devices, body(): lax.ppermute(last[1], 'gx', far)  2.7 us
    ppermute x1, starting transfers between devices, body(): lax.ppermute(first[1], 'gx', far)  2.35 us
    pallas_call x1, Pallas kernels, body(): pl.pallas_call(inner_kernel, in_specs=[whole()] * 6 + [pl.BlockSpec(memor...  1.65 us
    pallas_call x1, Pallas kernels, body(): pl.pallas_call(mix_kernel, in_specs=[whole()] * 8, out_specs=[whole()] *...  1.54 us
  transfers between devices with their start and end apart: 4, of which 1 were waited for; matrix products, arithmetic and copies ran while one was open for 0% of the time, Pallas kernels for 9%

profile of v8, /device:TPU:1, one launch (start us, length us, event | category | flops | bytes accessed | tf_op | source)
XLA Modules:
  0.0 48.7 jit_solution(2088059955531047663)
XLA Ops:
  0.6 0.0 copy-start.1
  0.6 0.0 copy-start.2
  0.7 0.0 copy-start.8
  0.7 0.0 copy-start.7
  0.7 0.0 copy-start.6
  0.7 0.0 copy-start.5
  0.7 0.0 copy-start
  0.7 0.0 copy-start.3
  0.7 0.0 copy-start.4
  0.7 0.0 copy-start.9
  0.7 0.0 copy-start.10
  0.8 0.0 copy-start.11
  0.8 3.6 %forward_yz.1 = (f32[128,128]{1,0:T(8,128)S(1)}, bf16[32,32768]{1,0:T(8,128)(2,1)S(1)}) custom-call(bf16[32,32768]{1,0:T(8,128)(2,1)} %bitcast.23, f32[1,32]{1,0:T(1,128)} %bitcast.25, bf16[256,256]{1,0:T(8,128)(2,1)} %constant.14.clone.table_z, bf16[264,1024]{1,0:T(8,128)(2,1)} %constant.15.clone.table_y, f32[2,17,128]{2,1,0:T(8,128)} %constant.16.clone.turns), custom_call_target="tpu_custom_call" | custom-call | tf_op jit(solution)/shard_map/forward_yz/pallas_call | solution.py:611
  4.4 14.2 %all_to_all.10 = f32[32,4,128]{2,1,0:T(4,128)S(1)} all-to-all(f32[32,4,128]{2,1,0:T(4,128)S(1)} %bitcast.21), channel_id=1, replica_groups=mesh['groups'=1,'gx'=32] {'gx'}, dimensions={0} | all-to-all | bytes 131072 | tf_op jit(solution)/shard_map/all_to_all | solution.py:635
  18.6 0.0 copy-done.1
  18.6 0.0 copy-done.2
  18.6 0.0 copy-done.8
  18.6 0.0 copy-done.7
  18.6 0.0 copy-done.6
  18.6 0.0 copy-done.5
  18.6 0.0 copy-done
  18.6 1.5 %mix_modes.1 = (f32[128,128]{1,0:T(8,128)S(1)}, bf16[256,256]{1,0:T(8,128)(2,1)S(1)}, bf16[1024,256]{1,0:T(8,128)(2,1)S(1)}, bf16[32,1024]{1,0:T(8,128)(2,1)S(1)}) custom-call(f32[128,128]{1,0:T(8,128)S(1)} %bitcast.14, bf16[2,32,32,256]{3,2,1,0:T(8,128)(2,1)S(1)} %copy-done, bf16[1024,256]{1,0:T(8,128)(2,1)S(1)} %copy-done.2, ...), custom_call_target="tpu_custom_call" | custom-call | tf_op jit(solution)/shard_map/mix_modes/pallas_call | solution.py:640
  20.2 9.1 %all_to_all.11 = f32[32,4,128]{2,1,0:T(4,128)S(1)} all-to-all(f32[32,4,128]{2,1,0:T(4,128)S(1)} %bitcast.20), channel_id=1, replica_groups=mesh['groups'=1,'gx'=32] {'gx'}, dimensions={0} | all-to-all | bytes 131072 | tf_op jit(solution)/shard_map/all_to_all | solution.py:668
  29.3 0.0 copy-done.3
  29.3 0.0 copy-done.4
  29.3 0.0 copy-done.9
  29.3 0.0 copy-done.10
  29.3 0.0 copy-done.11
  29.3 5.5 %point_network.2 = (f32[3,192,128]{2,1,0:T(8,128)S(1)}, f32[3,192,128]{2,1,0:T(8,128)S(1)}, f32[192,128]{1,0:T(8,128)S(1)}) custom-call(f32[128,128]{1,0:T(8,128)S(1)} %bitcast.18, bf16[32,32768]{1,0:T(8,128)(2,1)S(1)} %get-tuple-element.18.values, bf16[256,256]{1,0:T(8,128)(2,1)S(1)} %get-tuple-element.19.wide_bypass, ...), custom_call_target="tpu_custom_call" | custom-call | flops 9830400000 | bytes 4915200 | tf_op jit(solution)/shard_map/point_network/pallas_call | solution.py:678
  34.8 2.3 %collective-permute-start = (f32[3,192,128]{2,1,0:T(8,128)S(1)}, f32[3,192,128]{2,1,0:T(8,128)S(1)}, u32[]{:S(2)}, u32[]{:S(2)}) collective-permute-start(f32[3,192,128]{2,1,0:T(8,128)S(1)} %get-tuple-element.28.refs_1_), channel_id=1, source_target_pairs={{1,2},{3,4},{5,6},{7,8},{9,10},{11,12},{13,14},{15,16},{17,18},{19... | collective-permute-start | bytes 884744 | tf_op jit(solution)/shard_map/ppermute | solution.py:705
  37.2 0.1 collective-permute-start.1
  37.3 2.5 %point_network.3 = (f32[3,64,128]{2,1,0:T(8,128)S(1)}, f32[3,64,128]{2,1,0:T(8,128)S(1)}, f32[64,128]{1,0:T(8,128)S(1)}) custom-call(f32[128,128]{1,0:T(8,128)S(1)} %bitcast.19, bf16[32,32768]{1,0:T(8,128)(2,1)S(1)} %get-tuple-element.18.values, bf16[256,256]{1,0:T(8,128)(2,1)S(1)} %get-tuple-element.19.wide_bypass, ...), custom_call_target="tpu_custom_call" | custom-call | flops 3276800000 | bytes 1638400 | tf_op jit(solution)/shard_map/point_network/pallas_call | solution.py:678
  39.8 3.6 %collective-permute-start.2 = (f32[3,64,128]{2,1,0:T(8,128)S(1)}, f32[3,64,128]{2,1,0:T(8,128)S(1)}, u32[]{:S(2)}, u32[]{:S(2)}) collective-permute-start(f32[3,64,128]{2,1,0:T(8,128)S(1)} %get-tuple-element.29.refs_5_), channel_id=1, source_target_pairs={{1,2},{3,4},{5,6},{7,8},{9,10},{11,12},{13,14},{15,16},{17,18},{19... | collective-permute-start | bytes 294920 | tf_op jit(solution)/shard_map/ppermute | solution.py:707
  43.5 0.1 collective-permute-start.3
  43.5 1.6 %faces_in_plane.1 = (f32[2,256,128]{2,1,0:T(8,128)}, f32[256,128]{1,0:T(8,128)S(1)}) custom-call(f32[3,192,128]{2,1,0:T(8,128)S(1)} %get-tuple-element.22.first.refs_0_, f32[3,64,128]{2,1,0:T(8,128)S(1)} %get-tuple-element.23.last.refs_4_, f32[192,128]{1,0:T(8,128)S(1)} %get-tuple-element.24.first_filled, f32[64,128]{1,0:T(8,128)S(1)} %get-tuple-element.25.last_filled, ...), custom_call_target="tpu_custom_call" | custom-call | tf_op jit(solution)/shard_map/faces_in_plane/pallas_call | solution.py:708
  45.2 2.7 %collective-permute-done.2.refs_6_ = f32[3,64,128]{2,1,0:T(8,128)S(1)} collective-permute-done((f32[3,64,128]{2,1,0:T(8,128)S(1)}, f32[3,64,128]{2,1,0:T(8,128)S(1)}, u32[]{:S(2)}, u32[]{:S(2)}) %collective-permute-start.2) | collective-permute-done | bytes 98336 | tf_op jit(solution)/shard_map/ppermute | solution.py:707
  47.9 0.0 collective-permute-done.3.refs_7_
  47.9 0.0 collective-permute-done.refs_2_
  47.9 0.0 collective-permute-done.1.refs_3_
  47.9 0.8 %faces_between_planes.1 = f32[256,128]{1,0:T(8,128)} custom-call(f32[256,128]{1,0:T(8,128)S(1)} %get-tuple-element.27.partial, f32[3,192,128]{2,1,0:T(8,128)S(1)} %get-tuple-element.22.first.refs_0_, f32[3,192,128]{2,1,0:T(8,128)S(1)} %get-tuple-element.28.refs_1_, f32[3,192,128]{2,1,0:T(8,128)S(1)} %collective-permute-done.refs_2_, ...), custom_call_target="tpu_custom_call" | custom-call | tf_op jit(solution)/shard_map/faces_between_planes/pallas_call | solution.py:719
Async XLA Ops:
  0.6 18.0 %copy-start.1 = (bf16[256,1024]{1,0:T(8,128)(2,1)S(1)}, bf16[256,1024]{1,0:T(8,128)(2,1)}, u32[]{:S(2)}) copy-start(bf16[256,1024]{1,0:T(8,128)(2,1)} %constant.18.clone.table_back) | copy-start | bytes 1572868
  0.6 18.0 %copy-start.2 = (bf16[1024,256]{1,0:T(8,128)(2,1)S(1)}, bf16[1024,256]{1,0:T(8,128)(2,1)}, u32[]{:S(2)}) copy-start(bf16[1024,256]{1,0:T(8,128)(2,1)} %constant.17.clone.table_x) | copy-start | bytes 1572868
  0.7 17.9 %copy-start.8 = (bf16[2,32]{1,0:T(2,128)(2,1)S(1)}, bf16[2,32]{1,0:T(2,128)(2,1)}, u32[]{:S(2)}) copy-start(bf16[2,32]{1,0:T(2,128)(2,1)} %decode.1) | copy-start | bytes 388
  0.7 17.9 %copy-start.7 = (bf16[32,128]{1,0:T(8,128)(2,1)S(1)}, bf16[32,128]{1,0:T(8,128)(2,1)}, u32[]{:S(2)}) copy-start(bf16[32,128]{1,0:T(8,128)(2,1)} %mlp_out.1) | copy-start | bytes 24580
  0.7 17.9 %copy-start.6 = (bf16[128,32]{0,1:T(8,128)(2,1)S(1)}, bf16[128,32]{0,1:T(8,128)(2,1)}, u32[]{:S(2)}) copy-start(bf16[128,32]{0,1:T(8,128)(2,1)} %param.22) | copy-start | bytes 24580
  0.7 17.9 %copy-start.5 = (bf16[32,32]{1,0:T(8,128)(2,1)S(1)}, bf16[32,32]{1,0:T(8,128)(2,1)}, u32[]{:S(2)}) copy-start(bf16[32,32]{1,0:T(8,128)(2,1)} %bypass.1) | copy-start | bytes 6148
  0.7 17.9 %copy-start = (bf16[2,32,32,256]{3,2,1,0:T(8,128)(2,1)S(1)}, bf16[2,32,32,256]{3,2,1,0:T(8,128)(2,1)}, u32[]{:S(2)}) copy-start(bf16[2,32,32,256]{3,2,1,0:T(8,128)(2,1)} %weight.1) | copy-start | bytes 3145732
  0.7 28.6 %copy-start.3 = (s32[3,1,32768]{2,1,0:T(1,128)S(1)}, s32[3,1,32768]{2,1,0:T(1,128)}, u32[]{:S(2)}) copy-start(s32[3,1,32768]{2,1,0:T(1,128)} %param.26) | copy-start | bytes 1179652
  0.7 28.6 %copy-start.4 = (s32[1,32768]{1,0:T(1,128)S(1)}, s32[1,32768]{1,0:T(1,128)}, u32[]{:S(2)}) copy-start(s32[1,32768]{1,0:T(1,128)} %param.25) | copy-start | bytes 393220
  0.7 28.6 %copy-start.9 = (f32[8]{0:T(128)S(1)}, f32[8]{0:T(128)}, u32[]{:S(2)}) copy-start(f32[8]{0:T(128)} %perm_table.5) | copy-start | bytes 100
  0.7 28.6 %copy-start.10 = (bf16[768,512]{1,0:T(8,128)(2,1)S(1)}, bf16[768,512]{1,0:T(8,128)(2,1)}, u32[]{:S(2)}) copy-start(bf16[768,512]{1,0:T(8,128)(2,1)} %constant.19.clone.tables) | copy-start | bytes 2359300
  0.8 28.6 %copy-start.11 = (f32[2,32,128]{2,1,0:T(8,128)S(1)}, f32[2,32,128]{2,1,0:T(8,128)}, u32[]{:S(2)}) copy-start(f32[2,32,128]{2,1,0:T(8,128)} %constant.20.clone.turns) | copy-start | bytes 98308
  34.8 13.1 %collective-permute-start = (f32[3,192,128]{2,1,0:T(8,128)S(1)}, f32[3,192,128]{2,1,0:T(8,128)S(1)}, u32[]{:S(2)}, u32[]{:S(2)}) collective-permute-start(f32[3,192,128]{2,1,0:T(8,128)S(1)} %get-tuple-element.28.refs_1_), channel_id=1, source_target_pairs={{1,2},{3,4},{5,6},{7,8},{9,10},{11,12},{13,14},{15,16},{17,18},{19... | collective-permute-start | bytes 884744 | tf_op jit(solution)/shard_map/ppermute | solution.py:705
  37.2 10.7 %collective-permute-start.1 = (f32[3,192,128]{2,1,0:T(8,128)S(1)}, f32[3,192,128]{2,1,0:T(8,128)S(1)}, u32[]{:S(2)}, u32[]{:S(2)}) collective-permute-start(f32[3,192,128]{2,1,0:T(8,128)S(1)} %get-tuple-element.22.first.refs_0_), channel_id=1, source_target_pairs={{0,1},{2,3},{4,5},{6,7},{8,9},{10,11},{12,13},{14,15},{16,17},{18,... | collective-permute-start | bytes 884744 | tf_op jit(solution)/shard_map/ppermute | solution.py:705
  39.8 8.1 %collective-permute-start.2 = (f32[3,64,128]{2,1,0:T(8,128)S(1)}, f32[3,64,128]{2,1,0:T(8,128)S(1)}, u32[]{:S(2)}, u32[]{:S(2)}) collective-permute-start(f32[3,64,128]{2,1,0:T(8,128)S(1)} %get-tuple-element.29.refs_5_), channel_id=1, source_target_pairs={{1,2},{3,4},{5,6},{7,8},{9,10},{11,12},{13,14},{15,16},{17,18},{19... | collective-permute-start | bytes 294920 | tf_op jit(solution)/shard_map/ppermute | solution.py:707
  43.5 4.4 %collective-permute-start.3 = (f32[3,64,128]{2,1,0:T(8,128)S(1)}, f32[3,64,128]{2,1,0:T(8,128)S(1)}, u32[]{:S(2)}, u32[]{:S(2)}) collective-permute-start(f32[3,64,128]{2,1,0:T(8,128)S(1)} %get-tuple-element.23.last.refs_4_), channel_id=1, source_target_pairs={{0,1},{2,3},{4,5},{6,7},{8,9},{10,11},{12,13},{14,15},{16,17},{18,... | collective-permute-start | bytes 294920 | tf_op jit(solution)/shard_map/ppermute | solution.py:707

commit v9 on v8

--- a/solution.py
+++ b/solution.py
@@ -567,7 +567,7 @@
 
     cut = refs[0].shape[1]
     for at, sides in ((slice(0, cut), refs[:4]), (slice(cut, ROWS), refs[4:8])):
-        residual[at] = partial[at] + flow(sides[0], sides[3]) + flow(sides[1], sides[2])
+        residual[at] = partial[at] + flow(sides[0], sides[2]) + flow(sides[1], sides[3])
 
 
 def near(x):
@@ -702,7 +702,7 @@
     near_by = [(i, i + 1) for i in range(0, devices, 2)]
     near_by = near_by + [(b, a) for a, b in near_by]
     *first, first_filled = network(0, ROWS - QUARTER)
-    first_other = [lax.ppermute(first[1], "gx", far), lax.ppermute(first[0], "gx", near_by)]
+    first_other = [lax.ppermute(first[0], "gx", near_by), lax.ppermute(first[1], "gx", far)]
     *last, last_filled = network(ROWS - QUARTER, QUARTER)
     last_other = [lax.ppermute(last[1], "gx", far), lax.ppermute(last[0], "gx", near_by)]
     fields, partial = pl.pallas_call(
@@ -723,7 +723,7 @@
         out_shape=jax.ShapeDtypeStruct((ROWS, LANES), F32),
         compiler_params=params(),
         name="faces_between_planes",
-    )(partial, *first, *first_other, *last, *last_other)
+    )(partial, *first, *first_other, *last, *last_other[::-1])
     return (fields.reshape(2, 1, cells), residual.reshape(1, cells))
 
 

time: 48.9 us -> 48.9 us (level)
  no operation moved by 1% of the time
where the time goes in v9:
time: 48.9 us; the launch traced here: 48.7 us
  blocking collectives  23.3 us (48%)
  Pallas kernels  15.7 us (32%)
  starting transfers between devices  6.11 us (12%)
  waiting for transfers between devices  2.71 us (6%)
  between operations  0.85 us (2%)
    all_to_all x2, blocking collectives, body(): blocks = lax.all_to_all(blocks, 'gx', 0, 0, tiled=True)  23.3 us
    pallas_call x2, Pallas kernels, network(): pl.pallas_call(functools.partial(point_kernel, first=first), in_specs=[wh...  8.05 us
    pallas_call x1, Pallas kernels, body(): pl.pallas_call(forward_kernel, in_specs=[pl.BlockSpec(memory_space=pl.ANY...  3.65 us
    ppermute x1, starting transfers between devices, body(): lax.ppermute(last[1], 'gx', far)  3.63 us
    ppermute x1, waiting for transfers between devices, body(): lax.ppermute(last[1], 'gx', far)  2.7 us
    ppermute x1, starting transfers between devices, body(): lax.ppermute(first[1], 'gx', far)  2.35 us
    pallas_call x1, Pallas kernels, body(): pl.pallas_call(inner_kernel, in_specs=[whole()] * 6 + [pl.BlockSpec(memor...  1.65 us
    pallas_call x1, Pallas kernels, body(): pl.pallas_call(mix_kernel, in_specs=[whole()] * 8, out_specs=[whole()] *...  1.54 us
  transfers between devices with their start and end apart: 4, of which 1 were waited for; matrix products, arithmetic and copies ran while one was open for 0% of the time, Pallas kernels for 9%

profile of v9, /device:TPU:1, one launch (start us, length us, event | category | flops | bytes accessed | tf_op | source)
XLA Modules:
  0.0 48.7 jit_solution(10176683437741451080)
XLA Ops:
  0.6 0.0 copy-start.1
  0.6 0.0 copy-start.2
  0.7 0.0 copy-start.8
  0.7 0.0 copy-start.7
  0.7 0.0 copy-start.6
  0.7 0.0 copy-start.5
  0.7 0.0 copy-start
  0.7 0.0 copy-start.3
  0.7 0.0 copy-start.4
  0.7 0.0 copy-start.9
  0.7 0.0 copy-start.10
  0.8 0.0 copy-start.11
  0.8 3.6 %forward_yz.1 = (f32[128,128]{1,0:T(8,128)S(1)}, bf16[32,32768]{1,0:T(8,128)(2,1)S(1)}) custom-call(bf16[32,32768]{1,0:T(8,128)(2,1)} %bitcast.23, f32[1,32]{1,0:T(1,128)} %bitcast.25, bf16[256,256]{1,0:T(8,128)(2,1)} %constant.14.clone.table_z, bf16[264,1024]{1,0:T(8,128)(2,1)} %constant.15.clone.table_y, f32[2,17,128]{2,1,0:T(8,128)} %constant.16.clone.turns), custom_call_target="tpu_custom_call" | custom-call | tf_op jit(solution)/shard_map/forward_yz/pallas_call | solution.py:611
  4.4 14.2 %all_to_all.10 = f32[32,4,128]{2,1,0:T(4,128)S(1)} all-to-all(f32[32,4,128]{2,1,0:T(4,128)S(1)} %bitcast.21), channel_id=1, replica_groups=mesh['groups'=1,'gx'=32] {'gx'}, dimensions={0} | all-to-all | bytes 131072 | tf_op jit(solution)/shard_map/all_to_all | solution.py:635
  18.6 0.0 copy-done.1
  18.6 0.0 copy-done.2
  18.6 0.0 copy-done.8
  18.6 0.0 copy-done.7
  18.6 0.0 copy-done.6
  18.6 0.0 copy-done.5
  18.6 0.0 copy-done
  18.6 1.5 %mix_modes.1 = (f32[128,128]{1,0:T(8,128)S(1)}, bf16[256,256]{1,0:T(8,128)(2,1)S(1)}, bf16[1024,256]{1,0:T(8,128)(2,1)S(1)}, bf16[32,1024]{1,0:T(8,128)(2,1)S(1)}) custom-call(f32[128,128]{1,0:T(8,128)S(1)} %bitcast.14, bf16[2,32,32,256]{3,2,1,0:T(8,128)(2,1)S(1)} %copy-done, bf16[1024,256]{1,0:T(8,128)(2,1)S(1)} %copy-done.2, ...), custom_call_target="tpu_custom_call" | custom-call | tf_op jit(solution)/shard_map/mix_modes/pallas_call | solution.py:640
  20.2 9.1 %all_to_all.11 = f32[32,4,128]{2,1,0:T(4,128)S(1)} all-to-all(f32[32,4,128]{2,1,0:T(4,128)S(1)} %bitcast.20), channel_id=1, replica_groups=mesh['groups'=1,'gx'=32] {'gx'}, dimensions={0} | all-to-all | bytes 131072 | tf_op jit(solution)/shard_map/all_to_all | solution.py:668
  29.3 0.0 copy-done.3
  29.3 0.0 copy-done.4
  29.3 0.0 copy-done.9
  29.3 0.0 copy-done.10
  29.3 0.0 copy-done.11
  29.3 5.5 %point_network.2 = (f32[3,192,128]{2,1,0:T(8,128)S(1)}, f32[3,192,128]{2,1,0:T(8,128)S(1)}, f32[192,128]{1,0:T(8,128)S(1)}) custom-call(f32[128,128]{1,0:T(8,128)S(1)} %bitcast.18, bf16[32,32768]{1,0:T(8,128)(2,1)S(1)} %get-tuple-element.18.values, bf16[256,256]{1,0:T(8,128)(2,1)S(1)} %get-tuple-element.19.wide_bypass, ...), custom_call_target="tpu_custom_call" | custom-call | flops 9830400000 | bytes 4915200 | tf_op jit(solution)/shard_map/point_network/pallas_call | solution.py:678
  34.8 2.3 %collective-permute-start.1 = (f32[3,192,128]{2,1,0:T(8,128)S(1)}, f32[3,192,128]{2,1,0:T(8,128)S(1)}, u32[]{:S(2)}, u32[]{:S(2)}) collective-permute-start(f32[3,192,128]{2,1,0:T(8,128)S(1)} %get-tuple-element.28.refs_1_), channel_id=1, source_target_pairs={{1,2},{3,4},{5,6},{7,8},{9,10},{11,12},{13,14},{15,16},{17,18},{19... | collective-permute-start | bytes 884744 | tf_op jit(solution)/shard_map/ppermute | solution.py:705
  37.2 0.1 collective-permute-start
  37.3 2.5 %point_network.3 = (f32[3,64,128]{2,1,0:T(8,128)S(1)}, f32[3,64,128]{2,1,0:T(8,128)S(1)}, f32[64,128]{1,0:T(8,128)S(1)}) custom-call(f32[128,128]{1,0:T(8,128)S(1)} %bitcast.19, bf16[32,32768]{1,0:T(8,128)(2,1)S(1)} %get-tuple-element.18.values, bf16[256,256]{1,0:T(8,128)(2,1)S(1)} %get-tuple-element.19.wide_bypass, ...), custom_call_target="tpu_custom_call" | custom-call | flops 3276800000 | bytes 1638400 | tf_op jit(solution)/shard_map/point_network/pallas_call | solution.py:678
  39.8 3.6 %collective-permute-start.3 = (f32[3,64,128]{2,1,0:T(8,128)S(1)}, f32[3,64,128]{2,1,0:T(8,128)S(1)}, u32[]{:S(2)}, u32[]{:S(2)}) collective-permute-start(f32[3,64,128]{2,1,0:T(8,128)S(1)} %get-tuple-element.29.refs_5_), channel_id=1, source_target_pairs={{1,2},{3,4},{5,6},{7,8},{9,10},{11,12},{13,14},{15,16},{17,18},{19... | collective-permute-start | bytes 294920 | tf_op jit(solution)/shard_map/ppermute | solution.py:707
  43.5 0.1 collective-permute-start.2
  43.5 1.6 %faces_in_plane.1 = (f32[2,256,128]{2,1,0:T(8,128)}, f32[256,128]{1,0:T(8,128)S(1)}) custom-call(f32[3,192,128]{2,1,0:T(8,128)S(1)} %get-tuple-element.22.first.refs_0_, f32[3,64,128]{2,1,0:T(8,128)S(1)} %get-tuple-element.23.last.refs_4_, f32[192,128]{1,0:T(8,128)S(1)} %get-tuple-element.24.first_filled, f32[64,128]{1,0:T(8,128)S(1)} %get-tuple-element.25.last_filled, ...), custom_call_target="tpu_custom_call" | custom-call | tf_op jit(solution)/shard_map/faces_in_plane/pallas_call | solution.py:708
  45.2 2.7 %collective-permute-done.3.refs_7_ = f32[3,64,128]{2,1,0:T(8,128)S(1)} collective-permute-done((f32[3,64,128]{2,1,0:T(8,128)S(1)}, f32[3,64,128]{2,1,0:T(8,128)S(1)}, u32[]{:S(2)}, u32[]{:S(2)}) %collective-permute-start.3) | collective-permute-done | bytes 98336 | tf_op jit(solution)/shard_map/ppermute | solution.py:707
  47.9 0.0 collective-permute-done.2.refs_6_
  47.9 0.0 collective-permute-done.1.refs_3_
  47.9 0.0 collective-permute-done.refs_2_
  47.9 0.8 %faces_between_planes.1 = f32[256,128]{1,0:T(8,128)} custom-call(f32[256,128]{1,0:T(8,128)S(1)} %get-tuple-element.27.partial, f32[3,192,128]{2,1,0:T(8,128)S(1)} %get-tuple-element.22.first.refs_0_, f32[3,192,128]{2,1,0:T(8,128)S(1)} %get-tuple-element.28.refs_1_, f32[3,192,128]{2,1,0:T(8,128)S(1)} %collective-permute-done.refs_2_, ...), custom_call_target="tpu_custom_call" | custom-call | tf_op jit(solution)/shard_map/faces_between_planes/pallas_call | solution.py:719
Async XLA Ops:
  0.6 18.0 %copy-start.1 = (bf16[256,1024]{1,0:T(8,128)(2,1)S(1)}, bf16[256,1024]{1,0:T(8,128)(2,1)}, u32[]{:S(2)}) copy-start(bf16[256,1024]{1,0:T(8,128)(2,1)} %constant.18.clone.table_back) | copy-start | bytes 1572868
  0.6 18.0 %copy-start.2 = (bf16[1024,256]{1,0:T(8,128)(2,1)S(1)}, bf16[1024,256]{1,0:T(8,128)(2,1)}, u32[]{:S(2)}) copy-start(bf16[1024,256]{1,0:T(8,128)(2,1)} %constant.17.clone.table_x) | copy-start | bytes 1572868
  0.7 17.9 %copy-start.8 = (bf16[2,32]{1,0:T(2,128)(2,1)S(1)}, bf16[2,32]{1,0:T(2,128)(2,1)}, u32[]{:S(2)}) copy-start(bf16[2,32]{1,0:T(2,128)(2,1)} %decode.1) | copy-start | bytes 388
  0.7 17.9 %copy-start.7 = (bf16[32,128]{1,0:T(8,128)(2,1)S(1)}, bf16[32,128]{1,0:T(8,128)(2,1)}, u32[]{:S(2)}) copy-start(bf16[32,128]{1,0:T(8,128)(2,1)} %mlp_out.1) | copy-start | bytes 24580
  0.7 17.9 %copy-start.6 = (bf16[128,32]{0,1:T(8,128)(2,1)S(1)}, bf16[128,32]{0,1:T(8,128)(2,1)}, u32[]{:S(2)}) copy-start(bf16[128,32]{0,1:T(8,128)(2,1)} %param.22) | copy-start | bytes 24580
  0.7 17.9 %copy-start.5 = (bf16[32,32]{1,0:T(8,128)(2,1)S(1)}, bf16[32,32]{1,0:T(8,128)(2,1)}, u32[]{:S(2)}) copy-start(bf16[32,32]{1,0:T(8,128)(2,1)} %bypass.1) | copy-start | bytes 6148
  0.7 17.9 %copy-start = (bf16[2,32,32,256]{3,2,1,0:T(8,128)(2,1)S(1)}, bf16[2,32,32,256]{3,2,1,0:T(8,128)(2,1)}, u32[]{:S(2)}) copy-start(bf16[2,32,32,256]{3,2,1,0:T(8,128)(2,1)} %weight.1) | copy-start | bytes 3145732
  0.7 28.6 %copy-start.3 = (s32[3,1,32768]{2,1,0:T(1,128)S(1)}, s32[3,1,32768]{2,1,0:T(1,128)}, u32[]{:S(2)}) copy-start(s32[3,1,32768]{2,1,0:T(1,128)} %param.26) | copy-start | bytes 1179652
  0.7 28.6 %copy-start.4 = (s32[1,32768]{1,0:T(1,128)S(1)}, s32[1,32768]{1,0:T(1,128)}, u32[]{:S(2)}) copy-start(s32[1,32768]{1,0:T(1,128)} %param.25) | copy-start | bytes 393220
  0.7 28.6 %copy-start.9 = (f32[8]{0:T(128)S(1)}, f32[8]{0:T(128)}, u32[]{:S(2)}) copy-start(f32[8]{0:T(128)} %perm_table.5) | copy-start | bytes 100
  0.7 28.6 %copy-start.10 = (bf16[768,512]{1,0:T(8,128)(2,1)S(1)}, bf16[768,512]{1,0:T(8,128)(2,1)}, u32[]{:S(2)}) copy-start(bf16[768,512]{1,0:T(8,128)(2,1)} %constant.19.clone.tables) | copy-start | bytes 2359300
  0.8 28.6 %copy-start.11 = (f32[2,32,128]{2,1,0:T(8,128)S(1)}, f32[2,32,128]{2,1,0:T(8,128)}, u32[]{:S(2)}) copy-start(f32[2,32,128]{2,1,0:T(8,128)} %constant.20.clone.turns) | copy-start | bytes 98308
  34.8 13.1 %collective-permute-start.1 = (f32[3,192,128]{2,1,0:T(8,128)S(1)}, f32[3,192,128]{2,1,0:T(8,128)S(1)}, u32[]{:S(2)}, u32[]{:S(2)}) collective-permute-start(f32[3,192,128]{2,1,0:T(8,128)S(1)} %get-tuple-element.28.refs_1_), channel_id=1, source_target_pairs={{1,2},{3,4},{5,6},{7,8},{9,10},{11,12},{13,14},{15,16},{17,18},{19... | collective-permute-start | bytes 884744 | tf_op jit(solution)/shard_map/ppermute | solution.py:705
  37.2 10.7 %collective-permute-start = (f32[3,192,128]{2,1,0:T(8,128)S(1)}, f32[3,192,128]{2,1,0:T(8,128)S(1)}, u32[]{:S(2)}, u32[]{:S(2)}) collective-permute-start(f32[3,192,128]{2,1,0:T(8,128)S(1)} %get-tuple-element.22.first.refs_0_), channel_id=1, source_target_pairs={{0,1},{2,3},{4,5},{6,7},{8,9},{10,11},{12,13},{14,15},{16,17},{18,... | collective-permute-start | bytes 884744 | tf_op jit(solution)/shard_map/ppermute | solution.py:705
  39.8 8.1 %collective-permute-start.3 = (f32[3,64,128]{2,1,0:T(8,128)S(1)}, f32[3,64,128]{2,1,0:T(8,128)S(1)}, u32[]{:S(2)}, u32[]{:S(2)}) collective-permute-start(f32[3,64,128]{2,1,0:T(8,128)S(1)} %get-tuple-element.29.refs_5_), channel_id=1, source_target_pairs={{1,2},{3,4},{5,6},{7,8},{9,10},{11,12},{13,14},{15,16},{17,18},{19... | collective-permute-start | bytes 294920 | tf_op jit(solution)/shard_map/ppermute | solution.py:707
  43.5 4.4 %collective-permute-start.2 = (f32[3,64,128]{2,1,0:T(8,128)S(1)}, f32[3,64,128]{2,1,0:T(8,128)S(1)}, u32[]{:S(2)}, u32[]{:S(2)}) collective-permute-start(f32[3,64,128]{2,1,0:T(8,128)S(1)} %get-tuple-element.23.last.refs_4_), channel_id=1, source_target_pairs={{0,1},{2,3},{4,5},{6,7},{8,9},{10,11},{12,13},{14,15},{16,17},{18,... | collective-permute-start | bytes 294920 | tf_op jit(solution)/shard_map/ppermute | solution.py:707
